TPU v7x, 32 devices: a whole 2x2x4 slice. The times are simulated.
32 devices in a mesh: outer: 4 (over y, x), inner: 8 (over z, core).
Axes of the slice: x: 2, y: 2, z: 4, core: 2. Of those that a mesh axis runs over, the one named last changes fastest.
Arguments:
- points: float32 [3584, 256], P(('outer', 'inner')), may hold values from -36 to 36
- vectors: float32 [3584, 128], P(('outer', 'inner')), may hold values from -6 to 6
- lengthscales: float32 [256], replicated, may hold values from 8 to 32
- outputscale: float32 [1], replicated, may hold values from 0.03 to 0.12
- noise: float32 [1], replicated, may hold values from 0.3 to 3
Outputs:
- product: float32 [3584, 128], P(('outer', 'inner'))
All inputs are finite; a program needn't handle non-finite values.
Results may differ from a plain program's by a relative error of at most 0.00024.
Values sent between devices are 32-bit elements; how exact they have to be, the bound alone decides.
No kernel may reach another device: no remote copies, remote signals or barrier semaphores. Data moves between devices by JAX's collectives and lax.ppermute only.
A program may use at most 128 MiB of HBM per device.

v0:
```python
import jax
import jax.numpy as jnp
from jax import lax
from jax.sharding import PartitionSpec as P


def matern(dist2, amplitude):
    scaled_r = jnp.sqrt(5.0) * jnp.sqrt(jnp.maximum(dist2, 0.0))
    return amplitude * (1.0 + scaled_r + scaled_r * scaled_r / 3.0) * jnp.exp(-scaled_r)


def row_norms(rows):
    return jnp.sum(rows * rows, axis=1)


def kernel_tile(rows, norms_here, cols, col_norms, amplitude):
    inner_prod = jnp.dot(
        rows, cols.T, precision=lax.Precision.HIGHEST, preferred_element_type=jnp.float32
    )
    dist2 = norms_here[:, None] + col_norms[None, :] - 2.0 * inner_prod
    return matern(dist2, amplitude)


def apply_tile(tile, values):
    return jnp.dot(
        tile, values, precision=lax.Precision.HIGHEST, preferred_element_type=jnp.float32
    )


def per_device(points, vectors, lengthscales, outputscale, noise):
    amplitude = outputscale[0]
    scaled = points / lengthscales[None, :]
    sqnorm = row_norms(scaled)
    piece_rows = lax.all_gather(scaled, ("outer", "inner"), axis=0, tiled=True)
    piece_values = lax.all_gather(vectors, ("outer", "inner"), axis=0, tiled=True)
    tile = kernel_tile(scaled, sqnorm, piece_rows, row_norms(piece_rows), amplitude)
    total = apply_tile(tile, piece_values)
    return total + noise[0] * vectors


def solution(mesh):
    placed = (P(("outer", "inner"), None), P(("outer", "inner"), None), P(), P(), P())
    return jax.shard_map(
        per_device,
        mesh=mesh,
        in_specs=placed,
        out_specs=P(("outer", "inner"), None),
        check_vma=False,
    )
```

profile of v0, /device:TPU:0, one launch (start us, length us, event | category | flops | bytes accessed | tf_op | source)
XLA Modules:
  0.0 142.2 jit_solution(13806589943837288145)
XLA Ops:
  6.5 0.0 all-gather.3.cloned.1.call-start
  6.5 1.7 %multiply_reduce_fusion.1 = (f32[112]{0:T(128)S(1)}, f32[112,256]{1,0:T(8,128)}) fusion(f32[112,256]{1,0:T(8,128)} %param.5, f32[256]{0:T(256)} %param.7), kind=kLoop, calls=%fused_computation.19 | loop fusion | flops 85904 | bytes 230848 | tf_op jit(solution)/shard_map/reduce_sum | solution.py:13
  8.2 0.0 copy-start.1
  8.2 0.0 all-gather.3.cloned.1.call-update
  8.2 0.0 all-gather.5.cloned.1.call-start
  8.3 0.7 all-gather.5.cloned.1.call-update
  10.3 63.2 %all-gather.3.cloned.1.call-done = f32[3584,256]{1,0:T(8,128)} async-done(((f32[112,256]{1,0:T(8,128)}), f32[3584,256]{1,0:T(8,128)}) %all-gather.3.cloned.1.call-update) | async-done | bytes 3670032 | tf_op jit(solution)/shard_map/all_gather | solution.py:34
  73.5 0.0 copy-start
  73.5 2.7 %multiply_reduce_fusion = f32[3584]{0:T(1024)S(1)} fusion(f32[3584,256]{1,0:T(8,128)} %all-gather.3.cloned.1.call-done), kind=kLoop, calls=%fused_computation.5 | loop fusion | flops 1831424 | bytes 3684352 | tf_op jit(solution)/shard_map/reduce_sum | solution.py:13
  76.2 0.0 copy-done.1
  76.3 0.4 copy-done
  76.6 0.0 copy-start.2
  76.7 4.0 %fusion.3 = f32[112,3584]{1,0:T(8,128)S(1)} fusion(f32[112,256]{1,0:T(8,128)S(1)} %copy-done.1, f32[3584,256]{1,0:T(8,128)S(1)} %copy-done, f32[3584]{0:T(1024)S(1)} %multiply_reduce_fusion, f32[112]{0:T(128)S(1)} %get-tuple-element.5), kind=kOutput, calls=%fused_computation.4 | convolution fusion | flops 1235132416 | bytes 5405120 | tf_op jit(solution)/shard_map/dot_general | solution.py:17
  80.6 50.5 %all-gather.5.cloned.1.call-done = f32[3584,128]{1,0:T(8,128)} async-done(((f32[112,128]{1,0:T(8,128)}), f32[3584,128]{1,0:T(8,128)}) %all-gather.5.cloned.1.call-update) | async-done | bytes 1835024 | tf_op jit(solution)/shard_map/all_gather | solution.py:35
  131.2 0.0 copy-done.2
  131.2 4.2 %fusion.13 = f32[112,128]{1,0:T(8,128)} fusion(f32[3584,128]{1,0:T(8,128)} %all-gather.5.cloned.1.call-done, f32[112,3584]{1,0:T(8,128)S(1)} %fusion.3, f32[]{:T(128)} %bitcast.5, f32[112,128]{1,0:T(8,128)S(1)} %copy-done.2, f32[]{:T(128)} %bitcast.6), kind=kOutput, calls=%fused_computation.15 | convolution fusion | flops 619401216 | bytes 3555336 | tf_op jit(solution)/shard_map/dot_general | solution.py:25
Async XLA Ops:
  6.5 67.0 %all-gather.3.cloned.1.call-start = ((), (), s32[]{:S(2)}) async-start(), calls=%async_computation | async-start | bytes 3784704 | tf_op jit(solution)/shard_map/all_gather | solution.py:34
  8.2 68.0 %copy-start.1 = (f32[112,256]{1,0:T(8,128)S(1)}, f32[112,256]{1,0:T(8,128)}, u32[]{:S(2)}) copy-start(f32[112,256]{1,0:T(8,128)} %get-tuple-element.6) | copy-start | bytes 344068
  8.2 122.9 %all-gather.5.cloned.1.call-start = ((), (), s32[]{:S(2)}) async-start(), calls=%async_computation.1 | async-start | bytes 1892352 | tf_op jit(solution)/shard_map/all_gather | solution.py:35
  73.5 3.1 %copy-start = (f32[3584,256]{1,0:T(8,128)S(1)}, f32[3584,256]{1,0:T(8,128)}, u32[]{:S(2)}) copy-start(f32[3584,256]{1,0:T(8,128)} %all-gather.3.cloned.1.call-done) | copy-start | bytes 11010052
  76.6 54.5 %copy-start.2 = (f32[112,128]{1,0:T(8,128)S(1)}, f32[112,128]{1,0:T(8,128)}, u32[]{:S(2)}) copy-start(f32[112,128]{1,0:T(8,128)} %param.6) | copy-start | bytes 172036
Sparse Core Ops, SparseCore 0:
  10.2 63.2 all-gather.2
  76.4 54.7 all-gather.4
where the time goes:
time: 142 us
  waiting for transfers between devices  114 us (80%)
  between operations  14.7 us (10%)
  matrix products  8.21 us (6%)
  other arithmetic  4.39 us (3%)
    all_gather x1, waiting for transfers between devices, per_device(): piece_rows = lax.all_gather(scaled, ('outer', 'inner'), axis=0, tiled=True)  63.2 us
    all_gather x1, waiting for transfers between devices, per_device(): lax.all_gather(vectors, ('outer', 'inner'), axis=0, tiled=True)  50.5 us
    reduce_sum x2, other arithmetic, row_norms(): return jnp.sum(rows * rows, axis=1)  4.39 us
    dot_general x1, matrix products, apply_tile(): jnp.dot(tile, values, precision=lax.Precision.HIGHEST, preferred_element_...  4.23 us
    dot_general x1, matrix products, kernel_tile(): jnp.dot(rows, cols.T, precision=lax.Precision.HIGHEST, preferred_element_...  3.97 us
  transfers between devices with their start and end apart: 2, of which 2 were waited for; matrix products, arithmetic and copies ran while one was open for 5% of the time, Pallas kernels for 0%

commit v1 on v0

v1 whole, which is shorter than its diff:
```python
import jax
import jax.numpy as jnp
from jax import lax
from jax.sharding import PartitionSpec as P

AXES = ("outer", "inner")
CORES = 2


def matern(dist2, amplitude):
    scaled_r = jnp.sqrt(5.0) * jnp.sqrt(jnp.maximum(dist2, 0.0))
    return amplitude * (1.0 + scaled_r + scaled_r * scaled_r / 3.0) * jnp.exp(-scaled_r)


def row_norms(rows):
    return jnp.sum(rows * rows, axis=1)


def partner(index, step, size):
    return index ^ step if size & (size - 1) == 0 else (index + step) % size


def solution(mesh):
    n_outer, n_inner = mesh.shape["outer"], mesh.shape["inner"]
    n_line = n_inner // CORES

    def linear(outer, line, core):
        return outer * n_inner + line * CORES + core

    places = [(o, z, c) for o in range(n_outer) for z in range(n_line) for c in range(CORES)]

    def along_line(step):
        return [(linear(o, z, c), linear(o, partner(z, step, n_line), c)) for o, z, c in places]

    def along_outer(step):
        return [(linear(o, z, c), linear(partner(o, step, n_outer), z, c)) for o, z, c in places]

    other_core = [(linear(o, z, c), linear(o, z, c ^ 1)) for o, z, c in places]

    def per_device(points, vectors, lengthscales, outputscale, noise):
        here = points.shape[0]
        features = points.shape[1]
        row_blocks = [points] + [lax.ppermute(points, AXES, along_line(k)) for k in range(1, n_line)]
        both = jnp.concatenate([points, vectors], axis=1)
        col_blocks = [both] + [lax.ppermute(both, AXES, along_outer(k)) for k in range(1, n_outer)]
        cols_mine = jnp.concatenate(col_blocks, axis=0)
        cols_theirs = lax.ppermute(cols_mine, AXES, other_core)
        cols = jnp.concatenate([cols_mine, cols_theirs], axis=0)
        rows = jnp.concatenate(row_blocks, axis=0) / lengthscales[None, :]
        values = cols[:, features:]
        cols = cols[:, :features] / lengthscales[None, :]
        inner_prod = jnp.dot(rows, cols.T, precision=lax.Precision.HIGHEST, preferred_element_type=jnp.float32)
        dist2 = row_norms(rows)[:, None] + row_norms(cols)[None, :] - 2.0 * inner_prod
        tile = matern(dist2, outputscale[0])
        partial = jnp.dot(tile, values, precision=lax.Precision.HIGHEST, preferred_element_type=jnp.float32)
        total = partial[:here] + noise[0] * vectors
        for k in range(1, n_line):
            back = [(b, a) for a, b in along_line(k)]
            total = total + lax.ppermute(partial[k * here : (k + 1) * here], AXES, back)
        return total

    placed = (P(AXES, None), P(AXES, None), P(), P(), P())
    return jax.shard_map(per_device, mesh=mesh, in_specs=placed, out_specs=P(AXES, None), check_vma=False)
```

time: 142 us -> 42 us (0.30)
  waiting for transfers between devices: 114 us -> 19.6 us
  starting transfers between devices: 0.04 us -> 13.5 us
  between operations: 14.7 us -> 1.41 us
  matrix products: 8.21 us -> 4.21 us
  other arithmetic: 4.39 us -> 1.06 us
  local copies, waits for them, and re-layouts: 0.4 us -> 1.93 us
    all_gather x2 -> x0, waiting for transfers between devices: 114 us -> none  [the longest x1 63.2 us: per_device(): piece_rows = lax.all_gather(scaled, ('outer', 'inner'), axis=0, tiled=True)]
    ppermute x0 -> x10, waiting for transfers between devices: none -> 19.6 us  [the longest x3 8.84 us: per_device(): lax.ppermute(points, AXES, along_line(k))]
    ppermute x0 -> x10, starting transfers between devices: none -> 13.5 us  [the longest x3 4.54 us: per_device(): lax.ppermute(both, AXES, along_outer(k))]
    reduce_sum x2, other arithmetic: 4.39 us -> 0.37 us  [row_norms(): return jnp.sum(rows * rows, axis=1)]
    dot_general x2, matrix products: 8.21 us -> 4.21 us  [the longest x1 2.54 us: per_device(): jnp.dot(tile, values, precision=lax.Precision.HIGHEST, preferred_element_...]
  transfers between devices with their start and end apart: 2 -> 10, of which waited for: 2 -> 6; matrix products, arithmetic and copies ran while one was open for 5% -> 0% of each run, Pallas kernels for 0% -> 0%
where the time goes in v1:
time: 42 us; the launch traced here: 41.8 us
  waiting for transfers between devices  19.6 us (47%)
  starting transfers between devices  13.5 us (32%)
  matrix products  4.21 us (10%)
  local copies, waits for them, and re-layouts  1.93 us (5%)
  between operations  1.41 us (3%)
  other arithmetic  1.06 us (3%)
    ppermute x3, waiting for transfers between devices, per_device(): lax.ppermute(points, AXES, along_line(k))  8.84 us
    ppermute x3, waiting for transfers between devices, per_device(): lax.ppermute(both, AXES, along_outer(k))  7.98 us
    ppermute x3, starting transfers between devices, per_device(): lax.ppermute(both, AXES, along_outer(k))  4.54 us
    ppermute x3, starting transfers between devices, per_device(): lax.ppermute(points, AXES, along_line(k))  4.45 us
    ppermute x3, starting transfers between devices, per_device(): total = total + lax.ppermute(partial[k * here:(k + 1) * here], AXES, back)  4.45 us
    ppermute x3, waiting for transfers between devices, per_device(): total = total + lax.ppermute(partial[k * here:(k + 1) * here], AXES, back)  2.82 us
    dot_general x1, matrix products, per_device(): jnp.dot(tile, values, precision=lax.Precision.HIGHEST, preferred_element_...  2.54 us
    dot_general x1, matrix products, per_device(): jnp.dot(rows, cols.T, precision=lax.Precision.HIGHEST, preferred_element_...  1.67 us
  transfers between devices with their start and end apart: 10, of which 6 were waited for; matrix products, arithmetic and copies ran while one was open for 0% of the time, Pallas kernels for 0%

profile of v1, /device:TPU:0, one launch (start us, length us, event | category | flops | bytes accessed | tf_op | source)
XLA Modules:
  0.0 41.8 jit_solution(12101610779329997248)
XLA Ops:
  0.0 0.0 copy-start
  0.0 0.0 copy-start.2
  0.0 1.0 %constant_dynamic-update-slice_fusion.1 = (f32[112,384]{1,0:T(8,128)S(1)}, f32[896,384]{1,0:T(8,128)S(1)}) fusion(f32[112,256]{1,0:T(8,128)} %param.5), kind=kLoop, calls=%fused_computation.35 | loop fusion | bytes 344064
  1.0 0.8 %constant_dynamic-update-slice_fusion = (f32[112,384]{1,0:T(8,128)S(1)}, f32[896,384]{1,0:T(8,128)S(1)}) fusion(f32[112,384]{1,0:T(8,128)S(1)} %get-tuple-element.8, f32[112,128]{1,0:T(8,128)} %param.6, f32[896,384]{1,0:T(8,128)S(1)} %get-tuple-element.9), kind=kLoop, calls=%fused_computation.34 | loop fusion | bytes 172032 | tf_op jit(solution)/shard_map/concatenate | solution.py:44
  1.8 3.0 %collective-permute-start.3 = (f32[112,384]{1,0:T(8,128)S(1)}, f32[112,384]{1,0:T(8,128)S(1)}, u32[]{:S(2)}, u32[]{:S(2)}) collective-permute-start(f32[112,384]{1,0:T(8,128)S(1)} %get-tuple-element.10), channel_id=1, source_target_pairs={{0,8},{1,9},{2,10},{3,11},{4,12},{5,13},{6,14},{7,15},{8,0},{9,1},... | collective-permute-start | bytes 516104 | tf_op jit(solution)/shard_map/ppermute | solution.py:45
  4.8 1.5 %collective-permute-start.4 = (f32[112,384]{1,0:T(8,128)S(1)}, f32[112,384]{1,0:T(8,128)S(1)}, u32[]{:S(2)}, u32[]{:S(2)}) collective-permute-start(f32[112,384]{1,0:T(8,128)S(1)} %get-tuple-element.10), channel_id=1, source_target_pairs={{0,16},{1,17},{2,18},{3,19},{4,20},{5,21},{6,22},{7,23},{8,24},{9,... | collective-permute-start | bytes 516104 | tf_op jit(solution)/shard_map/ppermute | solution.py:45
  6.3 0.0 collective-permute-start.5
  6.4 3.7 %collective-permute-done.3 = f32[112,384]{1,0:T(8,128)S(1)} collective-permute-done((f32[112,384]{1,0:T(8,128)S(1)}, f32[112,384]{1,0:T(8,128)S(1)}, u32[]{:S(2)}, u32[]{:S(2)}) %collective-permute-start.3) | collective-permute-done | bytes 172064 | tf_op jit(solution)/shard_map/ppermute | solution.py:45
  10.0 4.3 %collective-permute-done.4 = f32[112,384]{1,0:T(8,128)S(1)} collective-permute-done((f32[112,384]{1,0:T(8,128)S(1)}, f32[112,384]{1,0:T(8,128)S(1)}, u32[]{:S(2)}, u32[]{:S(2)}) %collective-permute-start.4) | collective-permute-done | bytes 172064 | tf_op jit(solution)/shard_map/ppermute | solution.py:45
  14.3 0.0 collective-permute-done.5
  14.4 0.1 collective-permute-start.6
  14.5 0.0 copy-done
  14.5 3.7 %collective-permute-start.2 = (f32[112,256]{1,0:T(8,128)S(1)}, f32[112,256]{1,0:T(8,128)S(1)}, u32[]{:S(2)}, u32[]{:S(2)}) collective-permute-start(f32[112,256]{1,0:T(8,128)S(1)} %copy-done), channel_id=1, source_target_pairs={{0,6},{1,7},{2,4},{3,5},{4,2},{5,3},{6,0},{7,1},{8,14},{9,15},{10,... | collective-permute-start | bytes 344072 | tf_op jit(solution)/shard_map/ppermute | solution.py:43
  18.2 0.0 collective-permute-start.1
  18.2 0.8 %collective-permute-start = (f32[112,256]{1,0:T(8,128)S(1)}, f32[112,256]{1,0:T(8,128)S(1)}, u32[]{:S(2)}, u32[]{:S(2)}) collective-permute-start(f32[112,256]{1,0:T(8,128)S(1)} %copy-done), channel_id=1, source_target_pairs={{0,2},{1,3},{2,0},{3,1},{4,6},{5,7},{6,4},{7,5},{8,10},{9,11},{10,... | collective-permute-start | bytes 344072 | tf_op jit(solution)/shard_map/ppermute | solution.py:43
  19.6 2.8 %collective-permute-done.2 = f32[112,256]{1,0:T(8,128)S(1)} collective-permute-done((f32[112,256]{1,0:T(8,128)S(1)}, f32[112,256]{1,0:T(8,128)S(1)}, u32[]{:S(2)}, u32[]{:S(2)}) %collective-permute-start.2) | collective-permute-done | bytes 114720 | tf_op jit(solution)/shard_map/ppermute | solution.py:43
  22.4 6.0 %collective-permute-done.1 = f32[112,256]{1,0:T(8,128)S(1)} collective-permute-done((f32[112,256]{1,0:T(8,128)S(1)}, f32[112,256]{1,0:T(8,128)S(1)}, u32[]{:S(2)}, u32[]{:S(2)}) %collective-permute-start.1) | collective-permute-done | bytes 114720 | tf_op jit(solution)/shard_map/ppermute | solution.py:43
  28.4 0.0 collective-permute-done
  28.4 0.0 copy-done.2
  28.4 0.2 multiply_reduce_fusion.1
  28.7 0.0 collective-permute-done.6
  28.7 0.2 multiply_reduce_fusion
  28.9 1.7 %fusion.24 = f32[448,896]{1,0:T(8,128)S(1)} fusion(f32[896,384]{1,0:T(8,128)S(1)} %constant_dynamic-update-slice_fusion.2, f32[256]{0:T(256)S(1)} %copy-done.2, f32[112,256]{1,0:T(8,128)S(1)} %collective-permute-done.2, f32[112,256]{1,0:T(8,128)S(1)} %collective-permute-done.1, f32[112,256]{1,0:T(8,128)S(1)} %collective-permute-done, f32[112,256]{1,0:T(8,128)S(1)} %copy-done), kind=kOutput, calls=%fused_computation.29 | convolution fusion | flops 1233813504 | bytes 2983936 | tf_op jit(solution)/shard_map/dot_general | solution.py:52
  30.6 0.0 copy-start.1
  30.6 2.5 %fusion = f32[448,128]{1,0:T(8,128)S(1)} fusion(f32[448,896]{1,0:T(8,128)S(1)} %fusion.24, f32[896]{0:T(1024)S(1)} %multiply_reduce_fusion, f32[448]{0:T(512)S(1)} %multiply_reduce_fusion.1, f32[]{:T(128)} %bitcast.2, f32[896,384]{1,0:T(8,128)S(1)} %constant_dynamic-update-slice_fusion.2), kind=kOutput, calls=%fused_computation | convolution fusion | flops 621379584 | bytes 2299908 | tf_op jit(solution)/shard_map/dot_general | solution.py:55
  33.2 2.6 %collective-permute-start.9 = (f32[112,128]{1,0:T(8,128)S(1)}, f32[112,128]{1,0:T(8,128)S(1)}, u32[]{:S(2)}, u32[]{:S(2)}) collective-permute-start(f32[112,128]{1,0:T(8,128)S(1)} %get-tuple-element.6), channel_id=1, source_target_pairs={{6,0},{7,1},{4,2},{5,3},{2,4},{3,5},{0,6},{1,7},{14,8},{15,9},{12,... | collective-permute-start | bytes 172040 | tf_op jit(solution)/shard_map/ppermute | solution.py:59
  35.8 0.0 collective-permute-start.8
  35.8 1.9 %collective-permute-start.7 = (f32[112,128]{1,0:T(8,128)S(1)}, f32[112,128]{1,0:T(8,128)S(1)}, u32[]{:S(2)}, u32[]{:S(2)}) collective-permute-start(f32[112,128]{1,0:T(8,128)S(1)} %get-tuple-element.5), channel_id=1, source_target_pairs={{2,0},{3,1},{0,2},{1,3},{6,4},{7,5},{4,6},{5,7},{10,8},{11,9},{8,1... | collective-permute-start | bytes 172040 | tf_op jit(solution)/shard_map/ppermute | solution.py:59
  38.3 1.0 %collective-permute-done.9 = f32[112,128]{1,0:T(8,128)S(1)} collective-permute-done((f32[112,128]{1,0:T(8,128)S(1)}, f32[112,128]{1,0:T(8,128)S(1)}, u32[]{:S(2)}, u32[]{:S(2)}) %collective-permute-start.9) | collective-permute-done | bytes 57376 | tf_op jit(solution)/shard_map/ppermute | solution.py:59
  39.3 1.8 %collective-permute-done.8 = f32[112,128]{1,0:T(8,128)S(1)} collective-permute-done((f32[112,128]{1,0:T(8,128)S(1)}, f32[112,128]{1,0:T(8,128)S(1)}, u32[]{:S(2)}, u32[]{:S(2)}) %collective-permute-start.8) | collective-permute-done | bytes 57376 | tf_op jit(solution)/shard_map/ppermute | solution.py:59
  41.1 0.0 collective-permute-done.7
  41.1 0.0 copy-done.1
  41.1 0.6 %fusion.27 = f32[112,128]{1,0:T(8,128)} fusion(f32[112,128]{1,0:T(8,128)S(1)} %collective-permute-done.9, f32[112,128]{1,0:T(8,128)S(1)} %collective-permute-done.8, f32[112,128]{1,0:T(8,128)S(1)} %collective-permute-done.7, f32[448,128]{1,0:T(8,128)S(1)} %fusion, f32[112,128]{1,0:T(8,128)S(1)} %copy-done.1, f32[]{:T(128)} %bitcast.3), kind=kLoop, calls=%fused_computation.33 | loop fusion | flops 71680 | bytes 344068 | tf_op jit(solution)/shard_map/add | solution.py:59
  (6 shorter events, 0.2 us)
Async XLA Ops:
  0.0 14.5 %copy-start = (f32[112,256]{1,0:T(8,128)S(1)}, f32[112,256]{1,0:T(8,128)}, u32[]{:S(2)}) copy-start(f32[112,256]{1,0:T(8,128)} %param.5) | copy-start | bytes 344068
  0.0 28.4 %copy-start.2 = (f32[256]{0:T(256)S(1)}, f32[256]{0:T(256)}, u32[]{:S(2)}) copy-start(f32[256]{0:T(256)} %param.7) | copy-start | bytes 3076
  1.8 8.2 %collective-permute-start.3 = (f32[112,384]{1,0:T(8,128)S(1)}, f32[112,384]{1,0:T(8,128)S(1)}, u32[]{:S(2)}, u32[]{:S(2)}) collective-permute-start(f32[112,384]{1,0:T(8,128)S(1)} %get-tuple-element.10), channel_id=1, source_target_pairs={{0,8},{1,9},{2,10},{3,11},{4,12},{5,13},{6,14},{7,15},{8,0},{9,1},... | collective-permute-start | bytes 516104 | tf_op jit(solution)/shard_map/ppermute | solution.py:45
  4.8 9.5 %collective-permute-start.4 = (f32[112,384]{1,0:T(8,128)S(1)}, f32[112,384]{1,0:T(8,128)S(1)}, u32[]{:S(2)}, u32[]{:S(2)}) collective-permute-start(f32[112,384]{1,0:T(8,128)S(1)} %get-tuple-element.10), channel_id=1, source_target_pairs={{0,16},{1,17},{2,18},{3,19},{4,20},{5,21},{6,22},{7,23},{8,24},{9,... | collective-permute-start | bytes 516104 | tf_op jit(solution)/shard_map/ppermute | solution.py:45
  6.3 8.0 %collective-permute-start.5 = (f32[112,384]{1,0:T(8,128)S(1)}, f32[112,384]{1,0:T(8,128)S(1)}, u32[]{:S(2)}, u32[]{:S(2)}) collective-permute-start(f32[112,384]{1,0:T(8,128)S(1)} %get-tuple-element.10), channel_id=1, source_target_pairs={{0,24},{1,25},{2,26},{3,27},{4,28},{5,29},{6,30},{7,31},{8,16},{9,... | collective-permute-start | bytes 516104 | tf_op jit(solution)/shard_map/ppermute | solution.py:45
  14.4 14.3 %collective-permute-start.6 = (f32[448,384]{1,0:T(8,128)S(1)}, f32[448,384]{1,0:T(8,128)S(1)}, u32[]{:S(2)}, u32[]{:S(2)}) collective-permute-start(f32[448,384]{1,0:T(8,128)S(1)} %pad_maximum_fusion), channel_id=1, source_target_pairs={{0,1},{1,0},{2,3},{3,2},{4,5},{5,4},{6,7},{7,6},{8,9},{9,8},{10,11... | collective-permute-start | bytes 2064392 | tf_op jit(solution)/shard_map/ppermute | solution.py:47
  14.5 7.9 %collective-permute-start.2 = (f32[112,256]{1,0:T(8,128)S(1)}, f32[112,256]{1,0:T(8,128)S(1)}, u32[]{:S(2)}, u32[]{:S(2)}) collective-permute-start(f32[112,256]{1,0:T(8,128)S(1)} %copy-done), channel_id=1, source_target_pairs={{0,6},{1,7},{2,4},{3,5},{4,2},{5,3},{6,0},{7,1},{8,14},{9,15},{10,... | collective-permute-start | bytes 344072 | tf_op jit(solution)/shard_map/ppermute | solution.py:43
  18.2 10.3 %collective-permute-start.1 = (f32[112,256]{1,0:T(8,128)S(1)}, f32[112,256]{1,0:T(8,128)S(1)}, u32[]{:S(2)}, u32[]{:S(2)}) collective-permute-start(f32[112,256]{1,0:T(8,128)S(1)} %copy-done), channel_id=1, source_target_pairs={{0,4},{1,5},{2,6},{3,7},{4,0},{5,1},{6,2},{7,3},{8,12},{9,13},{10,... | collective-permute-start | bytes 344072 | tf_op jit(solution)/shard_map/ppermute | solution.py:43
  18.2 10.3 %collective-permute-start = (f32[112,256]{1,0:T(8,128)S(1)}, f32[112,256]{1,0:T(8,128)S(1)}, u32[]{:S(2)}, u32[]{:S(2)}) collective-permute-start(f32[112,256]{1,0:T(8,128)S(1)} %copy-done), channel_id=1, source_target_pairs={{0,2},{1,3},{2,0},{3,1},{4,6},{5,7},{6,4},{7,5},{8,10},{9,11},{10,... | collective-permute-start | bytes 344072 | tf_op jit(solution)/shard_map/ppermute | solution.py:43
  30.6 10.5 %copy-start.1 = (f32[112,128]{1,0:T(8,128)S(1)}, f32[112,128]{1,0:T(8,128)}, u32[]{:S(2)}) copy-start(f32[112,128]{1,0:T(8,128)} %param.6) | copy-start | bytes 172036
  33.2 6.1 %collective-permute-start.9 = (f32[112,128]{1,0:T(8,128)S(1)}, f32[112,128]{1,0:T(8,128)S(1)}, u32[]{:S(2)}, u32[]{:S(2)}) collective-permute-start(f32[112,128]{1,0:T(8,128)S(1)} %get-tuple-element.6), channel_id=1, source_target_pairs={{6,0},{7,1},{4,2},{5,3},{2,4},{3,5},{0,6},{1,7},{14,8},{15,9},{12,... | collective-permute-start | bytes 172040 | tf_op jit(solution)/shard_map/ppermute | solution.py:59
  35.8 5.3 %collective-permute-start.8 = (f32[112,128]{1,0:T(8,128)S(1)}, f32[112,128]{1,0:T(8,128)S(1)}, u32[]{:S(2)}, u32[]{:S(2)}) collective-permute-start(f32[112,128]{1,0:T(8,128)S(1)} %get-tuple-element.7), channel_id=1, source_target_pairs={{4,0},{5,1},{6,2},{7,3},{0,4},{1,5},{2,6},{3,7},{12,8},{13,9},{14,... | collective-permute-start | bytes 172040 | tf_op jit(solution)/shard_map/ppermute | solution.py:59
  35.8 5.3 %collective-permute-start.7 = (f32[112,128]{1,0:T(8,128)S(1)}, f32[112,128]{1,0:T(8,128)S(1)}, u32[]{:S(2)}, u32[]{:S(2)}) collective-permute-start(f32[112,128]{1,0:T(8,128)S(1)} %get-tuple-element.5), channel_id=1, source_target_pairs={{2,0},{3,1},{0,2},{1,3},{6,4},{7,5},{4,6},{5,7},{10,8},{11,9},{8,1... | collective-permute-start | bytes 172040 | tf_op jit(solution)/shard_map/ppermute | solution.py:59

commit v2 on v1

v2 whole, which is shorter than its diff:
```python
import functools

import jax
import jax.numpy as jnp
from jax import lax
from jax.experimental import pallas as pl
from jax.experimental.pallas import tpu as pltpu
from jax.sharding import PartitionSpec as P

AXES = ("outer", "inner")
CORES = 2
VMEM = pl.BlockSpec(memory_space=pltpu.VMEM)
SMEM = pl.BlockSpec(memory_space=pltpu.SMEM)
BF16 = jnp.bfloat16
F32 = jnp.float32
LIMIT = 24 * 1024 * 1024


def partner(index, step, size):
    return index ^ step if size & (size - 1) == 0 else (index + step) % size


def split(x):
    high = x.astype(BF16)
    return high, (x - high.astype(F32)).astype(BF16)


def cost(us):
    return pl.CostEstimate(flops=int(us * 1e9), bytes_accessed=1024, transcendentals=0)


def contract_last(a, b, **kw):
    return lax.dot_general(a, b, (((1,), (1,)), ((), ())), preferred_element_type=F32, **kw)


def inverse_scale(scale_ref):
    return jnp.sqrt(F32(5.0)) / scale_ref[...]


def fill_rows(block, inverse, x_ref, norm_ref, at, here):
    x = block * inverse
    norm = jnp.sum(x * x, axis=1, keepdims=True)
    high, low = split(-2.0 * x)
    features = x.shape[1]
    x_ref[pl.ds(at, here), :features] = high
    x_ref[pl.ds(at, here), features:] = low
    norm_ref[pl.ds(at, here), :] = jnp.broadcast_to(norm, (here, norm_ref.shape[1]))


def rows_kernel(n, scale_ref, *refs):
    blocks, (x_ref, norm_ref) = refs[:n], refs[n:]
    here = blocks[0].shape[0]
    inverse = inverse_scale(scale_ref)
    for i, block in enumerate(blocks):
        fill_rows(block[...], inverse, x_ref, norm_ref, i * here, here)


def prepare_rows(scale, blocks, us):
    here, features = blocks[0].shape
    m = here * len(blocks)
    return pl.pallas_call(
        functools.partial(rows_kernel, len(blocks)),
        out_shape=(jax.ShapeDtypeStruct((m, 2 * features), BF16), jax.ShapeDtypeStruct((m, 128), F32)),
        in_specs=[VMEM] * (1 + len(blocks)),
        out_specs=(VMEM, VMEM),
        compiler_params=pltpu.CompilerParams(vmem_limit_bytes=LIMIT),
        cost_estimate=cost(us),
        name="rows",
    )(scale, *blocks)


def fill_cols(block, inverse, y_ref, v_ref, norm_ref):
    features = inverse.shape[1]
    y = block[:, :features] * inverse
    high, low = split(y)
    for i, part in enumerate((high, high, low, low)):
        y_ref[:, i * features : (i + 1) * features] = part
    squares = y * y
    ones = jnp.ones((8, features), F32)
    norm_ref[...] = contract_last(ones, squares, precision=lax.Precision.HIGHEST)
    vhigh, vlow = split(block[:, features:])
    v_ref[:, : vhigh.shape[1]] = vhigh
    v_ref[:, vhigh.shape[1] :] = vlow


def times_tile(x, norm, y_ref, v_ref, col_norm_ref, amplitude):
    dist2 = contract_last(jnp.concatenate([x, x], axis=1), y_ref[...])
    dist2 = jnp.maximum(dist2 + norm[:, :1] + col_norm_ref[:1, :], 1e-30)
    a = dist2 * lax.rsqrt(dist2)
    tile = (amplitude + amplitude * a + (amplitude / 3.0) * dist2) * jnp.exp(-a)
    high, low = split(tile)
    columns = v_ref.shape[1] // 2
    out = jnp.dot(high, v_ref[...], preferred_element_type=F32)
    out = out[:, :columns] + out[:, columns:]
    return out + jnp.dot(low, v_ref[:, :columns], preferred_element_type=F32)


def tile_kernel(plan, here, scale_ref, amp_ref, *refs):
    n_parts, has_start = plan
    parts, refs = refs[:n_parts], refs[n_parts:]
    x_ref, norm_ref, refs = refs[0], refs[1], refs[2:]
    if has_start:
        start_ref, refs = refs[0], refs[1:]
    out_ref, y_ref, v_ref, col_norm_ref = refs
    inverse = inverse_scale(scale_ref)
    amplitude = amp_ref[0]
    for p, part in enumerate(parts):
        fill_cols(part[...], inverse, y_ref, v_ref, col_norm_ref)
        for i in range(x_ref.shape[0] // here):
            at = slice(i * here, (i + 1) * here)
            out = times_tile(x_ref[at, :], norm_ref[at, :], y_ref, v_ref, col_norm_ref, amplitude)
            if p > 0:
                out = out + out_ref[at, :]
            elif has_start:
                out = out + start_ref[at, :]
            out_ref[at, :] = out


def times_columns(scale, amplitude, parts, rows, start, here, us):
    x, norm = rows
    m = x.shape[0]
    n, width = parts[0].shape
    features = scale.shape[1]
    columns = width - features
    given = [scale, amplitude, *parts, x, norm] + ([] if start is None else [start])
    specs = [VMEM, SMEM] + [VMEM] * (len(given) - 2)
    return pl.pallas_call(
        functools.partial(tile_kernel, (len(parts), start is not None), here),
        out_shape=jax.ShapeDtypeStruct((m, columns), F32),
        in_specs=specs,
        out_specs=VMEM,
        scratch_shapes=[
            pltpu.VMEM((n, 4 * features), BF16),
            pltpu.VMEM((n, 2 * columns), BF16),
            pltpu.VMEM((8, n), F32),
        ],
        compiler_params=pltpu.CompilerParams(vmem_limit_bytes=LIMIT),
        cost_estimate=cost(us),
        name="tile",
    )(*given)


def solution(mesh):
    n_outer, n_inner = mesh.shape["outer"], mesh.shape["inner"]
    n_line = n_inner // CORES

    def linear(outer, line, core):
        return outer * n_inner + line * CORES + core

    places = [(o, z, c) for o in range(n_outer) for z in range(n_line) for c in range(CORES)]

    def along_line(step):
        return [(linear(o, z, c), linear(o, partner(z, step, n_line), c)) for o, z, c in places]

    def along_outer(step):
        return [(linear(o, z, c), linear(partner(o, step, n_outer), z, c)) for o, z, c in places]

    other_core = [(linear(o, z, c), linear(o, z, c ^ 1)) for o, z, c in places]

    def per_device(points, vectors, lengthscales, outputscale, noise):
        here = points.shape[0]
        scale = lengthscales[None, :]
        lines = list(range(n_line - 1, 0, -1))
        far_lines, near_line = lines[:-1], lines[-1]
        n_far = here * len(far_lines)
        far = [lax.ppermute(points, AXES, along_line(k)) for k in far_lines]
        both = jnp.concatenate([points, vectors], axis=1)
        got = [lax.ppermute(both, AXES, along_outer(k)) for k in range(n_outer - 1, 0, -1)]
        late = lax.optimization_barrier((points, *got))
        near = lax.ppermute(late[0], AXES, along_line(near_line))
        cols_mine = jnp.concatenate([both, *late[1:]], axis=0)
        cols_theirs = lax.ppermute(cols_mine, AXES, other_core)

        x, norm = prepare_rows(scale, [*far, points], 40)
        first = times_columns(scale, outputscale, [cols_mine], (x, norm), None, here, 20)
        partial = times_columns(
            scale, outputscale, [cols_theirs], (x[:n_far], norm[:n_far]), first[:n_far], here, 10
        )
        x_near, norm_near = prepare_rows(scale, [near], 1)
        partial_near = times_columns(scale, outputscale, [cols_mine, cols_theirs], (x_near, norm_near), None, here, 10)
        own = times_columns(
            scale, outputscale, [cols_theirs], (x[n_far:], norm[n_far:]), first[n_far:], here, 10
        )
        total = own + noise[0] * vectors
        for i, k in enumerate(lines):
            back = [(b, a) for a, b in along_line(k)]
            sent = partial[i * here : (i + 1) * here] if i < len(far_lines) else partial_near
            total = total + lax.ppermute(sent, AXES, back)
        return total

    placed = (P(AXES, None), P(AXES, None), P(), P(), P())
    return jax.shard_map(per_device, mesh=mesh, in_specs=placed, out_specs=P(AXES, None), check_vma=False)
```

time: 42 us -> 33.2 us (0.79)
  waiting for transfers between devices: 19.6 us -> 9.23 us
  Pallas kernels: 0 us -> 6.75 us
  matrix products: 4.21 us -> 0 us
  local copies, waits for them, and re-layouts: 1.93 us -> 1.06 us
    pallas_call x0 -> x6, Pallas kernels: none -> 6.75 us  [the longest x4 6.49 us: times_columns(): pl.pallas_call(functools.partial(tile_kernel, (len(parts), start is not N...]
    ppermute x3, waiting for transfers between devices: 7.98 us -> 1.68 us  [per_device(): lax.ppermute(both, AXES, along_outer(k))]
    dot_general x2 -> x0, matrix products: 4.21 us -> none  [the longest x1 2.54 us: per_device(): jnp.dot(tile, values, precision=lax.Precision.HIGHEST, preferred_element_...]
    ppermute x6, waiting for transfers between devices: 11.7 us -> 7.54 us  [the longest x2 4 us: per_device(): far = [lax.ppermute(points, AXES, along_line(k)) for k in far_lines]]
    ppermute x6, starting transfers between devices: 8.91 us -> 10.2 us  [the longest x2 5.05 us: per_device(): far = [lax.ppermute(points, AXES, along_line(k)) for k in far_lines]]
    ppermute x3, starting transfers between devices: 4.54 us -> 3.55 us  [per_device(): lax.ppermute(both, AXES, along_outer(k))]
    concatenate x1, local copies, waits for them, and re-layouts: 0.83 us -> 0.01 us  [per_device(): both = jnp.concatenate([points, vectors], axis=1)]
    unnamed x10 -> x7, local copies, waits for them, and re-layouts: 1.04 us -> 0.99 us
  transfers between devices with their start and end apart: 10 -> 10, of which waited for: 6 -> 4; matrix products, arithmetic and copies ran while one was open for 0% -> 3% of each run, Pallas kernels for 0% -> 16%
where the time goes in v2:
time: 33.2 us; the launch traced here: 33 us
  starting transfers between devices  13.8 us (42%)
  waiting for transfers between devices  9.23 us (28%)
  Pallas kernels  6.75 us (20%)
  between operations  1.47 us (4%)
  local copies, waits for them, and re-layouts  1.06 us (3%)
  other arithmetic  0.69 us (2%)
    pallas_call x4, Pallas kernels, times_columns(): pl.pallas_call(functools.partial(tile_kernel, (len(parts), start is not N...  6.49 us
    ppermute x2, starting transfers between devices, per_device(): far = [lax.ppermute(points, AXES, along_line(k)) for k in far_lines]  5.05 us
    ppermute x3, starting transfers between devices, per_device(): total = total + lax.ppermute(sent, AXES, back)  4.52 us
    ppermute x2, waiting for transfers between devices, per_device(): far = [lax.ppermute(points, AXES, along_line(k)) for k in far_lines]  4 us
    ppermute x3, starting transfers between devices, per_device(): lax.ppermute(both, AXES, along_outer(k))  3.55 us
    ppermute x1, waiting for transfers between devices, per_device(): near = lax.ppermute(late[0], AXES, along_line(near_line))  1.99 us
    ppermute x3, waiting for transfers between devices, per_device(): lax.ppermute(both, AXES, along_outer(k))  1.68 us
    ppermute x3, waiting for transfers between devices, per_device(): total = total + lax.ppermute(sent, AXES, back)  1.55 us
  transfers between devices with their start and end apart: 10, of which 4 were waited for; matrix products, arithmetic and copies ran while one was open for 3% of the time, Pallas kernels for 16%

profile of v2, /device:TPU:0, one launch (start us, length us, event | category | flops | bytes accessed | tf_op | source)
XLA Modules:
  0.0 33.0 jit_solution(3558855171128218037)
XLA Ops:
  0.0 0.0 copy-start.2
  0.0 5.0 %collective-permute-start.4 = (f32[112,256]{1,0:T(8,128)}, f32[112,256]{1,0:T(8,128)S(1)}, u32[]{:S(2)}, u32[]{:S(2)}) collective-permute-start(f32[112,256]{1,0:T(8,128)} %refs_2_.1), channel_id=1, source_target_pairs={{0,6},{1,7},{2,4},{3,5},{4,2},{5,3},{6,0},{7,1},{8,14},{9,15},{10,... | collective-permute-start | bytes 344072 | tf_op jit(solution)/shard_map/ppermute | solution.py:166
  5.1 0.0 collective-permute-start.5
  5.1 1.0 %constant_dynamic-update-slice_fusion.1 = f32[112,384]{1,0:T(8,128)S(1)} fusion(f32[112,256]{1,0:T(8,128)} %refs_2_.1), kind=kLoop, calls=%fused_computation.3 | loop fusion | bytes 229376
  6.0 0.0 copy-done.2
  6.0 0.0 copy-start
  6.1 1.6 %collective-permute-start.2 = (f32[112,384]{1,0:T(8,128)S(1)}, f32[112,384]{1,0:T(8,128)S(1)}, u32[]{:S(2)}, u32[]{:S(2)}) collective-permute-start(f32[112,384]{1,0:T(8,128)S(1)} %constant_dynamic-update-slice_fusion), channel_id=1, source_target_pairs={{0,8},{1,9},{2,10},{3,11},{4,12},{5,13},{6,14},{7,15},{8,0},{9,1},... | collective-permute-start | bytes 516104 | tf_op jit(solution)/shard_map/ppermute | solution.py:168
  7.6 1.5 %collective-permute-start.1 = (f32[112,384]{1,0:T(8,128)S(1)}, f32[112,384]{1,0:T(8,128)S(1)}, u32[]{:S(2)}, u32[]{:S(2)}) collective-permute-start(f32[112,384]{1,0:T(8,128)S(1)} %constant_dynamic-update-slice_fusion), channel_id=1, source_target_pairs={{0,16},{1,17},{2,18},{3,19},{4,20},{5,21},{6,22},{7,23},{8,24},{9,... | collective-permute-start | bytes 516104 | tf_op jit(solution)/shard_map/ppermute | solution.py:168
  9.1 0.5 %collective-permute-start = (f32[112,384]{1,0:T(8,128)S(1)}, f32[112,384]{1,0:T(8,128)S(1)}, u32[]{:S(2)}, u32[]{:S(2)}) collective-permute-start(f32[112,384]{1,0:T(8,128)S(1)} %constant_dynamic-update-slice_fusion), channel_id=1, source_target_pairs={{0,24},{1,25},{2,26},{3,27},{4,28},{5,29},{6,30},{7,31},{8,16},{9,... | collective-permute-start | bytes 516104 | tf_op jit(solution)/shard_map/ppermute | solution.py:168
  10.9 0.0 copy-start.1
  10.9 0.0 collective-permute-done.4.refs_0_
  10.9 4.0 %collective-permute-done.5.refs_1_ = f32[112,256]{1,0:T(8,128)S(1)} collective-permute-done((f32[112,256]{1,0:T(8,128)}, f32[112,256]{1,0:T(8,128)S(1)}, u32[]{:S(2)}, u32[]{:S(2)}) %collective-permute-start.5) | collective-permute-done | bytes 114720 | tf_op jit(solution)/shard_map/ppermute | solution.py:166
  14.9 0.0 copy-done
  14.9 0.0 copy-done.1
  14.9 0.2 rows.2
  15.2 0.0 collective-permute-done.2
  15.2 1.7 %collective-permute-done.1 = f32[112,384]{1,0:T(8,128)S(1)} collective-permute-done((f32[112,384]{1,0:T(8,128)S(1)}, f32[112,384]{1,0:T(8,128)S(1)}, u32[]{:S(2)}, u32[]{:S(2)}) %collective-permute-start.1) | collective-permute-done | bytes 172064 | tf_op jit(solution)/shard_map/ppermute | solution.py:168
  16.9 0.0 collective-permute-done
  16.9 0.6 %collective-permute-start.8 = (f32[112,256]{1,0:T(8,128)S(1)}, f32[112,256]{1,0:T(8,128)S(1)}, u32[]{:S(2)}, u32[]{:S(2)}) collective-permute-start(f32[112,256]{1,0:T(8,128)S(1)} %copy-done), channel_id=1, source_target_pairs={{0,2},{1,3},{2,0},{3,1},{4,6},{5,7},{6,4},{7,5},{8,10},{9,11},{10,... | collective-permute-start | bytes 344072 | tf_op jit(solution)/shard_map/ppermute | solution.py:170
  17.5 0.1 collective-permute-start.3
  17.6 2.0 %tile.4 = f32[336,128]{1,0:T(8,128)S(1)} custom-call(f32[1,256]{1,0:T(1,128)S(1)} %bitcast.4, f32[1]{0:T(128)S(6)} %copy.7.amp_ref, f32[448,384]{1,0:T(8,128)S(1)} %pad_maximum_fusion.refs_0_, bf16[336,512]{1,0:T(8,128)(2,1)S(1)} %get-tuple-element.16.refs_1_, f32[336,128]{1,0:T(8,128)S(1)} %get-tuple-element.17.refs_2_), custom_call_target="tpu_custom_call" | custom-call | flops 20000000000 | bytes 1024 | tf_op jit(solution)/shard_map/tile/pallas_call | solution.py:127
  19.7 2.0 %collective-permute-done.8.refs_0_ = f32[112,256]{1,0:T(8,128)S(1)} collective-permute-done((f32[112,256]{1,0:T(8,128)S(1)}, f32[112,256]{1,0:T(8,128)S(1)}, u32[]{:S(2)}, u32[]{:S(2)}) %collective-permute-start.8) | collective-permute-done | bytes 114720 | tf_op jit(solution)/shard_map/ppermute | solution.py:170
  21.7 0.1 rows.3
  21.8 0.0 collective-permute-done.3.refs_0_.refs_1_
  21.8 1.5 %tile.6 = f32[224,128]{1,0:T(8,128)S(1)} custom-call(f32[1,256]{1,0:T(1,128)S(1)} %bitcast.6, f32[1]{0:T(128)S(6)} %copy.7.amp_ref, f32[448,384]{1,0:T(8,128)S(1)} %collective-permute-done.3.refs_0_.refs_1_, bf16[224,512]{1,0:T(8,128)(2,1)S(1)} %slice.27.refs_1_, f32[224,128]{1,0:T(8,128)S(1)} %slice.28.refs_2_, f32[224,128]{1,0:T(8,128)S(1)} %slice.33.refs_3_), custom_call_target="tpu_custom_call" | custom-call | flops 10000000000 | bytes 1024 | tf_op jit(solution)/shard_map/tile/pallas_call | solution.py:127
  23.3 2.2 %collective-permute-start.6 = (f32[112,128]{1,0:T(8,128)S(1)}, f32[112,128]{1,0:T(8,128)S(1)}, u32[]{:S(2)}, u32[]{:S(2)}) collective-permute-start(f32[112,128]{1,0:T(8,128)S(1)} %get-tuple-element.21), channel_id=1, source_target_pairs={{6,0},{7,1},{4,2},{5,3},{2,4},{3,5},{0,6},{1,7},{14,8},{15,9},{12,... | collective-permute-start | bytes 172040 | tf_op jit(solution)/shard_map/ppermute | solution.py:188
  25.6 0.6 %collective-permute-start.7 = (f32[112,128]{1,0:T(8,128)S(1)}, f32[112,128]{1,0:T(8,128)S(1)}, u32[]{:S(2)}, u32[]{:S(2)}) collective-permute-start(f32[112,128]{1,0:T(8,128)S(1)} %get-tuple-element.22), channel_id=1, source_target_pairs={{4,0},{5,1},{6,2},{7,3},{0,4},{1,5},{2,6},{3,7},{12,8},{13,9},{14,... | collective-permute-start | bytes 172040 | tf_op jit(solution)/shard_map/ppermute | solution.py:188
  26.2 1.9 %tile.7 = f32[112,128]{1,0:T(8,128)S(1)} custom-call(f32[1,256]{1,0:T(1,128)S(1)} %bitcast.7, f32[1]{0:T(128)S(6)} %copy.7.amp_ref, f32[448,384]{1,0:T(8,128)S(1)} %pad_maximum_fusion.refs_0_, f32[448,384]{1,0:T(8,128)S(1)} %collective-permute-done.3.refs_0_.refs_1_, bf16[112,512]{1,0:T(8,128)(2,1)S(1)} %get-tuple-element.19.refs_2_, ...), custom_call_target="tpu_custom_call" | custom-call | flops 10000000000 | bytes 1024 | tf_op jit(solution)/shard_map/tile/pallas_call | solution.py:127
  28.1 1.6 %collective-permute-start.9 = (f32[112,128]{1,0:T(8,128)S(1)}, f32[112,128]{1,0:T(8,128)S(1)}, u32[]{:S(2)}, u32[]{:S(2)}) collective-permute-start(f32[112,128]{1,0:T(8,128)S(1)} %tile.7), channel_id=1, source_target_pairs={{2,0},{3,1},{0,2},{1,3},{6,4},{7,5},{4,6},{5,7},{10,8},{11,9},{8,1... | collective-permute-start | bytes 172040 | tf_op jit(solution)/shard_map/ppermute | solution.py:188
  29.7 1.0 %tile.5 = f32[112,128]{1,0:T(8,128)S(1)} custom-call(f32[1,256]{1,0:T(1,128)S(1)} %bitcast.8, f32[1]{0:T(128)S(6)} %copy.7.amp_ref, f32[448,384]{1,0:T(8,128)S(1)} %collective-permute-done.3.refs_0_.refs_1_, bf16[112,512]{1,0:T(8,128)(2,1)S(1)} %slice.24.refs_1_, f32[112,128]{1,0:T(8,128)S(1)} %slice.25.refs_2_, f32[112,128]{1,0:T(8,128)S(1)} %slice.32.refs_3_), custom_call_target="tpu_custom_call" | custom-call | flops 10000000000 | bytes 1024 | tf_op jit(solution)/shard_map/tile/pallas_call | solution.py:127
  30.8 0.0 collective-permute-done.6
  30.8 0.0 collective-permute-done.7
  30.8 1.5 %collective-permute-done.9 = f32[112,128]{1,0:T(8,128)S(1)} collective-permute-done((f32[112,128]{1,0:T(8,128)S(1)}, f32[112,128]{1,0:T(8,128)S(1)}, u32[]{:S(2)}, u32[]{:S(2)}) %collective-permute-start.9) | collective-permute-done | bytes 57376 | tf_op jit(solution)/shard_map/ppermute | solution.py:188
  32.4 0.6 %add_add_fusion = f32[112,128]{1,0:T(8,128)} fusion(f32[112,128]{1,0:T(8,128)S(1)} %collective-permute-done.9, f32[112,128]{1,0:T(8,128)S(1)} %collective-permute-done.7, f32[112,128]{1,0:T(8,128)S(1)} %collective-permute-done.6, f32[112,128]{1,0:T(8,128)S(1)} %tile.5, f32[112,128]{1,0:T(8,128)S(1)} %copy-done.2, f32[]{:T(128)} %bitcast.2), kind=kLoop, calls=%fused_computation.1 | loop fusion | flops 71680 | bytes 344068 | tf_op jit(solution)/shard_map/add | solution.py:188
  (9 shorter events, 0.1 us)
Async XLA Ops:
  0.0 6.0 %copy-start.2 = (f32[112,128]{1,0:T(8,128)S(1)}, f32[112,128]{1,0:T(8,128)}, u32[]{:S(2)}) copy-start(f32[112,128]{1,0:T(8,128)} %param.6) | copy-start | bytes 172036
  0.0 10.9 %collective-permute-start.4 = (f32[112,256]{1,0:T(8,128)}, f32[112,256]{1,0:T(8,128)S(1)}, u32[]{:S(2)}, u32[]{:S(2)}) collective-permute-start(f32[112,256]{1,0:T(8,128)} %refs_2_.1), channel_id=1, source_target_pairs={{0,6},{1,7},{2,4},{3,5},{4,2},{5,3},{6,0},{7,1},{8,14},{9,15},{10,... | collective-permute-start | bytes 344072 | tf_op jit(solution)/shard_map/ppermute | solution.py:166
  5.1 9.9 %collective-permute-start.5 = (f32[112,256]{1,0:T(8,128)}, f32[112,256]{1,0:T(8,128)S(1)}, u32[]{:S(2)}, u32[]{:S(2)}) collective-permute-start(f32[112,256]{1,0:T(8,128)} %refs_2_.1), channel_id=1, source_target_pairs={{0,4},{1,5},{2,6},{3,7},{4,0},{5,1},{6,2},{7,3},{8,12},{9,13},{10,... | collective-permute-start | bytes 344072 | tf_op jit(solution)/shard_map/ppermute | solution.py:166
  6.0 8.9 %copy-start = (f32[112,256]{1,0:T(8,128)S(1)}, f32[112,256]{1,0:T(8,128)}, u32[]{:S(2)}) copy-start(f32[112,256]{1,0:T(8,128)} %refs_2_.1) | copy-start | bytes 344068
  6.1 9.1 %collective-permute-start.2 = (f32[112,384]{1,0:T(8,128)S(1)}, f32[112,384]{1,0:T(8,128)S(1)}, u32[]{:S(2)}, u32[]{:S(2)}) collective-permute-start(f32[112,384]{1,0:T(8,128)S(1)} %constant_dynamic-update-slice_fusion), channel_id=1, source_target_pairs={{0,8},{1,9},{2,10},{3,11},{4,12},{5,13},{6,14},{7,15},{8,0},{9,1},... | collective-permute-start | bytes 516104 | tf_op jit(solution)/shard_map/ppermute | solution.py:168
  7.6 9.2 %collective-permute-start.1 = (f32[112,384]{1,0:T(8,128)S(1)}, f32[112,384]{1,0:T(8,128)S(1)}, u32[]{:S(2)}, u32[]{:S(2)}) collective-permute-start(f32[112,384]{1,0:T(8,128)S(1)} %constant_dynamic-update-slice_fusion), channel_id=1, source_target_pairs={{0,16},{1,17},{2,18},{3,19},{4,20},{5,21},{6,22},{7,23},{8,24},{9,... | collective-permute-start | bytes 516104 | tf_op jit(solution)/shard_map/ppermute | solution.py:168
  9.1 7.7 %collective-permute-start = (f32[112,384]{1,0:T(8,128)S(1)}, f32[112,384]{1,0:T(8,128)S(1)}, u32[]{:S(2)}, u32[]{:S(2)}) collective-permute-start(f32[112,384]{1,0:T(8,128)S(1)} %constant_dynamic-update-slice_fusion), channel_id=1, source_target_pairs={{0,24},{1,25},{2,26},{3,27},{4,28},{5,29},{6,30},{7,31},{8,16},{9,... | collective-permute-start | bytes 516104 | tf_op jit(solution)/shard_map/ppermute | solution.py:168
  10.9 4.0 %copy-start.1 = (f32[256]{0:T(256)S(1)}, f32[256]{0:T(256)}, u32[]{:S(2)}) copy-start(f32[256]{0:T(256)} %param.7) | copy-start | bytes 3076
  16.9 4.8 %collective-permute-start.8 = (f32[112,256]{1,0:T(8,128)S(1)}, f32[112,256]{1,0:T(8,128)S(1)}, u32[]{:S(2)}, u32[]{:S(2)}) collective-permute-start(f32[112,256]{1,0:T(8,128)S(1)} %copy-done), channel_id=1, source_target_pairs={{0,2},{1,3},{2,0},{3,1},{4,6},{5,7},{6,4},{7,5},{8,10},{9,11},{10,... | collective-permute-start | bytes 344072 | tf_op jit(solution)/shard_map/ppermute | solution.py:170
  17.5 4.2 %collective-permute-start.3 = (f32[448,384]{1,0:T(8,128)S(1)}, f32[448,384]{1,0:T(8,128)S(1)}, u32[]{:S(2)}, u32[]{:S(2)}) collective-permute-start(f32[448,384]{1,0:T(8,128)S(1)} %pad_maximum_fusion.refs_0_), channel_id=1, source_target_pairs={{0,1},{1,0},{2,3},{3,2},{4,5},{5,4},{6,7},{7,6},{8,9},{9,8},{10,11... | collective-permute-start | bytes 2064392 | tf_op jit(solution)/shard_map/ppermute | solution.py:172
  23.3 7.5 %collective-permute-start.6 = (f32[112,128]{1,0:T(8,128)S(1)}, f32[112,128]{1,0:T(8,128)S(1)}, u32[]{:S(2)}, u32[]{:S(2)}) collective-permute-start(f32[112,128]{1,0:T(8,128)S(1)} %get-tuple-element.21), channel_id=1, source_target_pairs={{6,0},{7,1},{4,2},{5,3},{2,4},{3,5},{0,6},{1,7},{14,8},{15,9},{12,... | collective-permute-start | bytes 172040 | tf_op jit(solution)/shard_map/ppermute | solution.py:188
  25.6 5.2 %collective-permute-start.7 = (f32[112,128]{1,0:T(8,128)S(1)}, f32[112,128]{1,0:T(8,128)S(1)}, u32[]{:S(2)}, u32[]{:S(2)}) collective-permute-start(f32[112,128]{1,0:T(8,128)S(1)} %get-tuple-element.22), channel_id=1, source_target_pairs={{4,0},{5,1},{6,2},{7,3},{0,4},{1,5},{2,6},{3,7},{12,8},{13,9},{14,... | collective-permute-start | bytes 172040 | tf_op jit(solution)/shard_map/ppermute | solution.py:188
  28.1 4.2 %collective-permute-start.9 = (f32[112,128]{1,0:T(8,128)S(1)}, f32[112,128]{1,0:T(8,128)S(1)}, u32[]{:S(2)}, u32[]{:S(2)}) collective-permute-start(f32[112,128]{1,0:T(8,128)S(1)} %tile.7), channel_id=1, source_target_pairs={{2,0},{3,1},{0,2},{1,3},{6,4},{7,5},{4,6},{5,7},{10,8},{11,9},{8,1... | collective-permute-start | bytes 172040 | tf_op jit(solution)/shard_map/ppermute | solution.py:188

commit v3 on v1

v3 whole, which is shorter than its diff:
```python
import functools
import math

import jax
import jax.numpy as jnp
from jax import lax
from jax.experimental import pallas as pl
from jax.experimental.pallas import tpu as pltpu
from jax.sharding import PartitionSpec as P

AXES = ("outer", "inner")
CORES = 2
VMEM = pl.BlockSpec(memory_space=pltpu.VMEM)
SMEM = pl.BlockSpec(memory_space=pltpu.SMEM)
BF16 = jnp.bfloat16
F32 = jnp.float32
LIMIT = 24 * 1024 * 1024
LANES = 128
LN2 = math.log(2.0)


def partner(index, step, size):
    return index ^ step if size & (size - 1) == 0 else (index + step) % size


def split(x):
    high = x.astype(BF16)
    return high, (x - high.astype(F32)).astype(BF16)


def cost(us):
    return pl.CostEstimate(flops=int(us * 1e9), bytes_accessed=1024, transcendentals=0)


def params():
    return pltpu.CompilerParams(vmem_limit_bytes=LIMIT)


def kernel_scale(scale_ref):
    return (math.sqrt(5.0) / LN2) / scale_ref[...]


def norm_lanes(norm, first):
    high, mid = split(norm)
    low = (norm - high.astype(F32) - mid.astype(F32)).astype(BF16)
    lane = lax.broadcasted_iota(jnp.int32, (norm.shape[0], LANES), 1)
    out = jnp.where((lane >= 3 - first) & (lane < 6 - first), 1.0, 0.0)
    for i, part in enumerate((high, mid, low)):
        out = jnp.where(lane == first + i, part.astype(F32), out)
    return out.astype(BF16)


def put(ref, at, parts):
    start = 0
    for part in parts:
        ref[at, start : start + part.shape[1]] = part
        start += part.shape[1]


def fill_rows(x_ref, at, block, scale):
    x = block * scale
    norm = jnp.sum(x * x, axis=1, keepdims=True)
    high, low = split(-2.0 * x)
    put(x_ref, at, (high, low, high, low, norm_lanes(norm, 0)))


def fill_cols(y_ref, v_ref, block, scale, amplitude):
    features = scale.shape[1]
    y = block[:, :features] * scale
    norm = jnp.sum(y * y, axis=1, keepdims=True)
    high, low = split(y)
    put(y_ref, slice(None), (high, high, low, low, norm_lanes(norm, 3)))
    put(v_ref, slice(None), split(block[:, features:] * (amplitude * LN2)))


def rows_kernel(places, scale_ref, *refs):
    x_ref = refs[-1]
    scale = kernel_scale(scale_ref)
    for place, block in zip(places, refs):
        here = block.shape[0]
        fill_rows(x_ref, pl.ds(place * here, here), block[...], scale)


def prepare_rows(scale, blocks, places, total, x, us):
    here, features = blocks[0].shape
    given = [scale, *blocks] + ([] if x is None else [x])
    return pl.pallas_call(
        functools.partial(rows_kernel, places),
        out_shape=jax.ShapeDtypeStruct((here * total, 4 * features + LANES), BF16),
        in_specs=[VMEM] * len(given),
        out_specs=VMEM,
        input_output_aliases={} if x is None else {len(given) - 1: 0},
        compiler_params=params(),
        cost_estimate=cost(us),
        name="rows",
    )(*given)


def times_tile(x_ref, first, count, y_ref, v_ref):
    columns = v_ref.shape[1] // 2
    n = y_ref.shape[0]
    x = x_ref[first : first + count, :]
    total = None
    for at in range(0, n, 256):
        cols = slice(at, min(at + 256, n))
        b2 = lax.dot_general(x, y_ref[cols, :], (((1,), (1,)), ((), ())), preferred_element_type=F32)
        b2 = jnp.maximum(b2, 1e-30)
        b = b2 * lax.rsqrt(b2)
        tile = (b2 * (LN2 / 3.0) + b + (1.0 / LN2)) * jnp.exp2(-b)
        high, low = split(tile)
        part = jnp.dot(high, v_ref[cols, :], preferred_element_type=F32)
        part = part[:, :columns] + part[:, columns:]
        part = part + jnp.dot(low, v_ref[cols, :columns], preferred_element_type=F32)
        total = part if total is None else total + part
    return total


def tile_kernel(first, here, sizes, has_start, scale_ref, amp_ref, cols_ref, x_ref, *refs):
    n_in = 1 if has_start else 0
    given, outs, (y_ref, v_ref) = refs[:n_in], refs[n_in:-2], refs[-2:]
    fill_cols(y_ref, v_ref, cols_ref[...], kernel_scale(scale_ref), amp_ref[0])
    count = sum(sizes) * here
    total = times_tile(x_ref, first * here, count, y_ref, v_ref)
    if has_start:
        total = total + given[0][first * here : first * here + count, :]
    at = 0
    for size, out in zip(sizes, outs):
        out[...] = total[at * here : (at + size) * here, :]
        at += size


def times_columns(scale, amplitude, cols, x, first, sizes, start, here, us):
    n, width = cols.shape
    features = scale.shape[1]
    columns = width - features
    given = [scale, amplitude, cols, x] + ([] if start is None else [start])
    return pl.pallas_call(
        functools.partial(tile_kernel, first, here, sizes, start is not None),
        out_shape=[jax.ShapeDtypeStruct((size * here, columns), F32) for size in sizes],
        in_specs=[VMEM, SMEM] + [VMEM] * (len(given) - 2),
        out_specs=[VMEM] * len(sizes),
        scratch_shapes=[
            pltpu.VMEM((n, 4 * features + LANES), BF16),
            pltpu.VMEM((n, 2 * columns), BF16),
        ],
        compiler_params=params(),
        cost_estimate=cost(us),
        name="tile",
    )(*given)


def solution(mesh):
    n_outer, n_inner = mesh.shape["outer"], mesh.shape["inner"]
    n_line = n_inner // CORES

    def linear(outer, line, core):
        return outer * n_inner + line * CORES + core

    places = [(o, z, c) for o in range(n_outer) for z in range(n_line) for c in range(CORES)]

    def along_line(step):
        return [(linear(o, z, c), linear(o, partner(z, step, n_line), c)) for o, z, c in places]

    def along_outer(step):
        return [(linear(o, z, c), linear(partner(o, step, n_outer), z, c)) for o, z, c in places]

    other_core = [(linear(o, z, c), linear(o, z, c ^ 1)) for o, z, c in places]

    def per_device(points, vectors, lengthscales, outputscale, noise):
        here = points.shape[0]
        scale = lengthscales[None, :]
        lines = list(range(n_line - 1, 0, -1))
        far_lines, near_line = lines[:-1], lines[-1]
        n_far = len(far_lines)
        far = [lax.ppermute(points, AXES, along_line(k)) for k in far_lines]
        both = jnp.concatenate([points, vectors], axis=1)
        got = [lax.ppermute(both, AXES, along_outer(k)) for k in range(n_outer - 1, 0, -1)]
        late = lax.optimization_barrier((points, far[0]))
        near = lax.ppermute(late[0], AXES, along_line(near_line))
        cols_mine = jnp.concatenate([both, *got], axis=0)
        cols_theirs = lax.ppermute(cols_mine, AXES, other_core)

        x = prepare_rows(scale, [late[1], points], [0, n_far], n_line, None, 40)
        x = prepare_rows(scale, [*far[1:], near], [*range(1, n_far), n_line - 1], n_line, x, 1)
        tile = functools.partial(times_columns, scale, outputscale)
        (mine,) = tile(cols_mine, x, 0, [n_line], None, here, 20)
        back_far = tile(cols_theirs, x, 0, [1] * n_far, mine, here, 10)
        own, back_near = tile(cols_theirs, x, n_far, [1, 1], mine, here, 10)
        total = own + noise[0] * vectors
        for k, sent in zip(lines, [*back_far, back_near]):
            total = total + lax.ppermute(sent, AXES, [(b, a) for a, b in along_line(k)])
        return total

    placed = (P(AXES, None), P(AXES, None), P(), P(), P())
    return jax.shard_map(per_device, mesh=mesh, in_specs=placed, out_specs=P(AXES, None), check_vma=False)
```

time: 42 us -> 29.3 us (0.70)
  waiting for transfers between devices: 19.6 us -> 7.44 us
  Pallas kernels: 0 us -> 4.72 us
  matrix products: 4.21 us -> 0 us
  local copies, waits for them, and re-layouts: 1.93 us -> 0.96 us
    ppermute x6, waiting for transfers between devices: 11.7 us -> 1.98 us  [the longest x3 1.97 us: per_device(): total = total + lax.ppermute(sent, AXES, [(b, a) for a, b in along_line(k)])]
    pallas_call x0 -> x5, Pallas kernels: none -> 4.72 us  [the longest x3 4.44 us: times_columns(): pl.pallas_call(functools.partial(tile_kernel, first, here, sizes, start i...]
    dot_general x2 -> x0, matrix products: 4.21 us -> none  [the longest x1 2.54 us: per_device(): jnp.dot(tile, values, precision=lax.Precision.HIGHEST, preferred_element_...]
    ppermute x3, waiting for transfers between devices: 7.98 us -> 5.46 us  [per_device(): lax.ppermute(both, AXES, along_outer(k))]
    ppermute x6, starting transfers between devices: 8.91 us -> 10.3 us  [the longest x2 5.05 us: per_device(): far = [lax.ppermute(points, AXES, along_line(k)) for k in far_lines]]
    ppermute x3, starting transfers between devices: 4.54 us -> 3.55 us  [per_device(): lax.ppermute(both, AXES, along_outer(k))]
    concatenate x1, local copies, waits for them, and re-layouts: 0.83 us -> 0.01 us  [per_device(): both = jnp.concatenate([points, vectors], axis=1)]
    unnamed x10 -> x7, local copies, waits for them, and re-layouts: 1.04 us -> 0.95 us
  transfers between devices with their start and end apart: 10 -> 10, of which waited for: 6 -> 6; matrix products, arithmetic and copies ran while one was open for 0% -> 3% of each run, Pallas kernels for 0% -> 12%
where the time goes in v3:
time: 29.3 us; the launch traced here: 29.2 us
  starting transfers between devices  13.9 us (47%)
  waiting for transfers between devices  7.44 us (25%)
  Pallas kernels  4.72 us (16%)
  between operations  1.4 us (5%)
  local copies, waits for them, and re-layouts  0.96 us (3%)
  other arithmetic  0.69 us (2%)
    ppermute x3, waiting for transfers between devices, per_device(): lax.ppermute(both, AXES, along_outer(k))  5.46 us
    ppermute x2, starting transfers between devices, per_device(): far = [lax.ppermute(points, AXES, along_line(k)) for k in far_lines]  5.05 us
    ppermute x3, starting transfers between devices, per_device(): total = total + lax.ppermute(sent, AXES, [(b, a) for a, b in along_line(k)])  4.52 us
    pallas_call x3, Pallas kernels, times_columns(): pl.pallas_call(functools.partial(tile_kernel, first, here, sizes, start i...  4.44 us
    ppermute x3, starting transfers between devices, per_device(): lax.ppermute(both, AXES, along_outer(k))  3.55 us
    ppermute x3, waiting for transfers between devices, per_device(): total = total + lax.ppermute(sent, AXES, [(b, a) for a, b in along_line(k)])  1.97 us
    unnamed x7, local copies, waits for them, and re-layouts  0.95 us
    ppermute x1, starting transfers between devices, per_device(): near = lax.ppermute(late[0], AXES, along_line(near_line))  0.74 us
  transfers between devices with their start and end apart: 10, of which 6 were waited for; matrix products, arithmetic and copies ran while one was open for 3% of the time, Pallas kernels for 12%

profile of v3, /device:TPU:0, one launch (start us, length us, event | category | flops | bytes accessed | tf_op | source)
XLA Modules:
  0.0 29.2 jit_solution(4039091340086732634)
XLA Ops:
  0.0 0.0 copy-start
  0.0 0.0 copy-start.2
  0.0 5.0 %collective-permute-start.5 = (f32[112,256]{1,0:T(8,128)}, f32[112,256]{1,0:T(8,128)S(1)}, u32[]{:S(2)}, u32[]{:S(2)}) collective-permute-start(f32[112,256]{1,0:T(8,128)} %refs_1_.1), channel_id=1, source_target_pairs={{0,6},{1,7},{2,4},{3,5},{4,2},{5,3},{6,0},{7,1},{8,14},{9,15},{10,... | collective-permute-start | bytes 344072 | tf_op jit(solution)/shard_map/ppermute | solution.py:175
  5.1 0.9 %constant_dynamic-update-slice_fusion.1 = f32[112,384]{1,0:T(8,128)S(1)} fusion(f32[112,256]{1,0:T(8,128)} %refs_1_.1), kind=kLoop, calls=%fused_computation.3 | loop fusion | bytes 229376
  6.0 0.0 copy-done.2
  6.0 2.5 %collective-permute-start = (f32[112,384]{1,0:T(8,128)S(1)}, f32[112,384]{1,0:T(8,128)S(1)}, u32[]{:S(2)}, u32[]{:S(2)}) collective-permute-start(f32[112,384]{1,0:T(8,128)S(1)} %constant_dynamic-update-slice_fusion), channel_id=1, source_target_pairs={{0,24},{1,25},{2,26},{3,27},{4,28},{5,29},{6,30},{7,31},{8,16},{9,... | collective-permute-start | bytes 516104 | tf_op jit(solution)/shard_map/ppermute | solution.py:177
  8.5 0.5 %collective-permute-start.1 = (f32[112,384]{1,0:T(8,128)S(1)}, f32[112,384]{1,0:T(8,128)S(1)}, u32[]{:S(2)}, u32[]{:S(2)}) collective-permute-start(f32[112,384]{1,0:T(8,128)S(1)} %constant_dynamic-update-slice_fusion), channel_id=1, source_target_pairs={{0,16},{1,17},{2,18},{3,19},{4,20},{5,21},{6,22},{7,23},{8,24},{9,... | collective-permute-start | bytes 516104 | tf_op jit(solution)/shard_map/ppermute | solution.py:177
  9.0 0.5 %collective-permute-start.2 = (f32[112,384]{1,0:T(8,128)S(1)}, f32[112,384]{1,0:T(8,128)S(1)}, u32[]{:S(2)}, u32[]{:S(2)}) collective-permute-start(f32[112,384]{1,0:T(8,128)S(1)} %constant_dynamic-update-slice_fusion), channel_id=1, source_target_pairs={{0,8},{1,9},{2,10},{3,11},{4,12},{5,13},{6,14},{7,15},{8,0},{9,1},... | collective-permute-start | bytes 516104 | tf_op jit(solution)/shard_map/ppermute | solution.py:177
  9.6 0.0 copy-done
  9.6 0.0 collective-permute-start.4
  10.2 0.0 copy-start.1
  10.2 0.0 collective-permute-done.5.refs_0_
  10.3 0.7 %collective-permute-start.6 = (f32[112,256]{1,0:T(8,128)S(1)}, f32[112,256]{1,0:T(8,128)S(1)}, u32[]{:S(2)}, u32[]{:S(2)}) collective-permute-start(f32[112,256]{1,0:T(8,128)S(1)} %copy-done), channel_id=1, source_target_pairs={{0,2},{1,3},{2,0},{3,1},{4,6},{5,7},{6,4},{7,5},{8,10},{9,11},{10,... | collective-permute-start | bytes 344072 | tf_op jit(solution)/shard_map/ppermute | solution.py:179
  11.0 0.0 copy-done.1
  11.0 0.1 rows.2.refs_2_
  11.1 2.9 %collective-permute-done = f32[112,384]{1,0:T(8,128)S(1)} collective-permute-done((f32[112,384]{1,0:T(8,128)S(1)}, f32[112,384]{1,0:T(8,128)S(1)}, u32[]{:S(2)}, u32[]{:S(2)}) %collective-permute-start) | collective-permute-done | bytes 172064 | tf_op jit(solution)/shard_map/ppermute | solution.py:177
  14.0 2.5 %collective-permute-done.1 = f32[112,384]{1,0:T(8,128)S(1)} collective-permute-done((f32[112,384]{1,0:T(8,128)S(1)}, f32[112,384]{1,0:T(8,128)S(1)}, u32[]{:S(2)}, u32[]{:S(2)}) %collective-permute-start.1) | collective-permute-done | bytes 172064 | tf_op jit(solution)/shard_map/ppermute | solution.py:177
  16.5 0.1 collective-permute-done.2
  16.7 0.1 collective-permute-start.3
  16.7 0.0 collective-permute-done.4.refs_0_
  16.7 0.0 collective-permute-done.6.refs_1_
  16.8 0.1 rows.3.x_ref
  16.9 2.0 %tile.3.refs_0_ = f32[448,128]{1,0:T(8,128)S(1)} custom-call(f32[1,256]{1,0:T(1,128)S(1)} %bitcast.5, f32[1]{0:T(128)S(6)} %copy.9.amp_ref, f32[448,384]{1,0:T(8,128)S(1)} %pad_maximum_fusion.cols_ref, bf16[448,1152]{1,0:T(8,128)(2,1)S(1)} %rows.3.x_ref), custom_call_target="tpu_custom_call" | custom-call | flops 20000000000 | bytes 1024 | tf_op jit(solution)/shard_map/tile/pallas_call | solution.py:137
  18.9 0.0 collective-permute-done.3.cols_ref
  18.9 1.2 %tile.5 = (f32[112,128]{1,0:T(8,128)S(1)}, f32[112,128]{1,0:T(8,128)S(1)}) custom-call(f32[1,256]{1,0:T(1,128)S(1)} %bitcast.6, f32[1]{0:T(128)S(6)} %copy.9.amp_ref, f32[448,384]{1,0:T(8,128)S(1)} %collective-permute-done.3.cols_ref, bf16[448,1152]{1,0:T(8,128)(2,1)S(1)} %rows.3.x_ref, f32[448,128]{1,0:T(8,128)S(1)} %tile.3.refs_0_), custom_call_target="tpu_custom_call" | custom-call | flops 10000000000 | bytes 1024 | tf_op jit(solution)/shard_map/tile/pallas_call | solution.py:137
  20.1 1.6 %collective-permute-start.7 = (f32[112,128]{1,0:T(8,128)S(1)}, f32[112,128]{1,0:T(8,128)S(1)}, u32[]{:S(2)}, u32[]{:S(2)}) collective-permute-start(f32[112,128]{1,0:T(8,128)S(1)} %get-tuple-element.14), channel_id=1, source_target_pairs={{6,0},{7,1},{4,2},{5,3},{2,4},{3,5},{0,6},{1,7},{14,8},{15,9},{12,... | collective-permute-start | bytes 172040 | tf_op jit(solution)/shard_map/ppermute | solution.py:191
  21.8 0.0 collective-permute-start.8
  21.8 1.2 %tile.4 = (f32[112,128]{1,0:T(8,128)S(1)}, f32[112,128]{1,0:T(8,128)S(1)}) custom-call(f32[1,256]{1,0:T(1,128)S(1)} %bitcast.7, f32[1]{0:T(128)S(6)} %copy.9.amp_ref, f32[448,384]{1,0:T(8,128)S(1)} %collective-permute-done.3.cols_ref, bf16[448,1152]{1,0:T(8,128)(2,1)S(1)} %rows.3.x_ref, f32[448,128]{1,0:T(8,128)S(1)} %tile.3.refs_0_), custom_call_target="tpu_custom_call" | custom-call | flops 10000000000 | bytes 1024 | tf_op jit(solution)/shard_map/tile/pallas_call | solution.py:137
  23.0 2.9 %collective-permute-start.9 = (f32[112,128]{1,0:T(8,128)S(1)}, f32[112,128]{1,0:T(8,128)S(1)}, u32[]{:S(2)}, u32[]{:S(2)}) collective-permute-start(f32[112,128]{1,0:T(8,128)S(1)} %get-tuple-element.16), channel_id=1, source_target_pairs={{2,0},{3,1},{0,2},{1,3},{6,4},{7,5},{4,6},{5,7},{10,8},{11,9},{8,1... | collective-permute-start | bytes 172040 | tf_op jit(solution)/shard_map/ppermute | solution.py:191
  26.5 0.3 collective-permute-done.7
  26.8 1.3 %collective-permute-done.8 = f32[112,128]{1,0:T(8,128)S(1)} collective-permute-done((f32[112,128]{1,0:T(8,128)S(1)}, f32[112,128]{1,0:T(8,128)S(1)}, u32[]{:S(2)}, u32[]{:S(2)}) %collective-permute-start.8) | collective-permute-done | bytes 57376 | tf_op jit(solution)/shard_map/ppermute | solution.py:191
  28.2 0.4 %collective-permute-done.9 = f32[112,128]{1,0:T(8,128)S(1)} collective-permute-done((f32[112,128]{1,0:T(8,128)S(1)}, f32[112,128]{1,0:T(8,128)S(1)}, u32[]{:S(2)}, u32[]{:S(2)}) %collective-permute-start.9) | collective-permute-done | bytes 57376 | tf_op jit(solution)/shard_map/ppermute | solution.py:191
  28.5 0.6 %add_add_fusion = f32[112,128]{1,0:T(8,128)} fusion(f32[112,128]{1,0:T(8,128)S(1)} %collective-permute-done.9, f32[112,128]{1,0:T(8,128)S(1)} %collective-permute-done.8, f32[112,128]{1,0:T(8,128)S(1)} %collective-permute-done.7, f32[112,128]{1,0:T(8,128)S(1)} %get-tuple-element.13, f32[112,128]{1,0:T(8,128)S(1)} %copy-done.2, f32[]{:T(128)} %bitcast.2), kind=kLoop, calls=%fused_computation.1 | loop fusion | flops 71680 | bytes 344068 | tf_op jit(solution)/shard_map/add | solution.py:191
  (2 shorter events, 0.1 us)
Async XLA Ops:
  0.0 9.6 %copy-start = (f32[112,256]{1,0:T(8,128)S(1)}, f32[112,256]{1,0:T(8,128)}, u32[]{:S(2)}) copy-start(f32[112,256]{1,0:T(8,128)} %refs_1_.1) | copy-start | bytes 344068
  0.0 6.0 %copy-start.2 = (f32[112,128]{1,0:T(8,128)S(1)}, f32[112,128]{1,0:T(8,128)}, u32[]{:S(2)}) copy-start(f32[112,128]{1,0:T(8,128)} %param.6) | copy-start | bytes 172036
  0.0 10.2 %collective-permute-start.5 = (f32[112,256]{1,0:T(8,128)}, f32[112,256]{1,0:T(8,128)S(1)}, u32[]{:S(2)}, u32[]{:S(2)}) collective-permute-start(f32[112,256]{1,0:T(8,128)} %refs_1_.1), channel_id=1, source_target_pairs={{0,6},{1,7},{2,4},{3,5},{4,2},{5,3},{6,0},{7,1},{8,14},{9,15},{10,... | collective-permute-start | bytes 344072 | tf_op jit(solution)/shard_map/ppermute | solution.py:175
  6.0 8.0 %collective-permute-start = (f32[112,384]{1,0:T(8,128)S(1)}, f32[112,384]{1,0:T(8,128)S(1)}, u32[]{:S(2)}, u32[]{:S(2)}) collective-permute-start(f32[112,384]{1,0:T(8,128)S(1)} %constant_dynamic-update-slice_fusion), channel_id=1, source_target_pairs={{0,24},{1,25},{2,26},{3,27},{4,28},{5,29},{6,30},{7,31},{8,16},{9,... | collective-permute-start | bytes 516104 | tf_op jit(solution)/shard_map/ppermute | solution.py:177
  8.5 8.0 %collective-permute-start.1 = (f32[112,384]{1,0:T(8,128)S(1)}, f32[112,384]{1,0:T(8,128)S(1)}, u32[]{:S(2)}, u32[]{:S(2)}) collective-permute-start(f32[112,384]{1,0:T(8,128)S(1)} %constant_dynamic-update-slice_fusion), channel_id=1, source_target_pairs={{0,16},{1,17},{2,18},{3,19},{4,20},{5,21},{6,22},{7,23},{8,24},{9,... | collective-permute-start | bytes 516104 | tf_op jit(solution)/shard_map/ppermute | solution.py:177
  9.0 7.6 %collective-permute-start.2 = (f32[112,384]{1,0:T(8,128)S(1)}, f32[112,384]{1,0:T(8,128)S(1)}, u32[]{:S(2)}, u32[]{:S(2)}) collective-permute-start(f32[112,384]{1,0:T(8,128)S(1)} %constant_dynamic-update-slice_fusion), channel_id=1, source_target_pairs={{0,8},{1,9},{2,10},{3,11},{4,12},{5,13},{6,14},{7,15},{8,0},{9,1},... | collective-permute-start | bytes 516104 | tf_op jit(solution)/shard_map/ppermute | solution.py:177
  9.6 7.2 %collective-permute-start.4 = (f32[112,256]{1,0:T(8,128)S(1)}, f32[112,256]{1,0:T(8,128)S(1)}, u32[]{:S(2)}, u32[]{:S(2)}) collective-permute-start(f32[112,256]{1,0:T(8,128)S(1)} %copy-done), channel_id=1, source_target_pairs={{0,4},{1,5},{2,6},{3,7},{4,0},{5,1},{6,2},{7,3},{8,12},{9,13},{10,... | collective-permute-start | bytes 344072 | tf_op jit(solution)/shard_map/ppermute | solution.py:175
  10.2 0.8 %copy-start.1 = (f32[256]{0:T(256)S(1)}, f32[256]{0:T(256)}, u32[]{:S(2)}) copy-start(f32[256]{0:T(256)} %param.7) | copy-start | bytes 3076
  10.3 6.5 %collective-permute-start.6 = (f32[112,256]{1,0:T(8,128)S(1)}, f32[112,256]{1,0:T(8,128)S(1)}, u32[]{:S(2)}, u32[]{:S(2)}) collective-permute-start(f32[112,256]{1,0:T(8,128)S(1)} %copy-done), channel_id=1, source_target_pairs={{0,2},{1,3},{2,0},{3,1},{4,6},{5,7},{6,4},{7,5},{8,10},{9,11},{10,... | collective-permute-start | bytes 344072 | tf_op jit(solution)/shard_map/ppermute | solution.py:179
  16.7 2.2 %collective-permute-start.3 = (f32[448,384]{1,0:T(8,128)S(1)}, f32[448,384]{1,0:T(8,128)S(1)}, u32[]{:S(2)}, u32[]{:S(2)}) collective-permute-start(f32[448,384]{1,0:T(8,128)S(1)} %pad_maximum_fusion.cols_ref), channel_id=1, source_target_pairs={{0,1},{1,0},{2,3},{3,2},{4,5},{5,4},{6,7},{7,6},{8,9},{9,8},{10,11... | collective-permute-start | bytes 2064392 | tf_op jit(solution)/shard_map/ppermute | solution.py:181
  20.1 6.7 %collective-permute-start.7 = (f32[112,128]{1,0:T(8,128)S(1)}, f32[112,128]{1,0:T(8,128)S(1)}, u32[]{:S(2)}, u32[]{:S(2)}) collective-permute-start(f32[112,128]{1,0:T(8,128)S(1)} %get-tuple-element.14), channel_id=1, source_target_pairs={{6,0},{7,1},{4,2},{5,3},{2,4},{3,5},{0,6},{1,7},{14,8},{15,9},{12,... | collective-permute-start | bytes 172040 | tf_op jit(solution)/shard_map/ppermute | solution.py:191
  21.8 6.4 %collective-permute-start.8 = (f32[112,128]{1,0:T(8,128)S(1)}, f32[112,128]{1,0:T(8,128)S(1)}, u32[]{:S(2)}, u32[]{:S(2)}) collective-permute-start(f32[112,128]{1,0:T(8,128)S(1)} %get-tuple-element.15), channel_id=1, source_target_pairs={{4,0},{5,1},{6,2},{7,3},{0,4},{1,5},{2,6},{3,7},{12,8},{13,9},{14,... | collective-permute-start | bytes 172040 | tf_op jit(solution)/shard_map/ppermute | solution.py:191
  23.0 5.5 %collective-permute-start.9 = (f32[112,128]{1,0:T(8,128)S(1)}, f32[112,128]{1,0:T(8,128)S(1)}, u32[]{:S(2)}, u32[]{:S(2)}) collective-permute-start(f32[112,128]{1,0:T(8,128)S(1)} %get-tuple-element.16), channel_id=1, source_target_pairs={{2,0},{3,1},{0,2},{1,3},{6,4},{7,5},{4,6},{5,7},{10,8},{11,9},{8,1... | collective-permute-start | bytes 172040 | tf_op jit(solution)/shard_map/ppermute | solution.py:191

commit v4 on v3

--- a/solution.py
+++ b/solution.py
@@ -17,6 +17,7 @@
 LIMIT = 24 * 1024 * 1024
 LANES = 128
 LN2 = math.log(2.0)
+GROUP = 4
 
 
 def partner(index, step, size):
@@ -96,37 +97,29 @@
     )(*given)
 
 
-def times_tile(x_ref, first, count, y_ref, v_ref):
+def times_tile(x, y_ref, v_ref):
     columns = v_ref.shape[1] // 2
-    n = y_ref.shape[0]
-    x = x_ref[first : first + count, :]
-    total = None
-    for at in range(0, n, 256):
-        cols = slice(at, min(at + 256, n))
-        b2 = lax.dot_general(x, y_ref[cols, :], (((1,), (1,)), ((), ())), preferred_element_type=F32)
-        b2 = jnp.maximum(b2, 1e-30)
-        b = b2 * lax.rsqrt(b2)
-        tile = (b2 * (LN2 / 3.0) + b + (1.0 / LN2)) * jnp.exp2(-b)
-        high, low = split(tile)
-        part = jnp.dot(high, v_ref[cols, :], preferred_element_type=F32)
-        part = part[:, :columns] + part[:, columns:]
-        part = part + jnp.dot(low, v_ref[cols, :columns], preferred_element_type=F32)
-        total = part if total is None else total + part
-    return total
+    b2 = lax.dot_general(x, y_ref[...], (((1,), (1,)), ((), ())), preferred_element_type=F32)
+    b2 = jnp.maximum(b2, 1e-30)
+    b = b2 * lax.rsqrt(b2)
+    high, low = split((b2 * (LN2 / 3.0) + b + (1.0 / LN2)) * jnp.exp2(-b))
+    total = jnp.dot(high, v_ref[...], preferred_element_type=F32)
+    return total[:, :columns] + total[:, columns:] + jnp.dot(low, v_ref[:, :columns], preferred_element_type=F32)
 
 
 def tile_kernel(first, here, sizes, has_start, scale_ref, amp_ref, cols_ref, x_ref, *refs):
     n_in = 1 if has_start else 0
     given, outs, (y_ref, v_ref) = refs[:n_in], refs[n_in:-2], refs[-2:]
     fill_cols(y_ref, v_ref, cols_ref[...], kernel_scale(scale_ref), amp_ref[0])
-    count = sum(sizes) * here
-    total = times_tile(x_ref, first * here, count, y_ref, v_ref)
-    if has_start:
-        total = total + given[0][first * here : first * here + count, :]
-    at = 0
-    for size, out in zip(sizes, outs):
-        out[...] = total[at * here : (at + size) * here, :]
-        at += size
+    blocks = [(out, i) for out, size in zip(outs, sizes) for i in range(size)]
+    for at in range(0, len(blocks), GROUP):
+        group = blocks[at : at + GROUP]
+        rows = slice((first + at) * here, (first + at + len(group)) * here)
+        total = times_tile(x_ref[rows, :], y_ref, v_ref)
+        if has_start:
+            total = total + given[0][rows, :]
+        for j, (out, i) in enumerate(group):
+            out[i * here : (i + 1) * here, :] = total[j * here : (j + 1) * here, :]
 
 
 def times_columns(scale, amplitude, cols, x, first, sizes, start, here, us):

time: 29.3 us -> 28.6 us (0.976)
  Pallas kernels: 4.72 us -> 3.41 us
  waiting for transfers between devices: 7.44 us -> 8.08 us
    pallas_call x3, Pallas kernels: 4.44 us -> 3.12 us  [times_columns(): pl.pallas_call(functools.partial(tile_kernel, first, here, sizes, start i...]
    ppermute x1, waiting for transfers between devices: 0.01 us -> 0.61 us  [per_device(): cols_theirs = lax.ppermute(cols_mine, AXES, other_core)]
  transfers between devices with their start and end apart: 10 -> 10, of which waited for: 6 -> 7; matrix products, arithmetic and copies ran while one was open for 3% -> 3% of each run, Pallas kernels for 12% -> 9%
where the time goes in v4:
time: 28.6 us; the launch traced here: 28.5 us
  starting transfers between devices  13.9 us (49%)
  waiting for transfers between devices  8.08 us (28%)
  Pallas kernels  3.41 us (12%)
  between operations  1.4 us (5%)
  local copies, waits for them, and re-layouts  0.96 us (3%)
  other arithmetic  0.69 us (2%)
    ppermute x3, waiting for transfers between devices, per_device(): lax.ppermute(both, AXES, along_outer(k))  5.46 us
    ppermute x2, starting transfers between devices, per_device(): far = [lax.ppermute(points, AXES, along_line(k)) for k in far_lines]  5.05 us
    ppermute x3, starting transfers between devices, per_device(): total = total + lax.ppermute(sent, AXES, [(b, a) for a, b in along_line(k)])  4.52 us
    ppermute x3, starting transfers between devices, per_device(): lax.ppermute(both, AXES, along_outer(k))  3.55 us
    pallas_call x3, Pallas kernels, times_columns(): pl.pallas_call(functools.partial(tile_kernel, first, here, sizes, start i...  3.12 us
    ppermute x3, waiting for transfers between devices, per_device(): total = total + lax.ppermute(sent, AXES, [(b, a) for a, b in along_line(k)])  2 us
    unnamed x7, local copies, waits for them, and re-layouts  0.95 us
    ppermute x1, starting transfers between devices, per_device(): near = lax.ppermute(late[0], AXES, along_line(near_line))  0.74 us
  transfers between devices with their start and end apart: 10, of which 7 were waited for; matrix products, arithmetic and copies ran while one was open for 3% of the time, Pallas kernels for 9%

profile of v4, /device:TPU:0, one launch (start us, length us, event | category | flops | bytes accessed | tf_op | source)
XLA Modules:
  0.0 28.5 jit_solution(4046637206525673031)
XLA Ops:
  0.0 0.0 copy-start
  0.0 0.0 copy-start.2
  0.0 5.0 %collective-permute-start.5 = (f32[112,256]{1,0:T(8,128)}, f32[112,256]{1,0:T(8,128)S(1)}, u32[]{:S(2)}, u32[]{:S(2)}) collective-permute-start(f32[112,256]{1,0:T(8,128)} %refs_1_.1), channel_id=1, source_target_pairs={{0,6},{1,7},{2,4},{3,5},{4,2},{5,3},{6,0},{7,1},{8,14},{9,15},{10,... | collective-permute-start | bytes 344072 | tf_op jit(solution)/shard_map/ppermute | solution.py:168
  5.1 0.9 %constant_dynamic-update-slice_fusion.1 = f32[112,384]{1,0:T(8,128)S(1)} fusion(f32[112,256]{1,0:T(8,128)} %refs_1_.1), kind=kLoop, calls=%fused_computation.3 | loop fusion | bytes 229376
  6.0 0.0 copy-done.2
  6.0 2.5 %collective-permute-start = (f32[112,384]{1,0:T(8,128)S(1)}, f32[112,384]{1,0:T(8,128)S(1)}, u32[]{:S(2)}, u32[]{:S(2)}) collective-permute-start(f32[112,384]{1,0:T(8,128)S(1)} %constant_dynamic-update-slice_fusion), channel_id=1, source_target_pairs={{0,24},{1,25},{2,26},{3,27},{4,28},{5,29},{6,30},{7,31},{8,16},{9,... | collective-permute-start | bytes 516104 | tf_op jit(solution)/shard_map/ppermute | solution.py:170
  8.5 0.5 %collective-permute-start.1 = (f32[112,384]{1,0:T(8,128)S(1)}, f32[112,384]{1,0:T(8,128)S(1)}, u32[]{:S(2)}, u32[]{:S(2)}) collective-permute-start(f32[112,384]{1,0:T(8,128)S(1)} %constant_dynamic-update-slice_fusion), channel_id=1, source_target_pairs={{0,16},{1,17},{2,18},{3,19},{4,20},{5,21},{6,22},{7,23},{8,24},{9,... | collective-permute-start | bytes 516104 | tf_op jit(solution)/shard_map/ppermute | solution.py:170
  9.0 0.5 %collective-permute-start.2 = (f32[112,384]{1,0:T(8,128)S(1)}, f32[112,384]{1,0:T(8,128)S(1)}, u32[]{:S(2)}, u32[]{:S(2)}) collective-permute-start(f32[112,384]{1,0:T(8,128)S(1)} %constant_dynamic-update-slice_fusion), channel_id=1, source_target_pairs={{0,8},{1,9},{2,10},{3,11},{4,12},{5,13},{6,14},{7,15},{8,0},{9,1},... | collective-permute-start | bytes 516104 | tf_op jit(solution)/shard_map/ppermute | solution.py:170
  9.6 0.0 copy-done
  9.6 0.0 collective-permute-start.4
  10.2 0.0 copy-start.1
  10.2 0.0 collective-permute-done.5.refs_0_
  10.3 0.7 %collective-permute-start.6 = (f32[112,256]{1,0:T(8,128)S(1)}, f32[112,256]{1,0:T(8,128)S(1)}, u32[]{:S(2)}, u32[]{:S(2)}) collective-permute-start(f32[112,256]{1,0:T(8,128)S(1)} %copy-done), channel_id=1, source_target_pairs={{0,2},{1,3},{2,0},{3,1},{4,6},{5,7},{6,4},{7,5},{8,10},{9,11},{10,... | collective-permute-start | bytes 344072 | tf_op jit(solution)/shard_map/ppermute | solution.py:172
  11.0 0.0 copy-done.1
  11.0 0.1 rows.2.refs_2_
  11.1 2.9 %collective-permute-done = f32[112,384]{1,0:T(8,128)S(1)} collective-permute-done((f32[112,384]{1,0:T(8,128)S(1)}, f32[112,384]{1,0:T(8,128)S(1)}, u32[]{:S(2)}, u32[]{:S(2)}) %collective-permute-start) | collective-permute-done | bytes 172064 | tf_op jit(solution)/shard_map/ppermute | solution.py:170
  14.0 2.5 %collective-permute-done.1 = f32[112,384]{1,0:T(8,128)S(1)} collective-permute-done((f32[112,384]{1,0:T(8,128)S(1)}, f32[112,384]{1,0:T(8,128)S(1)}, u32[]{:S(2)}, u32[]{:S(2)}) %collective-permute-start.1) | collective-permute-done | bytes 172064 | tf_op jit(solution)/shard_map/ppermute | solution.py:170
  16.5 0.1 collective-permute-done.2
  16.7 0.1 collective-permute-start.3
  16.7 0.0 collective-permute-done.4.refs_0_
  16.7 0.0 collective-permute-done.6.refs_1_
  16.8 0.1 rows.3.x_ref
  16.9 1.3 %tile.3.refs_0_ = f32[448,128]{1,0:T(8,128)S(1)} custom-call(f32[1,256]{1,0:T(1,128)S(1)} %bitcast.5, f32[1]{0:T(128)S(6)} %copy.9.amp_ref, f32[448,384]{1,0:T(8,128)S(1)} %pad_maximum_fusion.cols_ref, bf16[448,1152]{1,0:T(8,128)(2,1)S(1)} %rows.3.x_ref), custom_call_target="tpu_custom_call" | custom-call | flops 20000000000 | bytes 1024 | tf_op jit(solution)/shard_map/tile/pallas_call | solution.py:130
  18.3 0.6 %collective-permute-done.3.cols_ref = f32[448,384]{1,0:T(8,128)S(1)} collective-permute-done((f32[448,384]{1,0:T(8,128)S(1)}, f32[448,384]{1,0:T(8,128)S(1)}, u32[]{:S(2)}, u32[]{:S(2)}) %collective-permute-start.3) | collective-permute-done | bytes 688160 | tf_op jit(solution)/shard_map/ppermute | solution.py:174
  18.9 0.9 %tile.5 = (f32[112,128]{1,0:T(8,128)S(1)}, f32[112,128]{1,0:T(8,128)S(1)}) custom-call(f32[1,256]{1,0:T(1,128)S(1)} %bitcast.6, f32[1]{0:T(128)S(6)} %copy.9.amp_ref, f32[448,384]{1,0:T(8,128)S(1)} %collective-permute-done.3.cols_ref, bf16[448,1152]{1,0:T(8,128)(2,1)S(1)} %rows.3.x_ref, f32[448,128]{1,0:T(8,128)S(1)} %tile.3.refs_0_), custom_call_target="tpu_custom_call" | custom-call | flops 10000000000 | bytes 1024 | tf_op jit(solution)/shard_map/tile/pallas_call | solution.py:130
  19.8 1.1 %collective-permute-start.7 = (f32[112,128]{1,0:T(8,128)S(1)}, f32[112,128]{1,0:T(8,128)S(1)}, u32[]{:S(2)}, u32[]{:S(2)}) collective-permute-start(f32[112,128]{1,0:T(8,128)S(1)} %get-tuple-element.14), channel_id=1, source_target_pairs={{6,0},{7,1},{4,2},{5,3},{2,4},{3,5},{0,6},{1,7},{14,8},{15,9},{12,... | collective-permute-start | bytes 172040 | tf_op jit(solution)/shard_map/ppermute | solution.py:184
  20.8 0.0 collective-permute-start.8
  20.8 0.9 %tile.4 = (f32[112,128]{1,0:T(8,128)S(1)}, f32[112,128]{1,0:T(8,128)S(1)}) custom-call(f32[1,256]{1,0:T(1,128)S(1)} %bitcast.7, f32[1]{0:T(128)S(6)} %copy.9.amp_ref, f32[448,384]{1,0:T(8,128)S(1)} %collective-permute-done.3.cols_ref, bf16[448,1152]{1,0:T(8,128)(2,1)S(1)} %rows.3.x_ref, f32[448,128]{1,0:T(8,128)S(1)} %tile.3.refs_0_), custom_call_target="tpu_custom_call" | custom-call | flops 10000000000 | bytes 1024 | tf_op jit(solution)/shard_map/tile/pallas_call | solution.py:130
  21.7 3.4 %collective-permute-start.9 = (f32[112,128]{1,0:T(8,128)S(1)}, f32[112,128]{1,0:T(8,128)S(1)}, u32[]{:S(2)}, u32[]{:S(2)}) collective-permute-start(f32[112,128]{1,0:T(8,128)S(1)} %get-tuple-element.16), channel_id=1, source_target_pairs={{2,0},{3,1},{0,2},{1,3},{6,4},{7,5},{4,6},{5,7},{10,8},{11,9},{8,1... | collective-permute-start | bytes 172040 | tf_op jit(solution)/shard_map/ppermute | solution.py:184
  25.8 0.6 %collective-permute-done.7 = f32[112,128]{1,0:T(8,128)S(1)} collective-permute-done((f32[112,128]{1,0:T(8,128)S(1)}, f32[112,128]{1,0:T(8,128)S(1)}, u32[]{:S(2)}, u32[]{:S(2)}) %collective-permute-start.7) | collective-permute-done | bytes 57376 | tf_op jit(solution)/shard_map/ppermute | solution.py:184
  26.4 0.8 %collective-permute-done.8 = f32[112,128]{1,0:T(8,128)S(1)} collective-permute-done((f32[112,128]{1,0:T(8,128)S(1)}, f32[112,128]{1,0:T(8,128)S(1)}, u32[]{:S(2)}, u32[]{:S(2)}) %collective-permute-start.8) | collective-permute-done | bytes 57376 | tf_op jit(solution)/shard_map/ppermute | solution.py:184
  27.2 0.6 %collective-permute-done.9 = f32[112,128]{1,0:T(8,128)S(1)} collective-permute-done((f32[112,128]{1,0:T(8,128)S(1)}, f32[112,128]{1,0:T(8,128)S(1)}, u32[]{:S(2)}, u32[]{:S(2)}) %collective-permute-start.9) | collective-permute-done | bytes 57376 | tf_op jit(solution)/shard_map/ppermute | solution.py:184
  27.8 0.6 %add_add_fusion = f32[112,128]{1,0:T(8,128)} fusion(f32[112,128]{1,0:T(8,128)S(1)} %collective-permute-done.9, f32[112,128]{1,0:T(8,128)S(1)} %collective-permute-done.8, f32[112,128]{1,0:T(8,128)S(1)} %collective-permute-done.7, f32[112,128]{1,0:T(8,128)S(1)} %get-tuple-element.13, f32[112,128]{1,0:T(8,128)S(1)} %copy-done.2, f32[]{:T(128)} %bitcast.2), kind=kLoop, calls=%fused_computation.1 | loop fusion | flops 71680 | bytes 344068 | tf_op jit(solution)/shard_map/add | solution.py:184
  (2 shorter events, 0.1 us)
Async XLA Ops:
  0.0 9.6 %copy-start = (f32[112,256]{1,0:T(8,128)S(1)}, f32[112,256]{1,0:T(8,128)}, u32[]{:S(2)}) copy-start(f32[112,256]{1,0:T(8,128)} %refs_1_.1) | copy-start | bytes 344068
  0.0 6.0 %copy-start.2 = (f32[112,128]{1,0:T(8,128)S(1)}, f32[112,128]{1,0:T(8,128)}, u32[]{:S(2)}) copy-start(f32[112,128]{1,0:T(8,128)} %param.6) | copy-start | bytes 172036
  0.0 10.2 %collective-permute-start.5 = (f32[112,256]{1,0:T(8,128)}, f32[112,256]{1,0:T(8,128)S(1)}, u32[]{:S(2)}, u32[]{:S(2)}) collective-permute-start(f32[112,256]{1,0:T(8,128)} %refs_1_.1), channel_id=1, source_target_pairs={{0,6},{1,7},{2,4},{3,5},{4,2},{5,3},{6,0},{7,1},{8,14},{9,15},{10,... | collective-permute-start | bytes 344072 | tf_op jit(solution)/shard_map/ppermute | solution.py:168
  6.0 8.0 %collective-permute-start = (f32[112,384]{1,0:T(8,128)S(1)}, f32[112,384]{1,0:T(8,128)S(1)}, u32[]{:S(2)}, u32[]{:S(2)}) collective-permute-start(f32[112,384]{1,0:T(8,128)S(1)} %constant_dynamic-update-slice_fusion), channel_id=1, source_target_pairs={{0,24},{1,25},{2,26},{3,27},{4,28},{5,29},{6,30},{7,31},{8,16},{9,... | collective-permute-start | bytes 516104 | tf_op jit(solution)/shard_map/ppermute | solution.py:170
  8.5 8.0 %collective-permute-start.1 = (f32[112,384]{1,0:T(8,128)S(1)}, f32[112,384]{1,0:T(8,128)S(1)}, u32[]{:S(2)}, u32[]{:S(2)}) collective-permute-start(f32[112,384]{1,0:T(8,128)S(1)} %constant_dynamic-update-slice_fusion), channel_id=1, source_target_pairs={{0,16},{1,17},{2,18},{3,19},{4,20},{5,21},{6,22},{7,23},{8,24},{9,... | collective-permute-start | bytes 516104 | tf_op jit(solution)/shard_map/ppermute | solution.py:170
  9.0 7.6 %collective-permute-start.2 = (f32[112,384]{1,0:T(8,128)S(1)}, f32[112,384]{1,0:T(8,128)S(1)}, u32[]{:S(2)}, u32[]{:S(2)}) collective-permute-start(f32[112,384]{1,0:T(8,128)S(1)} %constant_dynamic-update-slice_fusion), channel_id=1, source_target_pairs={{0,8},{1,9},{2,10},{3,11},{4,12},{5,13},{6,14},{7,15},{8,0},{9,1},... | collective-permute-start | bytes 516104 | tf_op jit(solution)/shard_map/ppermute | solution.py:170
  9.6 7.2 %collective-permute-start.4 = (f32[112,256]{1,0:T(8,128)S(1)}, f32[112,256]{1,0:T(8,128)S(1)}, u32[]{:S(2)}, u32[]{:S(2)}) collective-permute-start(f32[112,256]{1,0:T(8,128)S(1)} %copy-done), channel_id=1, source_target_pairs={{0,4},{1,5},{2,6},{3,7},{4,0},{5,1},{6,2},{7,3},{8,12},{9,13},{10,... | collective-permute-start | bytes 344072 | tf_op jit(solution)/shard_map/ppermute | solution.py:168
  10.2 0.8 %copy-start.1 = (f32[256]{0:T(256)S(1)}, f32[256]{0:T(256)}, u32[]{:S(2)}) copy-start(f32[256]{0:T(256)} %param.7) | copy-start | bytes 3076
  10.3 6.5 %collective-permute-start.6 = (f32[112,256]{1,0:T(8,128)S(1)}, f32[112,256]{1,0:T(8,128)S(1)}, u32[]{:S(2)}, u32[]{:S(2)}) collective-permute-start(f32[112,256]{1,0:T(8,128)S(1)} %copy-done), channel_id=1, source_target_pairs={{0,2},{1,3},{2,0},{3,1},{4,6},{5,7},{6,4},{7,5},{8,10},{9,11},{10,... | collective-permute-start | bytes 344072 | tf_op jit(solution)/shard_map/ppermute | solution.py:172
  16.7 2.2 %collective-permute-start.3 = (f32[448,384]{1,0:T(8,128)S(1)}, f32[448,384]{1,0:T(8,128)S(1)}, u32[]{:S(2)}, u32[]{:S(2)}) collective-permute-start(f32[448,384]{1,0:T(8,128)S(1)} %pad_maximum_fusion.cols_ref), channel_id=1, source_target_pairs={{0,1},{1,0},{2,3},{3,2},{4,5},{5,4},{6,7},{7,6},{8,9},{9,8},{10,11... | collective-permute-start | bytes 2064392 | tf_op jit(solution)/shard_map/ppermute | solution.py:174
  19.8 6.7 %collective-permute-start.7 = (f32[112,128]{1,0:T(8,128)S(1)}, f32[112,128]{1,0:T(8,128)S(1)}, u32[]{:S(2)}, u32[]{:S(2)}) collective-permute-start(f32[112,128]{1,0:T(8,128)S(1)} %get-tuple-element.14), channel_id=1, source_target_pairs={{6,0},{7,1},{4,2},{5,3},{2,4},{3,5},{0,6},{1,7},{14,8},{15,9},{12,... | collective-permute-start | bytes 172040 | tf_op jit(solution)/shard_map/ppermute | solution.py:184
  20.8 6.4 %collective-permute-start.8 = (f32[112,128]{1,0:T(8,128)S(1)}, f32[112,128]{1,0:T(8,128)S(1)}, u32[]{:S(2)}, u32[]{:S(2)}) collective-permute-start(f32[112,128]{1,0:T(8,128)S(1)} %get-tuple-element.15), channel_id=1, source_target_pairs={{4,0},{5,1},{6,2},{7,3},{0,4},{1,5},{2,6},{3,7},{12,8},{13,9},{14,... | collective-permute-start | bytes 172040 | tf_op jit(solution)/shard_map/ppermute | solution.py:184
  21.7 6.1 %collective-permute-start.9 = (f32[112,128]{1,0:T(8,128)S(1)}, f32[112,128]{1,0:T(8,128)S(1)}, u32[]{:S(2)}, u32[]{:S(2)}) collective-permute-start(f32[112,128]{1,0:T(8,128)S(1)} %get-tuple-element.16), channel_id=1, source_target_pairs={{2,0},{3,1},{0,2},{1,3},{6,4},{7,5},{4,6},{5,7},{10,8},{11,9},{8,1... | collective-permute-start | bytes 172040 | tf_op jit(solution)/shard_map/ppermute | solution.py:184

commit v5 on v4

v5 whole, which is shorter than its diff:
```python
import functools
import math

import jax
import jax.numpy as jnp
from jax import lax
from jax.experimental import pallas as pl
from jax.experimental.pallas import tpu as pltpu
from jax.sharding import PartitionSpec as P

AXES = ("outer", "inner")
CORES = 2
VMEM = pl.BlockSpec(memory_space=pltpu.VMEM)
SMEM = pl.BlockSpec(memory_space=pltpu.SMEM)
BF16 = jnp.bfloat16
F32 = jnp.float32
LIMIT = 24 * 1024 * 1024
LANES = 128
LN2 = math.log(2.0)
GROUP = 4


def partner(index, step, size):
    return index ^ step if size & (size - 1) == 0 else (index + step) % size


def split(x):
    high = x.astype(BF16)
    return high, (x - high.astype(F32)).astype(BF16)


def cost(us):
    return pl.CostEstimate(flops=int(us * 1e9), bytes_accessed=1024, transcendentals=0)


def params():
    return pltpu.CompilerParams(vmem_limit_bytes=LIMIT)


def kernel_scale(scale_ref):
    return (math.sqrt(5.0) / LN2) / scale_ref[...]


def norm_lanes(norm, first):
    high, mid = split(norm)
    low = (norm - high.astype(F32) - mid.astype(F32)).astype(BF16)
    lane = lax.broadcasted_iota(jnp.int32, (norm.shape[0], LANES), 1)
    out = jnp.where((lane >= 3 - first) & (lane < 6 - first), 1.0, 0.0)
    for i, part in enumerate((high, mid, low)):
        out = jnp.where(lane == first + i, part.astype(F32), out)
    return out.astype(BF16)


def put(ref, at, parts):
    start = 0
    for part in parts:
        ref[at, start : start + part.shape[1]] = part
        start += part.shape[1]


def fill_rows(x_ref, at, block, scale):
    x = block * scale
    norm = jnp.sum(x * x, axis=1, keepdims=True)
    high, low = split(-2.0 * x)
    put(x_ref, at, (high, low, high, low, norm_lanes(norm, 0)))


def fill_cols(y_ref, v_ref, at, block, scale, amplitude):
    features = scale.shape[1]
    y = block[:, :features] * scale
    norm = jnp.sum(y * y, axis=1, keepdims=True)
    high, low = split(y)
    put(y_ref, at, (high, high, low, low, norm_lanes(norm, 3)))
    put(v_ref, at, split(block[:, features:] * (amplitude * LN2)))


def blank_kernel(out_ref):
    out_ref[...] = jnp.zeros_like(out_ref)


def blank(shape, us):
    return pl.pallas_call(
        blank_kernel,
        out_shape=jax.ShapeDtypeStruct(shape, F32),
        out_specs=VMEM,
        compiler_params=params(),
        cost_estimate=cost(us),
        name="blank",
    )()


def join_kernel(a_ref, b_ref, _, out_ref):
    put(out_ref, slice(None), (a_ref[...], b_ref[...]))


def join(a, b, out):
    return pl.pallas_call(
        join_kernel,
        out_shape=jax.ShapeDtypeStruct(out.shape, out.dtype),
        in_specs=[VMEM] * 3,
        out_specs=VMEM,
        input_output_aliases={2: 0},
        compiler_params=params(),
        cost_estimate=cost(1),
        name="join",
    )(a, b, out)


def rows_kernel(scale_ref, *refs):
    n = len(refs) // 2
    scale = kernel_scale(scale_ref)
    for block, x_ref in zip(refs[:n], refs[n:]):
        fill_rows(x_ref, slice(None), block[...], scale)


def prepare_rows(scale, blocks, us):
    here, features = blocks[0].shape
    return pl.pallas_call(
        rows_kernel,
        out_shape=[jax.ShapeDtypeStruct((here, 4 * features + LANES), BF16)] * len(blocks),
        in_specs=[VMEM] * (1 + len(blocks)),
        out_specs=[VMEM] * len(blocks),
        compiler_params=params(),
        cost_estimate=cost(us),
        name="rows",
    )(scale, *blocks)


def times_tile(x, y_ref, v_ref):
    columns = v_ref.shape[1] // 2
    b2 = lax.dot_general(x, y_ref[...], (((1,), (1,)), ((), ())), preferred_element_type=F32)
    b2 = jnp.maximum(b2, 1e-30)
    b = b2 * lax.rsqrt(b2)
    high, low = split((b2 * (LN2 / 3.0) + b + (1.0 / LN2)) * jnp.exp2(-b))
    total = jnp.dot(high, v_ref[...], preferred_element_type=F32)
    return total[:, :columns] + total[:, columns:] + jnp.dot(low, v_ref[:, :columns], preferred_element_type=F32)


def fill_all(cols, y_ref, v_ref, scale, amplitude):
    at = 0
    for block in cols:
        fill_cols(y_ref, v_ref, slice(at, at + block.shape[0]), block[...], scale, amplitude)
        at += block.shape[0]


def groups(n):
    return [range(first, min(first + GROUP, n)) for first in range(0, n, GROUP)]


def tile_kernel(n_cols, n_rows, scale_ref, amp_ref, noise_ref, *refs):
    cols, rows, rest = refs[:n_cols], refs[n_cols : n_cols + n_rows], refs[n_cols + n_rows :]
    starts, outs, (y_ref, v_ref) = rest[: -n_rows - 2], rest[-n_rows - 2 : -2], rest[-2:]
    here = rows[0].shape[0]
    fill_all(cols, y_ref, v_ref, kernel_scale(scale_ref), amp_ref[0])
    for group in groups(n_rows):
        total = times_tile(jnp.concatenate([rows[i][...] for i in group], axis=0), y_ref, v_ref)
        for j, i in enumerate(group):
            out = total[j * here : (j + 1) * here, :]
            if starts:
                out = out + starts[i][...]
            elif i == 0:
                out = out + noise_ref[0] * cols[0][:here, -out.shape[1] :]
            outs[i][...] = out


def prepared_shapes(cols, features):
    n, width = sum(block.shape[0] for block in cols), cols[0].shape[1]
    return [
        jax.ShapeDtypeStruct((n, 4 * features + LANES), BF16),
        jax.ShapeDtypeStruct((n, 2 * (width - features)), BF16),
    ]


def times_columns(scale, amplitude, noise, cols, rows, starts, us):
    here = rows[0].shape[0]
    features = scale.shape[1]
    given = [scale, amplitude, noise, *cols, *rows, *starts]
    *outs, y, v = pl.pallas_call(
        functools.partial(tile_kernel, len(cols), len(rows)),
        out_shape=[jax.ShapeDtypeStruct((here, cols[0].shape[1] - features), F32)] * len(rows)
        + prepared_shapes(cols, features),
        in_specs=[VMEM, SMEM, SMEM] + [VMEM] * (len(given) - 3),
        out_specs=[VMEM] * (len(rows) + 2),
        compiler_params=params(),
        cost_estimate=cost(us),
        name="tile",
    )(*given)
    return outs, (y, v)


def last_kernel(n_blocks, scale_ref, *refs):
    blocks, prepared, outs, xs = refs[:n_blocks], refs[n_blocks : -2 * n_blocks], refs[-2 * n_blocks : -n_blocks], refs[-n_blocks:]
    scale = kernel_scale(scale_ref)
    here = blocks[0].shape[0]
    for block, x_ref in zip(blocks, xs):
        fill_rows(x_ref, slice(None), block[...], scale)
    for group in groups(n_blocks):
        x = jnp.concatenate([xs[i][...] for i in group], axis=0)
        total = times_tile(x, *prepared)
        for j, i in enumerate(group):
            outs[i][...] = total[j * here : (j + 1) * here, :]


def times_prepared(scale, blocks, prepared, us):
    n = len(blocks)
    here, features = blocks[0].shape
    columns = prepared[0][1].shape[1] // 2
    given = [scale, *blocks, *prepared[0]]
    out = pl.pallas_call(
        functools.partial(last_kernel, n),
        out_shape=[jax.ShapeDtypeStruct((here, columns), F32)] * n
        + [jax.ShapeDtypeStruct((here, 4 * features + LANES), BF16)] * n,
        in_specs=[VMEM] * len(given),
        out_specs=[VMEM] * (2 * n),
        compiler_params=params(),
        cost_estimate=cost(us),
        name="last",
    )(*given)
    return out[:n], out[n:]


def near_kernel(y_ref, v_ref, *refs):
    n = len(refs) // 3
    rows, starts, outs = refs[:n], refs[n : 2 * n], refs[2 * n :]
    here = rows[0].shape[0]
    total = times_tile(jnp.concatenate([row[...] for row in rows], axis=0), y_ref, v_ref)
    for i in range(n):
        outs[i][...] = starts[i][...] + total[i * here : (i + 1) * here, :]


def times_near(prepared, rows, starts, us):
    return pl.pallas_call(
        near_kernel,
        out_shape=[jax.ShapeDtypeStruct(start.shape, F32) for start in starts],
        in_specs=[VMEM] * (2 + 2 * len(rows)),
        out_specs=[VMEM] * len(rows),
        compiler_params=params(),
        cost_estimate=cost(us),
        name="near",
    )(*prepared, *rows, *starts)


def add_kernel(*refs):
    out = refs[0][...]
    for ref in refs[1:-1]:
        out = out + ref[...]
    refs[-1][...] = out


def add_most(parts, us):
    return pl.pallas_call(
        add_kernel,
        out_shape=jax.ShapeDtypeStruct(parts[0].shape, F32),
        in_specs=[VMEM] * len(parts),
        out_specs=VMEM,
        compiler_params=params(),
        cost_estimate=cost(us),
        name="add",
    )(*parts)


def solution(mesh):
    n_outer, n_inner = mesh.shape["outer"], mesh.shape["inner"]
    n_line = n_inner // CORES

    def linear(outer, line, core):
        return outer * n_inner + line * CORES + core

    places = [(o, z, c) for o in range(n_outer) for z in range(n_line) for c in range(CORES)]

    def along_line(step):
        return [(linear(o, z, c), linear(o, partner(z, step, n_line), c)) for o, z, c in places]

    def along_outer(step):
        return [(linear(o, z, c), linear(partner(o, step, n_outer), z, c)) for o, z, c in places]

    other_core = [(linear(o, z, c), linear(o, z, c ^ 1)) for o, z, c in places]

    def per_device(points, vectors, lengthscales, outputscale, noise):
        scale = lengthscales[None, :]
        half = n_line // 2
        direct = list(range(1, half + 1))
        forwarded = list(range(half + 1, n_line))
        points_of = {half: lax.ppermute(points, AXES, along_line(half))}
        here, features = points.shape
        both = blank((here, features + vectors.shape[1]), 20)
        both = join(points, vectors, both)
        got = [lax.ppermute(both, AXES, along_outer(k)) for k in range(n_outer - 1, 0, -1)]
        for k in direct[:-1]:
            points_of[k] = lax.ppermute(points, AXES, along_line(k))
        for k in forwarded:
            points_of[k] = lax.ppermute(points_of[half], AXES, along_line(k - half))
        cols_mine = jnp.concatenate([both, *got], axis=0)
        cols_theirs = lax.ppermute(cols_mine, AXES, other_core)

        x = dict(zip([half, 0], prepare_rows(scale, [points_of[half], points], 40)))
        x |= dict(zip(direct[:-1], prepare_rows(scale, [points_of[k] for k in direct[:-1]], 1)))
        ks = [0, *direct]
        part, mine = times_columns(scale, outputscale, noise, [cols_mine], [x[k] for k in ks], [], 20)
        total = dict(zip(ks, part))
        last = lax.optimization_barrier((*[points_of[k] for k in forwarded], *part))[: len(forwarded)]
        part, x_last = times_prepared(scale, last, [mine], 10)
        total |= dict(zip(forwarded, part))
        x |= dict(zip(forwarded, x_last))
        ks = [*forwarded, *direct[1:]]
        part, theirs = times_columns(scale, outputscale, noise, [cols_theirs], [x[k] for k in ks], [total[k] for k in ks], 10)
        total |= dict(zip(ks, part))
        total |= dict(zip([0, 1], times_near(theirs, [x[0], x[1]], [total[0], total[1]], 10)))
        got = [
            lax.ppermute(total[k], AXES, [(b, a) for a, b in along_line(k)]) for k in [*direct[1:], *forwarded, 1]
        ]
        return add_most([total[0], *got[:-1]], 10) + got[-1]

    placed = (P(AXES, None), P(AXES, None), P(), P(), P())
    return jax.shard_map(per_device, mesh=mesh, in_specs=placed, out_specs=P(AXES, None), check_vma=False)
```

time: 28.6 us -> 27.7 us (0.969)
  local copies, waits for them, and re-layouts: 0.96 us -> 0.16 us
  waiting for transfers between devices: 8.08 us -> 7.66 us
  Pallas kernels: 3.41 us -> 3.77 us
    ppermute x3, waiting for transfers between devices: 5.46 us -> 1.4 us  [per_device(): lax.ppermute(both, AXES, along_outer(k))]
    ppermute x6, waiting for transfers between devices: 2.01 us -> 5.95 us  [the longest x3 4.15 us: per_device(): lax.ppermute(total[k], AXES, [(b, a) for a, b in along_line(k)])]
    unnamed x7 -> x6, local copies, waits for them, and re-layouts: 0.95 us -> 0.16 us
    pallas_call x5 -> x9, Pallas kernels: 3.41 us -> 3.77 us  [the longest x2 2.02 us: times_columns(): pl.pallas_call(functools.partial(tile_kernel, len(cols), len(rows)), out_...]
    ppermute x1, waiting for transfers between devices: 0.61 us -> 0.3 us  [per_device(): cols_theirs = lax.ppermute(cols_mine, AXES, other_core)]
  transfers between devices with their start and end apart: 10 -> 10, of which waited for: 7 -> 6; matrix products, arithmetic and copies ran while one was open for 3% -> 0% of each run, Pallas kernels for 9% -> 10%
where the time goes in v5:
time: 27.7 us; the launch traced here: 27.5 us
  starting transfers between devices  13.8 us (50%)
  waiting for transfers between devices  7.66 us (28%)
  Pallas kernels  3.77 us (14%)
  between operations  1.42 us (5%)
  other arithmetic  0.68 us (2%)
    ppermute x3, waiting for transfers between devices, per_device(): lax.ppermute(total[k], AXES, [(b, a) for a, b in along_line(k)])  4.15 us
    ppermute x3, starting transfers between devices, per_device(): lax.ppermute(total[k], AXES, [(b, a) for a, b in along_line(k)])  4.07 us
    ppermute x1, starting transfers between devices, per_device(): points_of = {half: lax.ppermute(points, AXES, along_line(half))}  4.04 us
    ppermute x3, starting transfers between devices, per_device(): lax.ppermute(both, AXES, along_outer(k))  3.55 us
    pallas_call x2, Pallas kernels, times_columns(): pl.pallas_call(functools.partial(tile_kernel, len(cols), len(rows)), out_...  2.02 us
    ppermute x1, waiting for transfers between devices, per_device(): points_of[k] = lax.ppermute(points, AXES, along_line(k))  1.8 us
    ppermute x1, starting transfers between devices, per_device(): points_of[k] = lax.ppermute(points, AXES, along_line(k))  1.58 us
    ppermute x3, waiting for transfers between devices, per_device(): lax.ppermute(both, AXES, along_outer(k))  1.4 us
  transfers between devices with their start and end apart: 10, of which 6 were waited for; matrix products, arithmetic and copies ran while one was open for 0% of the time, Pallas kernels for 10%

profile of v5, /device:TPU:0, one launch (start us, length us, event | category | flops | bytes accessed | tf_op | source)
XLA Modules:
  0.0 27.5 jit_solution(17694055898411962424)
XLA Ops:
  0.0 0.0 copy-start
  0.0 0.0 copy-start.1
  0.0 4.0 %collective-permute-start.4 = (f32[112,256]{1,0:T(8,128)}, f32[112,256]{1,0:T(8,128)S(1)}, u32[]{:S(2)}, u32[]{:S(2)}) collective-permute-start(f32[112,256]{1,0:T(8,128)} %refs_1_.1), channel_id=1, source_target_pairs={{0,4},{1,5},{2,6},{3,7},{4,0},{5,1},{6,2},{7,3},{8,12},{9,13},{10,... | collective-permute-start | bytes 344072 | tf_op jit(solution)/shard_map/ppermute | solution.py:284
  4.1 0.0 copy-done
  4.1 0.0 copy-done.1
  4.1 2.5 %collective-permute-start = (f32[112,384]{1,0:T(8,128)S(1)}, f32[112,384]{1,0:T(8,128)S(1)}, u32[]{:S(2)}, u32[]{:S(2)}) collective-permute-start(f32[112,384]{1,0:T(8,128)S(1)} %join.1), channel_id=1, source_target_pairs={{0,24},{1,25},{2,26},{3,27},{4,28},{5,29},{6,30},{7,31},{8,16},{9,... | collective-permute-start | bytes 516104 | tf_op jit(solution)/shard_map/ppermute | solution.py:288
  6.6 0.5 %collective-permute-start.1 = (f32[112,384]{1,0:T(8,128)S(1)}, f32[112,384]{1,0:T(8,128)S(1)}, u32[]{:S(2)}, u32[]{:S(2)}) collective-permute-start(f32[112,384]{1,0:T(8,128)S(1)} %join.1), channel_id=1, source_target_pairs={{0,16},{1,17},{2,18},{3,19},{4,20},{5,21},{6,22},{7,23},{8,24},{9,... | collective-permute-start | bytes 516104 | tf_op jit(solution)/shard_map/ppermute | solution.py:288
  7.1 0.5 %collective-permute-start.2 = (f32[112,384]{1,0:T(8,128)S(1)}, f32[112,384]{1,0:T(8,128)S(1)}, u32[]{:S(2)}, u32[]{:S(2)}) collective-permute-start(f32[112,384]{1,0:T(8,128)S(1)} %join.1), channel_id=1, source_target_pairs={{0,8},{1,9},{2,10},{3,11},{4,12},{5,13},{6,14},{7,15},{8,0},{9,1},... | collective-permute-start | bytes 516104 | tf_op jit(solution)/shard_map/ppermute | solution.py:288
  7.7 1.6 %collective-permute-start.6 = (f32[112,256]{1,0:T(8,128)S(1)}, f32[112,256]{1,0:T(8,128)S(1)}, u32[]{:S(2)}, u32[]{:S(2)}) collective-permute-start(f32[112,256]{1,0:T(8,128)S(1)} %copy-done), channel_id=1, source_target_pairs={{0,2},{1,3},{2,0},{3,1},{4,6},{5,7},{6,4},{7,5},{8,10},{9,11},{10,... | collective-permute-start | bytes 344072 | tf_op jit(solution)/shard_map/ppermute | solution.py:290
  10.5 0.0 copy-start.2
  10.5 0.0 collective-permute-done.4.refs_0_
  10.6 0.5 %collective-permute-start.5 = (f32[112,256]{1,0:T(8,128)S(1)}, f32[112,256]{1,0:T(8,128)S(1)}, u32[]{:S(2)}, u32[]{:S(2)}) collective-permute-start(f32[112,256]{1,0:T(8,128)S(1)} %collective-permute-done.4.refs_0_), channel_id=1, source_target_pairs={{0,2},{1,3},{2,0},{3,1},{4,6},{5,7},{6,4},{7,5},{8,10},{9,11},{10,... | collective-permute-start | bytes 344072 | tf_op jit(solution)/shard_map/ppermute | solution.py:292
  11.1 0.1 copy-done.2
  11.2 0.1 rows.2
  11.4 1.8 %collective-permute-done.6.refs_0_ = f32[112,256]{1,0:T(8,128)S(1)} collective-permute-done((f32[112,256]{1,0:T(8,128)S(1)}, f32[112,256]{1,0:T(8,128)S(1)}, u32[]{:S(2)}, u32[]{:S(2)}) %collective-permute-start.6) | collective-permute-done | bytes 114720 | tf_op jit(solution)/shard_map/ppermute | solution.py:290
  13.2 0.1 rows.3.refs_2_.refs_1_
  13.3 0.0 collective-permute-done
  13.3 1.3 %collective-permute-done.1 = f32[112,384]{1,0:T(8,128)S(1)} collective-permute-done((f32[112,384]{1,0:T(8,128)S(1)}, f32[112,384]{1,0:T(8,128)S(1)}, u32[]{:S(2)}, u32[]{:S(2)}) %collective-permute-start.1) | collective-permute-done | bytes 172064 | tf_op jit(solution)/shard_map/ppermute | solution.py:288
  14.6 0.1 collective-permute-done.2
  14.7 0.1 collective-permute-start.3
  14.8 1.1 %tile.2 = (f32[112,128]{1,0:T(8,128)S(1)}, f32[112,128]{1,0:T(8,128)S(1)}, f32[112,128]{1,0:T(8,128)S(1)}, bf16[448,1152]{1,0:T(8,128)(2,1)S(1)}, bf16[448,256]{1,0:T(8,128)(2,1)S(1)}) custom-call(f32[1,256]{1,0:T(1,128)S(1)} %bitcast.3, f32[1]{0:T(128)S(6)} %copy.8.amp_ref, f32[1]{0:T(128)S(6)} %copy.9.noise_ref, f32[448,384]{1,0:T(8,128)S(1)} %pad_maximum_fusion.refs_0_, ...), custom_call_target="tpu_custom_call" | custom-call | flops 20000000000 | bytes 1024 | tf_op jit(solution)/shard_map/tile/pallas_call | solution.py:178
  15.9 0.0 collective-permute-done.5.refs_0_
  16.0 0.7 %last.1 = (f32[112,128]{1,0:T(8,128)S(1)}, bf16[112,1152]{1,0:T(8,128)(2,1)S(1)}) custom-call(f32[1,256]{1,0:T(1,128)S(1)} %bitcast.4, f32[112,256]{1,0:T(8,128)S(1)} %collective-permute-done.5.refs_0_, bf16[448,1152]{1,0:T(8,128)(2,1)S(1)} %get-tuple-element.27.refs_1_, bf16[448,256]{1,0:T(8,128)(2,1)S(1)} %get-tuple-element.28.refs_2_), custom_call_target="tpu_custom_call" | custom-call | flops 10000000000 | bytes 1024 | tf_op jit(solution)/shard_map/last/pallas_call | solution.py:209
  16.6 0.3 %collective-permute-done.3.refs_0_ = f32[448,384]{1,0:T(8,128)S(1)} collective-permute-done((f32[448,384]{1,0:T(8,128)S(1)}, f32[448,384]{1,0:T(8,128)S(1)}, u32[]{:S(2)}, u32[]{:S(2)}) %collective-permute-start.3) | collective-permute-done | bytes 688160 | tf_op jit(solution)/shard_map/ppermute | solution.py:294
  16.9 0.9 %tile.3 = (f32[112,128]{1,0:T(8,128)S(1)}, f32[112,128]{1,0:T(8,128)S(1)}, bf16[448,1152]{1,0:T(8,128)(2,1)S(1)}, bf16[448,256]{1,0:T(8,128)(2,1)S(1)}) custom-call(f32[1,256]{1,0:T(1,128)S(1)} %bitcast.5, f32[1]{0:T(128)S(6)} %copy.8.amp_ref, f32[1]{0:T(128)S(6)} %copy.9.noise_ref, f32[448,384]{1,0:T(8,128)S(1)} %collective-permute-done.3.refs_0_, ...), custom_call_target="tpu_custom_call" | custom-call | flops 10000000000 | bytes 1024 | tf_op jit(solution)/shard_map/tile/pallas_call | solution.py:178
  17.8 1.2 %collective-permute-start.7 = (f32[112,128]{1,0:T(8,128)S(1)}, f32[112,128]{1,0:T(8,128)S(1)}, u32[]{:S(2)}, u32[]{:S(2)}) collective-permute-start(f32[112,128]{1,0:T(8,128)S(1)} %get-tuple-element.34), channel_id=1, source_target_pairs={{4,0},{5,1},{6,2},{7,3},{0,4},{1,5},{2,6},{3,7},{12,8},{13,9},{14,... | collective-permute-start | bytes 172040 | tf_op jit(solution)/shard_map/ppermute | solution.py:310
  19.0 2.8 %collective-permute-start.8 = (f32[112,128]{1,0:T(8,128)S(1)}, f32[112,128]{1,0:T(8,128)S(1)}, u32[]{:S(2)}, u32[]{:S(2)}) collective-permute-start(f32[112,128]{1,0:T(8,128)S(1)} %get-tuple-element.35), channel_id=1, source_target_pairs={{6,0},{7,1},{4,2},{5,3},{2,4},{3,5},{0,6},{1,7},{14,8},{15,9},{12,... | collective-permute-start | bytes 172040 | tf_op jit(solution)/shard_map/ppermute | solution.py:310
  21.8 0.8 %near.1 = (f32[112,128]{1,0:T(8,128)S(1)}, f32[112,128]{1,0:T(8,128)S(1)}) custom-call(bf16[448,1152]{1,0:T(8,128)(2,1)S(1)} %get-tuple-element.31.y_ref, bf16[448,256]{1,0:T(8,128)(2,1)S(1)} %get-tuple-element.32.v_ref, bf16[112,1152]{1,0:T(8,128)(2,1)S(1)} %get-tuple-element.21.refs_1_.refs_0_, bf16[112,1152]{1,0:T(8,128)(2,1)S(1)} %rows.3.refs_2_.refs_1_, ...), custom_call_target="tpu_custom_call" | custom-call | flops 10000000000 | bytes 1024 | tf_op jit(solution)/shard_map/near/pallas_call | solution.py:232
  22.6 0.1 collective-permute-start.9
  22.7 3.1 %collective-permute-done.7.refs_1_ = f32[112,128]{1,0:T(8,128)S(1)} collective-permute-done((f32[112,128]{1,0:T(8,128)S(1)}, f32[112,128]{1,0:T(8,128)S(1)}, u32[]{:S(2)}, u32[]{:S(2)}) %collective-permute-start.7) | collective-permute-done | bytes 57376 | tf_op jit(solution)/shard_map/ppermute | solution.py:310
  25.9 0.0 collective-permute-done.8.refs_2_
  25.9 1.0 %collective-permute-done.9 = f32[112,128]{1,0:T(8,128)S(1)} collective-permute-done((f32[112,128]{1,0:T(8,128)S(1)}, f32[112,128]{1,0:T(8,128)S(1)}, u32[]{:S(2)}, u32[]{:S(2)}) %collective-permute-start.9) | collective-permute-done | bytes 57376 | tf_op jit(solution)/shard_map/ppermute | solution.py:310
  26.9 0.6 %add.4 = f32[112,128]{1,0:T(8,128)} add(f32[112,128]{1,0:T(8,128)S(1)} %add.5, f32[112,128]{1,0:T(8,128)S(1)} %collective-permute-done.9) | non-fusion elementwise | flops 14336 | bytes 172032 | tf_op jit(solution)/shard_map/add | solution.py:312
  (4 shorter events, 0.1 us)
Async XLA Ops:
  0.0 4.1 %copy-start = (f32[112,256]{1,0:T(8,128)S(1)}, f32[112,256]{1,0:T(8,128)}, u32[]{:S(2)}) copy-start(f32[112,256]{1,0:T(8,128)} %refs_1_.1) | copy-start | bytes 344068
  0.0 4.1 %copy-start.1 = (f32[112,128]{1,0:T(8,128)S(1)}, f32[112,128]{1,0:T(8,128)}, u32[]{:S(2)}) copy-start(f32[112,128]{1,0:T(8,128)} %b_ref.1) | copy-start | bytes 172036
  0.0 10.5 %collective-permute-start.4 = (f32[112,256]{1,0:T(8,128)}, f32[112,256]{1,0:T(8,128)S(1)}, u32[]{:S(2)}, u32[]{:S(2)}) collective-permute-start(f32[112,256]{1,0:T(8,128)} %refs_1_.1), channel_id=1, source_target_pairs={{0,4},{1,5},{2,6},{3,7},{4,0},{5,1},{6,2},{7,3},{8,12},{9,13},{10,... | collective-permute-start | bytes 344072 | tf_op jit(solution)/shard_map/ppermute | solution.py:284
  4.1 9.2 %collective-permute-start = (f32[112,384]{1,0:T(8,128)S(1)}, f32[112,384]{1,0:T(8,128)S(1)}, u32[]{:S(2)}, u32[]{:S(2)}) collective-permute-start(f32[112,384]{1,0:T(8,128)S(1)} %join.1), channel_id=1, source_target_pairs={{0,24},{1,25},{2,26},{3,27},{4,28},{5,29},{6,30},{7,31},{8,16},{9,... | collective-permute-start | bytes 516104 | tf_op jit(solution)/shard_map/ppermute | solution.py:288
  6.6 8.0 %collective-permute-start.1 = (f32[112,384]{1,0:T(8,128)S(1)}, f32[112,384]{1,0:T(8,128)S(1)}, u32[]{:S(2)}, u32[]{:S(2)}) collective-permute-start(f32[112,384]{1,0:T(8,128)S(1)} %join.1), channel_id=1, source_target_pairs={{0,16},{1,17},{2,18},{3,19},{4,20},{5,21},{6,22},{7,23},{8,24},{9,... | collective-permute-start | bytes 516104 | tf_op jit(solution)/shard_map/ppermute | solution.py:288
  7.1 7.6 %collective-permute-start.2 = (f32[112,384]{1,0:T(8,128)S(1)}, f32[112,384]{1,0:T(8,128)S(1)}, u32[]{:S(2)}, u32[]{:S(2)}) collective-permute-start(f32[112,384]{1,0:T(8,128)S(1)} %join.1), channel_id=1, source_target_pairs={{0,8},{1,9},{2,10},{3,11},{4,12},{5,13},{6,14},{7,15},{8,0},{9,1},... | collective-permute-start | bytes 516104 | tf_op jit(solution)/shard_map/ppermute | solution.py:288
  7.7 5.5 %collective-permute-start.6 = (f32[112,256]{1,0:T(8,128)S(1)}, f32[112,256]{1,0:T(8,128)S(1)}, u32[]{:S(2)}, u32[]{:S(2)}) collective-permute-start(f32[112,256]{1,0:T(8,128)S(1)} %copy-done), channel_id=1, source_target_pairs={{0,2},{1,3},{2,0},{3,1},{4,6},{5,7},{6,4},{7,5},{8,10},{9,11},{10,... | collective-permute-start | bytes 344072 | tf_op jit(solution)/shard_map/ppermute | solution.py:290
  10.5 0.7 %copy-start.2 = (f32[256]{0:T(256)S(1)}, f32[256]{0:T(256)}, u32[]{:S(2)}) copy-start(f32[256]{0:T(256)} %param.7) | copy-start | bytes 3076
  10.6 5.4 %collective-permute-start.5 = (f32[112,256]{1,0:T(8,128)S(1)}, f32[112,256]{1,0:T(8,128)S(1)}, u32[]{:S(2)}, u32[]{:S(2)}) collective-permute-start(f32[112,256]{1,0:T(8,128)S(1)} %collective-permute-done.4.refs_0_), channel_id=1, source_target_pairs={{0,2},{1,3},{2,0},{3,1},{4,6},{5,7},{6,4},{7,5},{8,10},{9,11},{10,... | collective-permute-start | bytes 344072 | tf_op jit(solution)/shard_map/ppermute | solution.py:292
  14.7 2.2 %collective-permute-start.3 = (f32[448,384]{1,0:T(8,128)S(1)}, f32[448,384]{1,0:T(8,128)S(1)}, u32[]{:S(2)}, u32[]{:S(2)}) collective-permute-start(f32[448,384]{1,0:T(8,128)S(1)} %pad_maximum_fusion.refs_0_), channel_id=1, source_target_pairs={{0,1},{1,0},{2,3},{3,2},{4,5},{5,4},{6,7},{7,6},{8,9},{9,8},{10,11... | collective-permute-start | bytes 2064392 | tf_op jit(solution)/shard_map/ppermute | solution.py:294
  17.8 8.0 %collective-permute-start.7 = (f32[112,128]{1,0:T(8,128)S(1)}, f32[112,128]{1,0:T(8,128)S(1)}, u32[]{:S(2)}, u32[]{:S(2)}) collective-permute-start(f32[112,128]{1,0:T(8,128)S(1)} %get-tuple-element.34), channel_id=1, source_target_pairs={{4,0},{5,1},{6,2},{7,3},{0,4},{1,5},{2,6},{3,7},{12,8},{13,9},{14,... | collective-permute-start | bytes 172040 | tf_op jit(solution)/shard_map/ppermute | solution.py:310
  19.0 6.8 %collective-permute-start.8 = (f32[112,128]{1,0:T(8,128)S(1)}, f32[112,128]{1,0:T(8,128)S(1)}, u32[]{:S(2)}, u32[]{:S(2)}) collective-permute-start(f32[112,128]{1,0:T(8,128)S(1)} %get-tuple-element.35), channel_id=1, source_target_pairs={{6,0},{7,1},{4,2},{5,3},{2,4},{3,5},{0,6},{1,7},{14,8},{15,9},{12,... | collective-permute-start | bytes 172040 | tf_op jit(solution)/shard_map/ppermute | solution.py:310
  22.6 4.2 %collective-permute-start.9 = (f32[112,128]{1,0:T(8,128)S(1)}, f32[112,128]{1,0:T(8,128)S(1)}, u32[]{:S(2)}, u32[]{:S(2)}) collective-permute-start(f32[112,128]{1,0:T(8,128)S(1)} %get-tuple-element.36), channel_id=1, source_target_pairs={{2,0},{3,1},{0,2},{1,3},{6,4},{7,5},{4,6},{5,7},{10,8},{11,9},{8,1... | collective-permute-start | bytes 172040 | tf_op jit(solution)/shard_map/ppermute | solution.py:310

commit v6 on v5

--- a/solution.py
+++ b/solution.py
@@ -59,17 +59,18 @@
 
 
 def fill_rows(x_ref, at, block, scale):
-    x = block * scale
+    high, low = split(block * scale)
+    x = high.astype(F32) + low.astype(F32)
     norm = jnp.sum(x * x, axis=1, keepdims=True)
-    high, low = split(-2.0 * x)
+    high, low = (-2.0 * high.astype(F32)).astype(BF16), (-2.0 * low.astype(F32)).astype(BF16)
     put(x_ref, at, (high, low, high, low, norm_lanes(norm, 0)))
 
 
 def fill_cols(y_ref, v_ref, at, block, scale, amplitude):
     features = scale.shape[1]
-    y = block[:, :features] * scale
+    high, low = split(block[:, :features] * scale)
+    y = high.astype(F32) + low.astype(F32)
     norm = jnp.sum(y * y, axis=1, keepdims=True)
-    high, low = split(y)
     put(y_ref, at, (high, high, low, low, norm_lanes(norm, 3)))
     put(v_ref, at, split(block[:, features:] * (amplitude * LN2)))
 
@@ -285,7 +286,7 @@
         here, features = points.shape
         both = blank((here, features + vectors.shape[1]), 20)
         both = join(points, vectors, both)
-        got = [lax.ppermute(both, AXES, along_outer(k)) for k in range(n_outer - 1, 0, -1)]
+        got = [lax.ppermute(both, AXES, along_outer(k)) for k in [n_outer - 1, *range(1, n_outer - 1)]]
         for k in direct[:-1]:
             points_of[k] = lax.ppermute(points, AXES, along_line(k))
         for k in forwarded:
@@ -302,10 +303,10 @@
         part, x_last = times_prepared(scale, last, [mine], 10)
         total |= dict(zip(forwarded, part))
         x |= dict(zip(forwarded, x_last))
-        ks = [*forwarded, *direct[1:]]
+        ks = [*forwarded, *direct[1:], 1]
         part, theirs = times_columns(scale, outputscale, noise, [cols_theirs], [x[k] for k in ks], [total[k] for k in ks], 10)
         total |= dict(zip(ks, part))
-        total |= dict(zip([0, 1], times_near(theirs, [x[0], x[1]], [total[0], total[1]], 10)))
+        total |= dict(zip([0], times_near(theirs, [x[0]], [total[0]], 10)))
         got = [
             lax.ppermute(total[k], AXES, [(b, a) for a, b in along_line(k)]) for k in [*direct[1:], *forwarded, 1]
         ]

time: 27.7 us -> 27.5 us (level)
  transfers between devices with their start and end apart: 10 -> 10, of which waited for: 6 -> 5; matrix products, arithmetic and copies ran while one was open for 0% -> 0% of each run, Pallas kernels for 10% -> 10%
where the time goes in v6:
time: 27.5 us; the launch traced here: 27.3 us
  starting transfers between devices  13.8 us (50%)
  waiting for transfers between devices  7.39 us (27%)
  Pallas kernels  3.92 us (14%)
  between operations  1.42 us (5%)
  other arithmetic  0.68 us (2%)
    ppermute x1, starting transfers between devices, per_device(): points_of = {half: lax.ppermute(points, AXES, along_line(half))}  4.04 us
    ppermute x3, starting transfers between devices, per_device(): lax.ppermute(total[k], AXES, [(b, a) for a, b in along_line(k)])  4.01 us
    ppermute x3, waiting for transfers between devices, per_device(): lax.ppermute(total[k], AXES, [(b, a) for a, b in along_line(k)])  3.93 us
    ppermute x3, starting transfers between devices, per_device(): lax.ppermute(both, AXES, along_outer(k))  3.55 us
    pallas_call x2, Pallas kernels, times_columns(): pl.pallas_call(functools.partial(tile_kernel, len(cols), len(rows)), out_...  2.23 us
    ppermute x1, waiting for transfers between devices, per_device(): points_of[k] = lax.ppermute(points, AXES, along_line(k))  1.77 us
    ppermute x1, starting transfers between devices, per_device(): points_of[k] = lax.ppermute(points, AXES, along_line(k))  1.58 us
    ppermute x3, waiting for transfers between devices, per_device(): lax.ppermute(both, AXES, along_outer(k))  1.37 us
  transfers between devices with their start and end apart: 10, of which 5 were waited for; matrix products, arithmetic and copies ran while one was open for 0% of the time, Pallas kernels for 10%

profile of v6, /device:TPU:0, one launch (start us, length us, event | category | flops | bytes accessed | tf_op | source)
XLA Modules:
  0.0 27.3 jit_solution(14348855731424297288)
XLA Ops:
  0.0 0.0 copy-start
  0.0 0.0 copy-start.1
  0.0 4.0 %collective-permute-start.4 = (f32[112,256]{1,0:T(8,128)}, f32[112,256]{1,0:T(8,128)S(1)}, u32[]{:S(2)}, u32[]{:S(2)}) collective-permute-start(f32[112,256]{1,0:T(8,128)} %refs_1_.1), channel_id=1, source_target_pairs={{0,4},{1,5},{2,6},{3,7},{4,0},{5,1},{6,2},{7,3},{8,12},{9,13},{10,... | collective-permute-start | bytes 344072 | tf_op jit(solution)/shard_map/ppermute | solution.py:285
  4.1 0.0 copy-done
  4.1 0.0 copy-done.1
  4.1 2.5 %collective-permute-start = (f32[112,384]{1,0:T(8,128)S(1)}, f32[112,384]{1,0:T(8,128)S(1)}, u32[]{:S(2)}, u32[]{:S(2)}) collective-permute-start(f32[112,384]{1,0:T(8,128)S(1)} %join.1), channel_id=1, source_target_pairs={{0,24},{1,25},{2,26},{3,27},{4,28},{5,29},{6,30},{7,31},{8,16},{9,... | collective-permute-start | bytes 516104 | tf_op jit(solution)/shard_map/ppermute | solution.py:289
  6.6 0.5 %collective-permute-start.1 = (f32[112,384]{1,0:T(8,128)S(1)}, f32[112,384]{1,0:T(8,128)S(1)}, u32[]{:S(2)}, u32[]{:S(2)}) collective-permute-start(f32[112,384]{1,0:T(8,128)S(1)} %join.1), channel_id=1, source_target_pairs={{0,8},{1,9},{2,10},{3,11},{4,12},{5,13},{6,14},{7,15},{8,0},{9,1},... | collective-permute-start | bytes 516104 | tf_op jit(solution)/shard_map/ppermute | solution.py:289
  7.1 0.5 %collective-permute-start.2 = (f32[112,384]{1,0:T(8,128)S(1)}, f32[112,384]{1,0:T(8,128)S(1)}, u32[]{:S(2)}, u32[]{:S(2)}) collective-permute-start(f32[112,384]{1,0:T(8,128)S(1)} %join.1), channel_id=1, source_target_pairs={{0,16},{1,17},{2,18},{3,19},{4,20},{5,21},{6,22},{7,23},{8,24},{9,... | collective-permute-start | bytes 516104 | tf_op jit(solution)/shard_map/ppermute | solution.py:289
  7.7 1.6 %collective-permute-start.6 = (f32[112,256]{1,0:T(8,128)S(1)}, f32[112,256]{1,0:T(8,128)S(1)}, u32[]{:S(2)}, u32[]{:S(2)}) collective-permute-start(f32[112,256]{1,0:T(8,128)S(1)} %copy-done), channel_id=1, source_target_pairs={{0,2},{1,3},{2,0},{3,1},{4,6},{5,7},{6,4},{7,5},{8,10},{9,11},{10,... | collective-permute-start | bytes 344072 | tf_op jit(solution)/shard_map/ppermute | solution.py:291
  10.5 0.0 copy-start.2
  10.5 0.0 collective-permute-done.4.refs_0_
  10.6 0.5 %collective-permute-start.5 = (f32[112,256]{1,0:T(8,128)S(1)}, f32[112,256]{1,0:T(8,128)S(1)}, u32[]{:S(2)}, u32[]{:S(2)}) collective-permute-start(f32[112,256]{1,0:T(8,128)S(1)} %collective-permute-done.4.refs_0_), channel_id=1, source_target_pairs={{0,2},{1,3},{2,0},{3,1},{4,6},{5,7},{6,4},{7,5},{8,10},{9,11},{10,... | collective-permute-start | bytes 344072 | tf_op jit(solution)/shard_map/ppermute | solution.py:293
  11.1 0.1 copy-done.2
  11.2 0.2 rows.2
  11.4 1.8 %collective-permute-done.6.refs_0_ = f32[112,256]{1,0:T(8,128)S(1)} collective-permute-done((f32[112,256]{1,0:T(8,128)S(1)}, f32[112,256]{1,0:T(8,128)S(1)}, u32[]{:S(2)}, u32[]{:S(2)}) %collective-permute-start.6) | collective-permute-done | bytes 114720 | tf_op jit(solution)/shard_map/ppermute | solution.py:291
  13.2 0.1 rows.3.refs_2_.refs_3_
  13.3 0.0 collective-permute-done
  13.3 1.4 %collective-permute-done.1 = f32[112,384]{1,0:T(8,128)S(1)} collective-permute-done((f32[112,384]{1,0:T(8,128)S(1)}, f32[112,384]{1,0:T(8,128)S(1)}, u32[]{:S(2)}, u32[]{:S(2)}) %collective-permute-start.1) | collective-permute-done | bytes 172064 | tf_op jit(solution)/shard_map/ppermute | solution.py:289
  14.7 0.0 collective-permute-done.2
  14.7 0.1 collective-permute-start.3
  14.8 1.1 %tile.2 = (f32[112,128]{1,0:T(8,128)S(1)}, f32[112,128]{1,0:T(8,128)S(1)}, f32[112,128]{1,0:T(8,128)S(1)}, bf16[448,1152]{1,0:T(8,128)(2,1)S(1)}, bf16[448,256]{1,0:T(8,128)(2,1)S(1)}) custom-call(f32[1,256]{1,0:T(1,128)S(1)} %bitcast.3, f32[1]{0:T(128)S(6)} %copy.8.amp_ref, f32[1]{0:T(128)S(6)} %copy.9.noise_ref, f32[448,384]{1,0:T(8,128)S(1)} %pad_maximum_fusion.refs_0_, ...), custom_call_target="tpu_custom_call" | custom-call | flops 20000000000 | bytes 1024 | tf_op jit(solution)/shard_map/tile/pallas_call | solution.py:179
  15.9 0.0 collective-permute-done.5.refs_0_
  15.9 0.7 %last.1 = (f32[112,128]{1,0:T(8,128)S(1)}, bf16[112,1152]{1,0:T(8,128)(2,1)S(1)}) custom-call(f32[1,256]{1,0:T(1,128)S(1)} %bitcast.4, f32[112,256]{1,0:T(8,128)S(1)} %collective-permute-done.5.refs_0_, bf16[448,1152]{1,0:T(8,128)(2,1)S(1)} %get-tuple-element.26.refs_1_, bf16[448,256]{1,0:T(8,128)(2,1)S(1)} %get-tuple-element.27.refs_2_), custom_call_target="tpu_custom_call" | custom-call | flops 10000000000 | bytes 1024 | tf_op jit(solution)/shard_map/last/pallas_call | solution.py:210
  16.6 0.3 %collective-permute-done.3.refs_0_ = f32[448,384]{1,0:T(8,128)S(1)} collective-permute-done((f32[448,384]{1,0:T(8,128)S(1)}, f32[448,384]{1,0:T(8,128)S(1)}, u32[]{:S(2)}, u32[]{:S(2)}) %collective-permute-start.3) | collective-permute-done | bytes 688160 | tf_op jit(solution)/shard_map/ppermute | solution.py:295
  16.9 1.1 %tile.3 = (f32[112,128]{1,0:T(8,128)S(1)}, f32[112,128]{1,0:T(8,128)S(1)}, f32[112,128]{1,0:T(8,128)S(1)}, bf16[448,1152]{1,0:T(8,128)(2,1)S(1)}, bf16[448,256]{1,0:T(8,128)(2,1)S(1)}) custom-call(f32[1,256]{1,0:T(1,128)S(1)} %bitcast.5, f32[1]{0:T(128)S(6)} %copy.8.amp_ref, f32[1]{0:T(128)S(6)} %copy.9.noise_ref, ...), custom_call_target="tpu_custom_call" | custom-call | flops 10000000000 | bytes 1024 | tf_op jit(solution)/shard_map/tile/pallas_call | solution.py:179
  18.1 1.2 %collective-permute-start.7 = (f32[112,128]{1,0:T(8,128)S(1)}, f32[112,128]{1,0:T(8,128)S(1)}, u32[]{:S(2)}, u32[]{:S(2)}) collective-permute-start(f32[112,128]{1,0:T(8,128)S(1)} %get-tuple-element.32), channel_id=1, source_target_pairs={{4,0},{5,1},{6,2},{7,3},{0,4},{1,5},{2,6},{3,7},{12,8},{13,9},{14,... | collective-permute-start | bytes 172040 | tf_op jit(solution)/shard_map/ppermute | solution.py:311
  19.3 2.8 %collective-permute-start.8 = (f32[112,128]{1,0:T(8,128)S(1)}, f32[112,128]{1,0:T(8,128)S(1)}, u32[]{:S(2)}, u32[]{:S(2)}) collective-permute-start(f32[112,128]{1,0:T(8,128)S(1)} %get-tuple-element.33), channel_id=1, source_target_pairs={{6,0},{7,1},{4,2},{5,3},{2,4},{3,5},{0,6},{1,7},{14,8},{15,9},{12,... | collective-permute-start | bytes 172040 | tf_op jit(solution)/shard_map/ppermute | solution.py:311
  22.1 0.0 collective-permute-start.9
  22.1 0.7 %near.1.refs_0_ = f32[112,128]{1,0:T(8,128)S(1)} custom-call(bf16[448,1152]{1,0:T(8,128)(2,1)S(1)} %get-tuple-element.30.y_ref, bf16[448,256]{1,0:T(8,128)(2,1)S(1)} %get-tuple-element.31.v_ref, bf16[112,1152]{1,0:T(8,128)(2,1)S(1)} %get-tuple-element.20.refs_1_.refs_0_, f32[112,128]{1,0:T(8,128)S(1)} %get-tuple-element.22.refs_1_), custom_call_target="tpu_custom_call" | custom-call | flops 10000000000 | bytes 1024 | tf_op jit(solution)/shard_map/near/pallas_call | solution.py:233
  22.7 3.3 %collective-permute-done.7.refs_1_ = f32[112,128]{1,0:T(8,128)S(1)} collective-permute-done((f32[112,128]{1,0:T(8,128)S(1)}, f32[112,128]{1,0:T(8,128)S(1)}, u32[]{:S(2)}, u32[]{:S(2)}) %collective-permute-start.7) | collective-permute-done | bytes 57376 | tf_op jit(solution)/shard_map/ppermute | solution.py:311
  26.1 0.0 collective-permute-done.8.refs_2_
  26.1 0.6 %collective-permute-done.9 = f32[112,128]{1,0:T(8,128)S(1)} collective-permute-done((f32[112,128]{1,0:T(8,128)S(1)}, f32[112,128]{1,0:T(8,128)S(1)}, u32[]{:S(2)}, u32[]{:S(2)}) %collective-permute-start.9) | collective-permute-done | bytes 57376 | tf_op jit(solution)/shard_map/ppermute | solution.py:311
  26.7 0.6 %add.4 = f32[112,128]{1,0:T(8,128)} add(f32[112,128]{1,0:T(8,128)S(1)} %add.5, f32[112,128]{1,0:T(8,128)S(1)} %collective-permute-done.9) | non-fusion elementwise | flops 14336 | bytes 172032 | tf_op jit(solution)/shard_map/add | solution.py:313
  (4 shorter events, 0.1 us)
Async XLA Ops:
  0.0 4.1 %copy-start = (f32[112,256]{1,0:T(8,128)S(1)}, f32[112,256]{1,0:T(8,128)}, u32[]{:S(2)}) copy-start(f32[112,256]{1,0:T(8,128)} %refs_1_.1) | copy-start | bytes 344068
  0.0 4.1 %copy-start.1 = (f32[112,128]{1,0:T(8,128)S(1)}, f32[112,128]{1,0:T(8,128)}, u32[]{:S(2)}) copy-start(f32[112,128]{1,0:T(8,128)} %b_ref.1) | copy-start | bytes 172036
  0.0 10.5 %collective-permute-start.4 = (f32[112,256]{1,0:T(8,128)}, f32[112,256]{1,0:T(8,128)S(1)}, u32[]{:S(2)}, u32[]{:S(2)}) collective-permute-start(f32[112,256]{1,0:T(8,128)} %refs_1_.1), channel_id=1, source_target_pairs={{0,4},{1,5},{2,6},{3,7},{4,0},{5,1},{6,2},{7,3},{8,12},{9,13},{10,... | collective-permute-start | bytes 344072 | tf_op jit(solution)/shard_map/ppermute | solution.py:285
  4.1 9.2 %collective-permute-start = (f32[112,384]{1,0:T(8,128)S(1)}, f32[112,384]{1,0:T(8,128)S(1)}, u32[]{:S(2)}, u32[]{:S(2)}) collective-permute-start(f32[112,384]{1,0:T(8,128)S(1)} %join.1), channel_id=1, source_target_pairs={{0,24},{1,25},{2,26},{3,27},{4,28},{5,29},{6,30},{7,31},{8,16},{9,... | collective-permute-start | bytes 516104 | tf_op jit(solution)/shard_map/ppermute | solution.py:289
  6.6 8.1 %collective-permute-start.1 = (f32[112,384]{1,0:T(8,128)S(1)}, f32[112,384]{1,0:T(8,128)S(1)}, u32[]{:S(2)}, u32[]{:S(2)}) collective-permute-start(f32[112,384]{1,0:T(8,128)S(1)} %join.1), channel_id=1, source_target_pairs={{0,8},{1,9},{2,10},{3,11},{4,12},{5,13},{6,14},{7,15},{8,0},{9,1},... | collective-permute-start | bytes 516104 | tf_op jit(solution)/shard_map/ppermute | solution.py:289
  7.1 7.5 %collective-permute-start.2 = (f32[112,384]{1,0:T(8,128)S(1)}, f32[112,384]{1,0:T(8,128)S(1)}, u32[]{:S(2)}, u32[]{:S(2)}) collective-permute-start(f32[112,384]{1,0:T(8,128)S(1)} %join.1), channel_id=1, source_target_pairs={{0,16},{1,17},{2,18},{3,19},{4,20},{5,21},{6,22},{7,23},{8,24},{9,... | collective-permute-start | bytes 516104 | tf_op jit(solution)/shard_map/ppermute | solution.py:289
  7.7 5.5 %collective-permute-start.6 = (f32[112,256]{1,0:T(8,128)S(1)}, f32[112,256]{1,0:T(8,128)S(1)}, u32[]{:S(2)}, u32[]{:S(2)}) collective-permute-start(f32[112,256]{1,0:T(8,128)S(1)} %copy-done), channel_id=1, source_target_pairs={{0,2},{1,3},{2,0},{3,1},{4,6},{5,7},{6,4},{7,5},{8,10},{9,11},{10,... | collective-permute-start | bytes 344072 | tf_op jit(solution)/shard_map/ppermute | solution.py:291
  10.5 0.7 %copy-start.2 = (f32[256]{0:T(256)S(1)}, f32[256]{0:T(256)}, u32[]{:S(2)}) copy-start(f32[256]{0:T(256)} %param.7) | copy-start | bytes 3076
  10.6 5.4 %collective-permute-start.5 = (f32[112,256]{1,0:T(8,128)S(1)}, f32[112,256]{1,0:T(8,128)S(1)}, u32[]{:S(2)}, u32[]{:S(2)}) collective-permute-start(f32[112,256]{1,0:T(8,128)S(1)} %collective-permute-done.4.refs_0_), channel_id=1, source_target_pairs={{0,2},{1,3},{2,0},{3,1},{4,6},{5,7},{6,4},{7,5},{8,10},{9,11},{10,... | collective-permute-start | bytes 344072 | tf_op jit(solution)/shard_map/ppermute | solution.py:293
  14.7 2.2 %collective-permute-start.3 = (f32[448,384]{1,0:T(8,128)S(1)}, f32[448,384]{1,0:T(8,128)S(1)}, u32[]{:S(2)}, u32[]{:S(2)}) collective-permute-start(f32[448,384]{1,0:T(8,128)S(1)} %pad_maximum_fusion.refs_0_), channel_id=1, source_target_pairs={{0,1},{1,0},{2,3},{3,2},{4,5},{5,4},{6,7},{7,6},{8,9},{9,8},{10,11... | collective-permute-start | bytes 2064392 | tf_op jit(solution)/shard_map/ppermute | solution.py:295
  18.1 8.0 %collective-permute-start.7 = (f32[112,128]{1,0:T(8,128)S(1)}, f32[112,128]{1,0:T(8,128)S(1)}, u32[]{:S(2)}, u32[]{:S(2)}) collective-permute-start(f32[112,128]{1,0:T(8,128)S(1)} %get-tuple-element.32), channel_id=1, source_target_pairs={{4,0},{5,1},{6,2},{7,3},{0,4},{1,5},{2,6},{3,7},{12,8},{13,9},{14,... | collective-permute-start | bytes 172040 | tf_op jit(solution)/shard_map/ppermute | solution.py:311
  19.3 6.8 %collective-permute-start.8 = (f32[112,128]{1,0:T(8,128)S(1)}, f32[112,128]{1,0:T(8,128)S(1)}, u32[]{:S(2)}, u32[]{:S(2)}) collective-permute-start(f32[112,128]{1,0:T(8,128)S(1)} %get-tuple-element.33), channel_id=1, source_target_pairs={{6,0},{7,1},{4,2},{5,3},{2,4},{3,5},{0,6},{1,7},{14,8},{15,9},{12,... | collective-permute-start | bytes 172040 | tf_op jit(solution)/shard_map/ppermute | solution.py:311
  22.1 4.6 %collective-permute-start.9 = (f32[112,128]{1,0:T(8,128)S(1)}, f32[112,128]{1,0:T(8,128)S(1)}, u32[]{:S(2)}, u32[]{:S(2)}) collective-permute-start(f32[112,128]{1,0:T(8,128)S(1)} %get-tuple-element.34), channel_id=1, source_target_pairs={{2,0},{3,1},{0,2},{1,3},{6,4},{7,5},{4,6},{5,7},{10,8},{11,9},{8,1... | collective-permute-start | bytes 172040 | tf_op jit(solution)/shard_map/ppermute | solution.py:311

commit v7 on v6

--- a/solution.py
+++ b/solution.py
@@ -11,7 +11,6 @@
 AXES = ("outer", "inner")
 CORES = 2
 VMEM = pl.BlockSpec(memory_space=pltpu.VMEM)
-SMEM = pl.BlockSpec(memory_space=pltpu.SMEM)
 BF16 = jnp.bfloat16
 F32 = jnp.float32
 LIMIT = 24 * 1024 * 1024
@@ -152,7 +151,7 @@
     cols, rows, rest = refs[:n_cols], refs[n_cols : n_cols + n_rows], refs[n_cols + n_rows :]
     starts, outs, (y_ref, v_ref) = rest[: -n_rows - 2], rest[-n_rows - 2 : -2], rest[-2:]
     here = rows[0].shape[0]
-    fill_all(cols, y_ref, v_ref, kernel_scale(scale_ref), amp_ref[0])
+    fill_all(cols, y_ref, v_ref, kernel_scale(scale_ref), amp_ref[...])
     for group in groups(n_rows):
         total = times_tile(jnp.concatenate([rows[i][...] for i in group], axis=0), y_ref, v_ref)
         for j, i in enumerate(group):
@@ -160,7 +159,7 @@
             if starts:
                 out = out + starts[i][...]
             elif i == 0:
-                out = out + noise_ref[0] * cols[0][:here, -out.shape[1] :]
+                out = out + noise_ref[...] * cols[0][:here, -out.shape[1] :]
             outs[i][...] = out
 
 
@@ -175,12 +174,12 @@
 def times_columns(scale, amplitude, noise, cols, rows, starts, us):
     here = rows[0].shape[0]
     features = scale.shape[1]
-    given = [scale, amplitude, noise, *cols, *rows, *starts]
+    given = [scale, amplitude[None, :], noise[None, :], *cols, *rows, *starts]
     *outs, y, v = pl.pallas_call(
         functools.partial(tile_kernel, len(cols), len(rows)),
         out_shape=[jax.ShapeDtypeStruct((here, cols[0].shape[1] - features), F32)] * len(rows)
         + prepared_shapes(cols, features),
-        in_specs=[VMEM, SMEM, SMEM] + [VMEM] * (len(given) - 3),
+        in_specs=[VMEM] * len(given),
         out_specs=[VMEM] * (len(rows) + 2),
         compiler_params=params(),
         cost_estimate=cost(us),

time: 27.5 us -> 27.4 us (level)
  no operation moved by 1% of the time
where the time goes in v7:
time: 27.4 us; the launch traced here: 27.3 us
  starting transfers between devices  13.8 us (50%)
  waiting for transfers between devices  7.41 us (27%)
  Pallas kernels  3.83 us (14%)
  between operations  1.42 us (5%)
  other arithmetic  0.68 us (2%)
    ppermute x1, starting transfers between devices, per_device(): points_of = {half: lax.ppermute(points, AXES, along_line(half))}  4.04 us
    ppermute x3, starting transfers between devices, per_device(): lax.ppermute(total[k], AXES, [(b, a) for a, b in along_line(k)])  4.01 us
    ppermute x3, waiting for transfers between devices, per_device(): lax.ppermute(total[k], AXES, [(b, a) for a, b in along_line(k)])  3.91 us
    ppermute x3, starting transfers between devices, per_device(): lax.ppermute(both, AXES, along_outer(k))  3.55 us
    pallas_call x2, Pallas kernels, times_columns(): pl.pallas_call(functools.partial(tile_kernel, len(cols), len(rows)), out_...  2.14 us
    ppermute x1, waiting for transfers between devices, per_device(): points_of[k] = lax.ppermute(points, AXES, along_line(k))  1.77 us
    ppermute x1, starting transfers between devices, per_device(): points_of[k] = lax.ppermute(points, AXES, along_line(k))  1.58 us
    ppermute x3, waiting for transfers between devices, per_device(): lax.ppermute(both, AXES, along_outer(k))  1.37 us
  transfers between devices with their start and end apart: 10, of which 5 were waited for; matrix products, arithmetic and copies ran while one was open for 0% of the time, Pallas kernels for 10%

profile of v7, /device:TPU:0, one launch (start us, length us, event | category | flops | bytes accessed | tf_op | source)
XLA Modules:
  0.0 27.3 jit_solution(7199773734775303065)
XLA Ops:
  0.0 0.0 copy-start
  0.0 0.0 copy-start.1
  0.0 4.0 %collective-permute-start.4 = (f32[112,256]{1,0:T(8,128)}, f32[112,256]{1,0:T(8,128)S(1)}, u32[]{:S(2)}, u32[]{:S(2)}) collective-permute-start(f32[112,256]{1,0:T(8,128)} %refs_1_.1), channel_id=1, source_target_pairs={{0,4},{1,5},{2,6},{3,7},{4,0},{5,1},{6,2},{7,3},{8,12},{9,13},{10,... | collective-permute-start | bytes 344072 | tf_op jit(solution)/shard_map/ppermute | solution.py:284
  4.1 0.0 copy-done
  4.1 0.0 copy-done.1
  4.1 2.5 %collective-permute-start = (f32[112,384]{1,0:T(8,128)S(1)}, f32[112,384]{1,0:T(8,128)S(1)}, u32[]{:S(2)}, u32[]{:S(2)}) collective-permute-start(f32[112,384]{1,0:T(8,128)S(1)} %join.1), channel_id=1, source_target_pairs={{0,24},{1,25},{2,26},{3,27},{4,28},{5,29},{6,30},{7,31},{8,16},{9,... | collective-permute-start | bytes 516104 | tf_op jit(solution)/shard_map/ppermute | solution.py:288
  6.6 0.5 %collective-permute-start.1 = (f32[112,384]{1,0:T(8,128)S(1)}, f32[112,384]{1,0:T(8,128)S(1)}, u32[]{:S(2)}, u32[]{:S(2)}) collective-permute-start(f32[112,384]{1,0:T(8,128)S(1)} %join.1), channel_id=1, source_target_pairs={{0,8},{1,9},{2,10},{3,11},{4,12},{5,13},{6,14},{7,15},{8,0},{9,1},... | collective-permute-start | bytes 516104 | tf_op jit(solution)/shard_map/ppermute | solution.py:288
  7.1 0.5 %collective-permute-start.2 = (f32[112,384]{1,0:T(8,128)S(1)}, f32[112,384]{1,0:T(8,128)S(1)}, u32[]{:S(2)}, u32[]{:S(2)}) collective-permute-start(f32[112,384]{1,0:T(8,128)S(1)} %join.1), channel_id=1, source_target_pairs={{0,16},{1,17},{2,18},{3,19},{4,20},{5,21},{6,22},{7,23},{8,24},{9,... | collective-permute-start | bytes 516104 | tf_op jit(solution)/shard_map/ppermute | solution.py:288
  7.7 1.6 %collective-permute-start.6 = (f32[112,256]{1,0:T(8,128)S(1)}, f32[112,256]{1,0:T(8,128)S(1)}, u32[]{:S(2)}, u32[]{:S(2)}) collective-permute-start(f32[112,256]{1,0:T(8,128)S(1)} %copy-done), channel_id=1, source_target_pairs={{0,2},{1,3},{2,0},{3,1},{4,6},{5,7},{6,4},{7,5},{8,10},{9,11},{10,... | collective-permute-start | bytes 344072 | tf_op jit(solution)/shard_map/ppermute | solution.py:290
  10.5 0.0 copy-start.2
  10.5 0.0 collective-permute-done.4.refs_0_
  10.6 0.5 %collective-permute-start.5 = (f32[112,256]{1,0:T(8,128)S(1)}, f32[112,256]{1,0:T(8,128)S(1)}, u32[]{:S(2)}, u32[]{:S(2)}) collective-permute-start(f32[112,256]{1,0:T(8,128)S(1)} %collective-permute-done.4.refs_0_), channel_id=1, source_target_pairs={{0,2},{1,3},{2,0},{3,1},{4,6},{5,7},{6,4},{7,5},{8,10},{9,11},{10,... | collective-permute-start | bytes 344072 | tf_op jit(solution)/shard_map/ppermute | solution.py:292
  11.1 0.1 copy-done.2
  11.2 0.2 rows.2
  11.4 1.8 %collective-permute-done.6.refs_0_ = f32[112,256]{1,0:T(8,128)S(1)} collective-permute-done((f32[112,256]{1,0:T(8,128)S(1)}, f32[112,256]{1,0:T(8,128)S(1)}, u32[]{:S(2)}, u32[]{:S(2)}) %collective-permute-start.6) | collective-permute-done | bytes 114720 | tf_op jit(solution)/shard_map/ppermute | solution.py:290
  13.2 0.1 rows.3.refs_2_.refs_3_
  13.3 0.0 collective-permute-done
  13.3 1.4 %collective-permute-done.1 = f32[112,384]{1,0:T(8,128)S(1)} collective-permute-done((f32[112,384]{1,0:T(8,128)S(1)}, f32[112,384]{1,0:T(8,128)S(1)}, u32[]{:S(2)}, u32[]{:S(2)}) %collective-permute-start.1) | collective-permute-done | bytes 172064 | tf_op jit(solution)/shard_map/ppermute | solution.py:288
  14.7 0.0 collective-permute-done.2
  14.7 0.1 collective-permute-start.3
  14.8 1.1 %tile.2 = (f32[112,128]{1,0:T(8,128)S(1)}, f32[112,128]{1,0:T(8,128)S(1)}, f32[112,128]{1,0:T(8,128)S(1)}, bf16[448,1152]{1,0:T(8,128)(2,1)S(1)}, bf16[448,256]{1,0:T(8,128)(2,1)S(1)}) custom-call(f32[1,256]{1,0:T(1,128)S(1)} %bitcast.9, f32[1,1]{1,0:T(1,128)} %bitcast.3.amp_ref, f32[1,1]{1,0:T(1,128)} %bitcast.5.noise_ref, ...), custom_call_target="tpu_custom_call" | custom-call | flops 20000000000 | bytes 1024 | tf_op jit(solution)/shard_map/tile/pallas_call | solution.py:178
  15.9 0.0 collective-permute-done.5.refs_0_
  15.9 0.7 %last.1 = (f32[112,128]{1,0:T(8,128)S(1)}, bf16[112,1152]{1,0:T(8,128)(2,1)S(1)}) custom-call(f32[1,256]{1,0:T(1,128)S(1)} %bitcast.10, f32[112,256]{1,0:T(8,128)S(1)} %collective-permute-done.5.refs_0_, bf16[448,1152]{1,0:T(8,128)(2,1)S(1)} %get-tuple-element.26.refs_1_, bf16[448,256]{1,0:T(8,128)(2,1)S(1)} %get-tuple-element.27.refs_2_), custom_call_target="tpu_custom_call" | custom-call | flops 10000000000 | bytes 1024 | tf_op jit(solution)/shard_map/last/pallas_call | solution.py:209
  16.6 0.4 %collective-permute-done.3.refs_0_ = f32[448,384]{1,0:T(8,128)S(1)} collective-permute-done((f32[448,384]{1,0:T(8,128)S(1)}, f32[448,384]{1,0:T(8,128)S(1)}, u32[]{:S(2)}, u32[]{:S(2)}) %collective-permute-start.3) | collective-permute-done | bytes 688160 | tf_op jit(solution)/shard_map/ppermute | solution.py:294
  16.9 1.1 %tile.3 = (f32[112,128]{1,0:T(8,128)S(1)}, f32[112,128]{1,0:T(8,128)S(1)}, f32[112,128]{1,0:T(8,128)S(1)}, bf16[448,1152]{1,0:T(8,128)(2,1)S(1)}, bf16[448,256]{1,0:T(8,128)(2,1)S(1)}) custom-call(f32[1,256]{1,0:T(1,128)S(1)} %bitcast.11, f32[1,1]{1,0:T(1,128)} %bitcast.4.amp_ref, f32[1,1]{1,0:T(1,128)} %bitcast.6.noise_ref, ...), custom_call_target="tpu_custom_call" | custom-call | flops 10000000000 | bytes 1024 | tf_op jit(solution)/shard_map/tile/pallas_call | solution.py:178
  18.0 1.2 %collective-permute-start.7 = (f32[112,128]{1,0:T(8,128)S(1)}, f32[112,128]{1,0:T(8,128)S(1)}, u32[]{:S(2)}, u32[]{:S(2)}) collective-permute-start(f32[112,128]{1,0:T(8,128)S(1)} %get-tuple-element.32), channel_id=1, source_target_pairs={{4,0},{5,1},{6,2},{7,3},{0,4},{1,5},{2,6},{3,7},{12,8},{13,9},{14,... | collective-permute-start | bytes 172040 | tf_op jit(solution)/shard_map/ppermute | solution.py:310
  19.2 2.8 %collective-permute-start.8 = (f32[112,128]{1,0:T(8,128)S(1)}, f32[112,128]{1,0:T(8,128)S(1)}, u32[]{:S(2)}, u32[]{:S(2)}) collective-permute-start(f32[112,128]{1,0:T(8,128)S(1)} %get-tuple-element.33), channel_id=1, source_target_pairs={{6,0},{7,1},{4,2},{5,3},{2,4},{3,5},{0,6},{1,7},{14,8},{15,9},{12,... | collective-permute-start | bytes 172040 | tf_op jit(solution)/shard_map/ppermute | solution.py:310
  22.0 0.0 collective-permute-start.9
  22.0 0.7 %near.1.refs_0_ = f32[112,128]{1,0:T(8,128)S(1)} custom-call(bf16[448,1152]{1,0:T(8,128)(2,1)S(1)} %get-tuple-element.30.y_ref, bf16[448,256]{1,0:T(8,128)(2,1)S(1)} %get-tuple-element.31.v_ref, bf16[112,1152]{1,0:T(8,128)(2,1)S(1)} %get-tuple-element.20.refs_1_.refs_0_, f32[112,128]{1,0:T(8,128)S(1)} %get-tuple-element.22.refs_1_), custom_call_target="tpu_custom_call" | custom-call | flops 10000000000 | bytes 1024 | tf_op jit(solution)/shard_map/near/pallas_call | solution.py:232
  22.7 3.3 %collective-permute-done.7.refs_1_ = f32[112,128]{1,0:T(8,128)S(1)} collective-permute-done((f32[112,128]{1,0:T(8,128)S(1)}, f32[112,128]{1,0:T(8,128)S(1)}, u32[]{:S(2)}, u32[]{:S(2)}) %collective-permute-start.7) | collective-permute-done | bytes 57376 | tf_op jit(solution)/shard_map/ppermute | solution.py:310
  26.0 0.0 collective-permute-done.8.refs_2_
  26.1 0.6 %collective-permute-done.9 = f32[112,128]{1,0:T(8,128)S(1)} collective-permute-done((f32[112,128]{1,0:T(8,128)S(1)}, f32[112,128]{1,0:T(8,128)S(1)}, u32[]{:S(2)}, u32[]{:S(2)}) %collective-permute-start.9) | collective-permute-done | bytes 57376 | tf_op jit(solution)/shard_map/ppermute | solution.py:310
  26.6 0.6 %add.4 = f32[112,128]{1,0:T(8,128)} add(f32[112,128]{1,0:T(8,128)S(1)} %add.5, f32[112,128]{1,0:T(8,128)S(1)} %collective-permute-done.9) | non-fusion elementwise | flops 14336 | bytes 172032 | tf_op jit(solution)/shard_map/add | solution.py:312
  (4 shorter events, 0.1 us)
Async XLA Ops:
  0.0 4.1 %copy-start = (f32[112,256]{1,0:T(8,128)S(1)}, f32[112,256]{1,0:T(8,128)}, u32[]{:S(2)}) copy-start(f32[112,256]{1,0:T(8,128)} %refs_1_.1) | copy-start | bytes 344068
  0.0 4.1 %copy-start.1 = (f32[112,128]{1,0:T(8,128)S(1)}, f32[112,128]{1,0:T(8,128)}, u32[]{:S(2)}) copy-start(f32[112,128]{1,0:T(8,128)} %b_ref.1) | copy-start | bytes 172036
  0.0 10.5 %collective-permute-start.4 = (f32[112,256]{1,0:T(8,128)}, f32[112,256]{1,0:T(8,128)S(1)}, u32[]{:S(2)}, u32[]{:S(2)}) collective-permute-start(f32[112,256]{1,0:T(8,128)} %refs_1_.1), channel_id=1, source_target_pairs={{0,4},{1,5},{2,6},{3,7},{4,0},{5,1},{6,2},{7,3},{8,12},{9,13},{10,... | collective-permute-start | bytes 344072 | tf_op jit(solution)/shard_map/ppermute | solution.py:284
  4.1 9.2 %collective-permute-start = (f32[112,384]{1,0:T(8,128)S(1)}, f32[112,384]{1,0:T(8,128)S(1)}, u32[]{:S(2)}, u32[]{:S(2)}) collective-permute-start(f32[112,384]{1,0:T(8,128)S(1)} %join.1), channel_id=1, source_target_pairs={{0,24},{1,25},{2,26},{3,27},{4,28},{5,29},{6,30},{7,31},{8,16},{9,... | collective-permute-start | bytes 516104 | tf_op jit(solution)/shard_map/ppermute | solution.py:288
  6.6 8.1 %collective-permute-start.1 = (f32[112,384]{1,0:T(8,128)S(1)}, f32[112,384]{1,0:T(8,128)S(1)}, u32[]{:S(2)}, u32[]{:S(2)}) collective-permute-start(f32[112,384]{1,0:T(8,128)S(1)} %join.1), channel_id=1, source_target_pairs={{0,8},{1,9},{2,10},{3,11},{4,12},{5,13},{6,14},{7,15},{8,0},{9,1},... | collective-permute-start | bytes 516104 | tf_op jit(solution)/shard_map/ppermute | solution.py:288
  7.1 7.5 %collective-permute-start.2 = (f32[112,384]{1,0:T(8,128)S(1)}, f32[112,384]{1,0:T(8,128)S(1)}, u32[]{:S(2)}, u32[]{:S(2)}) collective-permute-start(f32[112,384]{1,0:T(8,128)S(1)} %join.1), channel_id=1, source_target_pairs={{0,16},{1,17},{2,18},{3,19},{4,20},{5,21},{6,22},{7,23},{8,24},{9,... | collective-permute-start | bytes 516104 | tf_op jit(solution)/shard_map/ppermute | solution.py:288
  7.7 5.5 %collective-permute-start.6 = (f32[112,256]{1,0:T(8,128)S(1)}, f32[112,256]{1,0:T(8,128)S(1)}, u32[]{:S(2)}, u32[]{:S(2)}) collective-permute-start(f32[112,256]{1,0:T(8,128)S(1)} %copy-done), channel_id=1, source_target_pairs={{0,2},{1,3},{2,0},{3,1},{4,6},{5,7},{6,4},{7,5},{8,10},{9,11},{10,... | collective-permute-start | bytes 344072 | tf_op jit(solution)/shard_map/ppermute | solution.py:290
  10.5 0.7 %copy-start.2 = (f32[256]{0:T(256)S(1)}, f32[256]{0:T(256)}, u32[]{:S(2)}) copy-start(f32[256]{0:T(256)} %param.7) | copy-start | bytes 3076
  10.6 5.3 %collective-permute-start.5 = (f32[112,256]{1,0:T(8,128)S(1)}, f32[112,256]{1,0:T(8,128)S(1)}, u32[]{:S(2)}, u32[]{:S(2)}) collective-permute-start(f32[112,256]{1,0:T(8,128)S(1)} %collective-permute-done.4.refs_0_), channel_id=1, source_target_pairs={{0,2},{1,3},{2,0},{3,1},{4,6},{5,7},{6,4},{7,5},{8,10},{9,11},{10,... | collective-permute-start | bytes 344072 | tf_op jit(solution)/shard_map/ppermute | solution.py:292
  14.7 2.2 %collective-permute-start.3 = (f32[448,384]{1,0:T(8,128)S(1)}, f32[448,384]{1,0:T(8,128)S(1)}, u32[]{:S(2)}, u32[]{:S(2)}) collective-permute-start(f32[448,384]{1,0:T(8,128)S(1)} %pad_maximum_fusion.refs_0_), channel_id=1, source_target_pairs={{0,1},{1,0},{2,3},{3,2},{4,5},{5,4},{6,7},{7,6},{8,9},{9,8},{10,11... | collective-permute-start | bytes 2064392 | tf_op jit(solution)/shard_map/ppermute | solution.py:294
  18.0 8.0 %collective-permute-start.7 = (f32[112,128]{1,0:T(8,128)S(1)}, f32[112,128]{1,0:T(8,128)S(1)}, u32[]{:S(2)}, u32[]{:S(2)}) collective-permute-start(f32[112,128]{1,0:T(8,128)S(1)} %get-tuple-element.32), channel_id=1, source_target_pairs={{4,0},{5,1},{6,2},{7,3},{0,4},{1,5},{2,6},{3,7},{12,8},{13,9},{14,... | collective-permute-start | bytes 172040 | tf_op jit(solution)/shard_map/ppermute | solution.py:310
  19.2 6.8 %collective-permute-start.8 = (f32[112,128]{1,0:T(8,128)S(1)}, f32[112,128]{1,0:T(8,128)S(1)}, u32[]{:S(2)}, u32[]{:S(2)}) collective-permute-start(f32[112,128]{1,0:T(8,128)S(1)} %get-tuple-element.33), channel_id=1, source_target_pairs={{6,0},{7,1},{4,2},{5,3},{2,4},{3,5},{0,6},{1,7},{14,8},{15,9},{12,... | collective-permute-start | bytes 172040 | tf_op jit(solution)/shard_map/ppermute | solution.py:310
  22.0 4.6 %collective-permute-start.9 = (f32[112,128]{1,0:T(8,128)S(1)}, f32[112,128]{1,0:T(8,128)S(1)}, u32[]{:S(2)}, u32[]{:S(2)}) collective-permute-start(f32[112,128]{1,0:T(8,128)S(1)} %get-tuple-element.34), channel_id=1, source_target_pairs={{2,0},{3,1},{0,2},{1,3},{6,4},{7,5},{4,6},{5,7},{10,8},{11,9},{8,1... | collective-permute-start | bytes 172040 | tf_op jit(solution)/shard_map/ppermute | solution.py:310

commit v8 on v7

--- a/solution.py
+++ b/solution.py
@@ -238,25 +238,6 @@
         cost_estimate=cost(us),
         name="near",
     )(*prepared, *rows, *starts)
-
-
-def add_kernel(*refs):
-    out = refs[0][...]
-    for ref in refs[1:-1]:
-        out = out + ref[...]
-    refs[-1][...] = out
-
-
-def add_most(parts, us):
-    return pl.pallas_call(
-        add_kernel,
-        out_shape=jax.ShapeDtypeStruct(parts[0].shape, F32),
-        in_specs=[VMEM] * len(parts),
-        out_specs=VMEM,
-        compiler_params=params(),
-        cost_estimate=cost(us),
-        name="add",
-    )(*parts)
 
 
 def solution(mesh):
@@ -309,7 +290,7 @@
         got = [
             lax.ppermute(total[k], AXES, [(b, a) for a, b in along_line(k)]) for k in [*direct[1:], *forwarded, 1]
         ]
-        return add_most([total[0], *got[:-1]], 10) + got[-1]
+        return sum(got, total[0])
 
     placed = (P(AXES, None), P(AXES, None), P(), P(), P())
     return jax.shard_map(per_device, mesh=mesh, in_specs=placed, out_specs=P(AXES, None), check_vma=False)

time: 27.4 us -> 27.4 us (level)
  no operation moved by 1% of the time
where the time goes in v8:
time: 27.4 us; the launch traced here: 27.3 us
  starting transfers between devices  13.8 us (50%)
  waiting for transfers between devices  7.45 us (27%)
  Pallas kernels  3.81 us (14%)
  between operations  1.42 us (5%)
  other arithmetic  0.68 us (2%)
    ppermute x1, starting transfers between devices, per_device(): points_of = {half: lax.ppermute(points, AXES, along_line(half))}  4.04 us
    ppermute x3, starting transfers between devices, per_device(): lax.ppermute(total[k], AXES, [(b, a) for a, b in along_line(k)])  4 us
    ppermute x3, waiting for transfers between devices, per_device(): lax.ppermute(total[k], AXES, [(b, a) for a, b in along_line(k)])  3.94 us
    ppermute x3, starting transfers between devices, per_device(): lax.ppermute(both, AXES, along_outer(k))  3.55 us
    pallas_call x2, Pallas kernels, times_columns(): pl.pallas_call(functools.partial(tile_kernel, len(cols), len(rows)), out_...  2.14 us
    ppermute x1, waiting for transfers between devices, per_device(): points_of[k] = lax.ppermute(points, AXES, along_line(k))  1.77 us
    ppermute x1, starting transfers between devices, per_device(): points_of[k] = lax.ppermute(points, AXES, along_line(k))  1.58 us
    ppermute x3, waiting for transfers between devices, per_device(): lax.ppermute(both, AXES, along_outer(k))  1.37 us
  transfers between devices with their start and end apart: 10, of which 5 were waited for; matrix products, arithmetic and copies ran while one was open for 0% of the time, Pallas kernels for 10%

profile of v8, /device:TPU:0, one launch (start us, length us, event | category | flops | bytes accessed | tf_op | source)
XLA Modules:
  0.0 27.3 jit_solution(18186697927249998516)
XLA Ops:
  0.0 0.0 copy-start
  0.0 0.0 copy-start.1
  0.0 4.0 %collective-permute-start.4 = (f32[112,256]{1,0:T(8,128)}, f32[112,256]{1,0:T(8,128)S(1)}, u32[]{:S(2)}, u32[]{:S(2)}) collective-permute-start(f32[112,256]{1,0:T(8,128)} %refs_1_.1), channel_id=1, source_target_pairs={{0,4},{1,5},{2,6},{3,7},{4,0},{5,1},{6,2},{7,3},{8,12},{9,13},{10,... | collective-permute-start | bytes 344072 | tf_op jit(solution)/shard_map/ppermute | solution.py:265
  4.1 0.0 copy-done
  4.1 0.0 copy-done.1
  4.1 2.5 %collective-permute-start = (f32[112,384]{1,0:T(8,128)S(1)}, f32[112,384]{1,0:T(8,128)S(1)}, u32[]{:S(2)}, u32[]{:S(2)}) collective-permute-start(f32[112,384]{1,0:T(8,128)S(1)} %join.1), channel_id=1, source_target_pairs={{0,24},{1,25},{2,26},{3,27},{4,28},{5,29},{6,30},{7,31},{8,16},{9,... | collective-permute-start | bytes 516104 | tf_op jit(solution)/shard_map/ppermute | solution.py:269
  6.6 0.5 %collective-permute-start.1 = (f32[112,384]{1,0:T(8,128)S(1)}, f32[112,384]{1,0:T(8,128)S(1)}, u32[]{:S(2)}, u32[]{:S(2)}) collective-permute-start(f32[112,384]{1,0:T(8,128)S(1)} %join.1), channel_id=1, source_target_pairs={{0,8},{1,9},{2,10},{3,11},{4,12},{5,13},{6,14},{7,15},{8,0},{9,1},... | collective-permute-start | bytes 516104 | tf_op jit(solution)/shard_map/ppermute | solution.py:269
  7.1 0.5 %collective-permute-start.2 = (f32[112,384]{1,0:T(8,128)S(1)}, f32[112,384]{1,0:T(8,128)S(1)}, u32[]{:S(2)}, u32[]{:S(2)}) collective-permute-start(f32[112,384]{1,0:T(8,128)S(1)} %join.1), channel_id=1, source_target_pairs={{0,16},{1,17},{2,18},{3,19},{4,20},{5,21},{6,22},{7,23},{8,24},{9,... | collective-permute-start | bytes 516104 | tf_op jit(solution)/shard_map/ppermute | solution.py:269
  7.7 1.6 %collective-permute-start.6 = (f32[112,256]{1,0:T(8,128)S(1)}, f32[112,256]{1,0:T(8,128)S(1)}, u32[]{:S(2)}, u32[]{:S(2)}) collective-permute-start(f32[112,256]{1,0:T(8,128)S(1)} %copy-done), channel_id=1, source_target_pairs={{0,2},{1,3},{2,0},{3,1},{4,6},{5,7},{6,4},{7,5},{8,10},{9,11},{10,... | collective-permute-start | bytes 344072 | tf_op jit(solution)/shard_map/ppermute | solution.py:271
  10.5 0.0 copy-start.2
  10.5 0.0 collective-permute-done.4.refs_0_
  10.6 0.5 %collective-permute-start.5 = (f32[112,256]{1,0:T(8,128)S(1)}, f32[112,256]{1,0:T(8,128)S(1)}, u32[]{:S(2)}, u32[]{:S(2)}) collective-permute-start(f32[112,256]{1,0:T(8,128)S(1)} %collective-permute-done.4.refs_0_), channel_id=1, source_target_pairs={{0,2},{1,3},{2,0},{3,1},{4,6},{5,7},{6,4},{7,5},{8,10},{9,11},{10,... | collective-permute-start | bytes 344072 | tf_op jit(solution)/shard_map/ppermute | solution.py:273
  11.1 0.1 copy-done.2
  11.2 0.2 rows.2
  11.4 1.8 %collective-permute-done.6.refs_0_ = f32[112,256]{1,0:T(8,128)S(1)} collective-permute-done((f32[112,256]{1,0:T(8,128)S(1)}, f32[112,256]{1,0:T(8,128)S(1)}, u32[]{:S(2)}, u32[]{:S(2)}) %collective-permute-start.6) | collective-permute-done | bytes 114720 | tf_op jit(solution)/shard_map/ppermute | solution.py:271
  13.2 0.1 rows.3.refs_2_.refs_3_
  13.3 0.0 collective-permute-done
  13.3 1.4 %collective-permute-done.1 = f32[112,384]{1,0:T(8,128)S(1)} collective-permute-done((f32[112,384]{1,0:T(8,128)S(1)}, f32[112,384]{1,0:T(8,128)S(1)}, u32[]{:S(2)}, u32[]{:S(2)}) %collective-permute-start.1) | collective-permute-done | bytes 172064 | tf_op jit(solution)/shard_map/ppermute | solution.py:269
  14.7 0.0 collective-permute-done.2
  14.7 0.1 collective-permute-start.3
  14.8 1.1 %tile.2 = (f32[112,128]{1,0:T(8,128)S(1)}, f32[112,128]{1,0:T(8,128)S(1)}, f32[112,128]{1,0:T(8,128)S(1)}, bf16[448,1152]{1,0:T(8,128)(2,1)S(1)}, bf16[448,256]{1,0:T(8,128)(2,1)S(1)}) custom-call(f32[1,256]{1,0:T(1,128)S(1)} %bitcast.9, f32[1,1]{1,0:T(1,128)} %bitcast.3.amp_ref, f32[1,1]{1,0:T(1,128)} %bitcast.5.noise_ref, ...), custom_call_target="tpu_custom_call" | custom-call | flops 20000000000 | bytes 1024 | tf_op jit(solution)/shard_map/tile/pallas_call | solution.py:178
  15.9 0.0 collective-permute-done.5.refs_0_
  15.9 0.7 %last.1 = (f32[112,128]{1,0:T(8,128)S(1)}, bf16[112,1152]{1,0:T(8,128)(2,1)S(1)}) custom-call(f32[1,256]{1,0:T(1,128)S(1)} %bitcast.10, f32[112,256]{1,0:T(8,128)S(1)} %collective-permute-done.5.refs_0_, bf16[448,1152]{1,0:T(8,128)(2,1)S(1)} %get-tuple-element.26.refs_1_, bf16[448,256]{1,0:T(8,128)(2,1)S(1)} %get-tuple-element.27.refs_2_), custom_call_target="tpu_custom_call" | custom-call | flops 10000000000 | bytes 1024 | tf_op jit(solution)/shard_map/last/pallas_call | solution.py:209
  16.6 0.4 %collective-permute-done.3.refs_0_ = f32[448,384]{1,0:T(8,128)S(1)} collective-permute-done((f32[448,384]{1,0:T(8,128)S(1)}, f32[448,384]{1,0:T(8,128)S(1)}, u32[]{:S(2)}, u32[]{:S(2)}) %collective-permute-start.3) | collective-permute-done | bytes 688160 | tf_op jit(solution)/shard_map/ppermute | solution.py:275
  16.9 1.1 %tile.3 = (f32[112,128]{1,0:T(8,128)S(1)}, f32[112,128]{1,0:T(8,128)S(1)}, f32[112,128]{1,0:T(8,128)S(1)}, bf16[448,1152]{1,0:T(8,128)(2,1)S(1)}, bf16[448,256]{1,0:T(8,128)(2,1)S(1)}) custom-call(f32[1,256]{1,0:T(1,128)S(1)} %bitcast.11, f32[1,1]{1,0:T(1,128)} %bitcast.4.amp_ref, f32[1,1]{1,0:T(1,128)} %bitcast.6.noise_ref, ...), custom_call_target="tpu_custom_call" | custom-call | flops 10000000000 | bytes 1024 | tf_op jit(solution)/shard_map/tile/pallas_call | solution.py:178
  18.0 1.2 %collective-permute-start.7 = (f32[112,128]{1,0:T(8,128)S(1)}, f32[112,128]{1,0:T(8,128)S(1)}, u32[]{:S(2)}, u32[]{:S(2)}) collective-permute-start(f32[112,128]{1,0:T(8,128)S(1)} %get-tuple-element.32), channel_id=1, source_target_pairs={{4,0},{5,1},{6,2},{7,3},{0,4},{1,5},{2,6},{3,7},{12,8},{13,9},{14,... | collective-permute-start | bytes 172040 | tf_op jit(solution)/shard_map/ppermute | solution.py:291
  19.2 2.8 %collective-permute-start.8 = (f32[112,128]{1,0:T(8,128)S(1)}, f32[112,128]{1,0:T(8,128)S(1)}, u32[]{:S(2)}, u32[]{:S(2)}) collective-permute-start(f32[112,128]{1,0:T(8,128)S(1)} %get-tuple-element.33), channel_id=1, source_target_pairs={{6,0},{7,1},{4,2},{5,3},{2,4},{3,5},{0,6},{1,7},{14,8},{15,9},{12,... | collective-permute-start | bytes 172040 | tf_op jit(solution)/shard_map/ppermute | solution.py:291
  22.0 0.0 collective-permute-start.9
  22.0 0.7 %near.1 = f32[112,128]{1,0:T(8,128)S(1)} custom-call(bf16[448,1152]{1,0:T(8,128)(2,1)S(1)} %get-tuple-element.30.y_ref, bf16[448,256]{1,0:T(8,128)(2,1)S(1)} %get-tuple-element.31.v_ref, bf16[112,1152]{1,0:T(8,128)(2,1)S(1)} %get-tuple-element.20.refs_1_.refs_0_, f32[112,128]{1,0:T(8,128)S(1)} %get-tuple-element.22.refs_1_), custom_call_target="tpu_custom_call" | custom-call | flops 10000000000 | bytes 1024 | tf_op jit(solution)/shard_map/near/pallas_call | solution.py:232
  22.7 3.4 %collective-permute-done.7 = f32[112,128]{1,0:T(8,128)S(1)} collective-permute-done((f32[112,128]{1,0:T(8,128)S(1)}, f32[112,128]{1,0:T(8,128)S(1)}, u32[]{:S(2)}, u32[]{:S(2)}) %collective-permute-start.7) | collective-permute-done | bytes 57376 | tf_op jit(solution)/shard_map/ppermute | solution.py:291
  26.1 0.0 collective-permute-done.8
  26.1 0.6 %collective-permute-done.9 = f32[112,128]{1,0:T(8,128)S(1)} collective-permute-done((f32[112,128]{1,0:T(8,128)S(1)}, f32[112,128]{1,0:T(8,128)S(1)}, u32[]{:S(2)}, u32[]{:S(2)}) %collective-permute-start.9) | collective-permute-done | bytes 57376 | tf_op jit(solution)/shard_map/ppermute | solution.py:291
  26.6 0.6 %add_add_fusion = f32[112,128]{1,0:T(8,128)} fusion(f32[112,128]{1,0:T(8,128)S(1)} %collective-permute-done.9, f32[112,128]{1,0:T(8,128)S(1)} %collective-permute-done.8, f32[112,128]{1,0:T(8,128)S(1)} %near.1, f32[112,128]{1,0:T(8,128)S(1)} %collective-permute-done.7), kind=kLoop, calls=%fused_computation.1 | loop fusion | flops 43008 | bytes 286720 | tf_op jit(solution)/shard_map/add | solution.py:293
  (3 shorter events, 0.1 us)
Async XLA Ops:
  0.0 4.1 %copy-start = (f32[112,256]{1,0:T(8,128)S(1)}, f32[112,256]{1,0:T(8,128)}, u32[]{:S(2)}) copy-start(f32[112,256]{1,0:T(8,128)} %refs_1_.1) | copy-start | bytes 344068
  0.0 4.1 %copy-start.1 = (f32[112,128]{1,0:T(8,128)S(1)}, f32[112,128]{1,0:T(8,128)}, u32[]{:S(2)}) copy-start(f32[112,128]{1,0:T(8,128)} %b_ref.1) | copy-start | bytes 172036
  0.0 10.5 %collective-permute-start.4 = (f32[112,256]{1,0:T(8,128)}, f32[112,256]{1,0:T(8,128)S(1)}, u32[]{:S(2)}, u32[]{:S(2)}) collective-permute-start(f32[112,256]{1,0:T(8,128)} %refs_1_.1), channel_id=1, source_target_pairs={{0,4},{1,5},{2,6},{3,7},{4,0},{5,1},{6,2},{7,3},{8,12},{9,13},{10,... | collective-permute-start | bytes 344072 | tf_op jit(solution)/shard_map/ppermute | solution.py:265
  4.1 9.2 %collective-permute-start = (f32[112,384]{1,0:T(8,128)S(1)}, f32[112,384]{1,0:T(8,128)S(1)}, u32[]{:S(2)}, u32[]{:S(2)}) collective-permute-start(f32[112,384]{1,0:T(8,128)S(1)} %join.1), channel_id=1, source_target_pairs={{0,24},{1,25},{2,26},{3,27},{4,28},{5,29},{6,30},{7,31},{8,16},{9,... | collective-permute-start | bytes 516104 | tf_op jit(solution)/shard_map/ppermute | solution.py:269
  6.6 8.1 %collective-permute-start.1 = (f32[112,384]{1,0:T(8,128)S(1)}, f32[112,384]{1,0:T(8,128)S(1)}, u32[]{:S(2)}, u32[]{:S(2)}) collective-permute-start(f32[112,384]{1,0:T(8,128)S(1)} %join.1), channel_id=1, source_target_pairs={{0,8},{1,9},{2,10},{3,11},{4,12},{5,13},{6,14},{7,15},{8,0},{9,1},... | collective-permute-start | bytes 516104 | tf_op jit(solution)/shard_map/ppermute | solution.py:269
  7.1 7.5 %collective-permute-start.2 = (f32[112,384]{1,0:T(8,128)S(1)}, f32[112,384]{1,0:T(8,128)S(1)}, u32[]{:S(2)}, u32[]{:S(2)}) collective-permute-start(f32[112,384]{1,0:T(8,128)S(1)} %join.1), channel_id=1, source_target_pairs={{0,16},{1,17},{2,18},{3,19},{4,20},{5,21},{6,22},{7,23},{8,24},{9,... | collective-permute-start | bytes 516104 | tf_op jit(solution)/shard_map/ppermute | solution.py:269
  7.7 5.5 %collective-permute-start.6 = (f32[112,256]{1,0:T(8,128)S(1)}, f32[112,256]{1,0:T(8,128)S(1)}, u32[]{:S(2)}, u32[]{:S(2)}) collective-permute-start(f32[112,256]{1,0:T(8,128)S(1)} %copy-done), channel_id=1, source_target_pairs={{0,2},{1,3},{2,0},{3,1},{4,6},{5,7},{6,4},{7,5},{8,10},{9,11},{10,... | collective-permute-start | bytes 344072 | tf_op jit(solution)/shard_map/ppermute | solution.py:271
  10.5 0.7 %copy-start.2 = (f32[256]{0:T(256)S(1)}, f32[256]{0:T(256)}, u32[]{:S(2)}) copy-start(f32[256]{0:T(256)} %param.7) | copy-start | bytes 3076
  10.6 5.3 %collective-permute-start.5 = (f32[112,256]{1,0:T(8,128)S(1)}, f32[112,256]{1,0:T(8,128)S(1)}, u32[]{:S(2)}, u32[]{:S(2)}) collective-permute-start(f32[112,256]{1,0:T(8,128)S(1)} %collective-permute-done.4.refs_0_), channel_id=1, source_target_pairs={{0,2},{1,3},{2,0},{3,1},{4,6},{5,7},{6,4},{7,5},{8,10},{9,11},{10,... | collective-permute-start | bytes 344072 | tf_op jit(solution)/shard_map/ppermute | solution.py:273
  14.7 2.2 %collective-permute-start.3 = (f32[448,384]{1,0:T(8,128)S(1)}, f32[448,384]{1,0:T(8,128)S(1)}, u32[]{:S(2)}, u32[]{:S(2)}) collective-permute-start(f32[448,384]{1,0:T(8,128)S(1)} %pad_maximum_fusion.refs_0_), channel_id=1, source_target_pairs={{0,1},{1,0},{2,3},{3,2},{4,5},{5,4},{6,7},{7,6},{8,9},{9,8},{10,11... | collective-permute-start | bytes 2064392 | tf_op jit(solution)/shard_map/ppermute | solution.py:275
  18.0 8.1 %collective-permute-start.7 = (f32[112,128]{1,0:T(8,128)S(1)}, f32[112,128]{1,0:T(8,128)S(1)}, u32[]{:S(2)}, u32[]{:S(2)}) collective-permute-start(f32[112,128]{1,0:T(8,128)S(1)} %get-tuple-element.32), channel_id=1, source_target_pairs={{4,0},{5,1},{6,2},{7,3},{0,4},{1,5},{2,6},{3,7},{12,8},{13,9},{14,... | collective-permute-start | bytes 172040 | tf_op jit(solution)/shard_map/ppermute | solution.py:291
  19.2 6.8 %collective-permute-start.8 = (f32[112,128]{1,0:T(8,128)S(1)}, f32[112,128]{1,0:T(8,128)S(1)}, u32[]{:S(2)}, u32[]{:S(2)}) collective-permute-start(f32[112,128]{1,0:T(8,128)S(1)} %get-tuple-element.33), channel_id=1, source_target_pairs={{6,0},{7,1},{4,2},{5,3},{2,4},{3,5},{0,6},{1,7},{14,8},{15,9},{12,... | collective-permute-start | bytes 172040 | tf_op jit(solution)/shard_map/ppermute | solution.py:291
  22.0 4.6 %collective-permute-start.9 = (f32[112,128]{1,0:T(8,128)S(1)}, f32[112,128]{1,0:T(8,128)S(1)}, u32[]{:S(2)}, u32[]{:S(2)}) collective-permute-start(f32[112,128]{1,0:T(8,128)S(1)} %get-tuple-element.34), channel_id=1, source_target_pairs={{2,0},{3,1},{0,2},{1,3},{6,4},{7,5},{4,6},{5,7},{10,8},{11,9},{8,1... | collective-permute-start | bytes 172040 | tf_op jit(solution)/shard_map/ppermute | solution.py:291

commit v9 on v8

--- a/solution.py
+++ b/solution.py
@@ -275,7 +275,7 @@
         cols_theirs = lax.ppermute(cols_mine, AXES, other_core)
 
         x = dict(zip([half, 0], prepare_rows(scale, [points_of[half], points], 40)))
-        x |= dict(zip(direct[:-1], prepare_rows(scale, [points_of[k] for k in direct[:-1]], 1)))
+        x |= dict(zip(direct[:-1], prepare_rows(scale, [points_of[k] for k in direct[:-1]], 8)))
         ks = [0, *direct]
         part, mine = times_columns(scale, outputscale, noise, [cols_mine], [x[k] for k in ks], [], 20)
         total = dict(zip(ks, part))

time: 27.4 us -> 27.4 us (level)
  no operation moved by 1% of the time
where the time goes in v9:
time: 27.4 us; the launch traced here: 27.3 us
  starting transfers between devices  13.8 us (50%)
  waiting for transfers between devices  7.45 us (27%)
  Pallas kernels  3.81 us (14%)
  between operations  1.42 us (5%)
  other arithmetic  0.68 us (2%)
    ppermute x1, starting transfers between devices, per_device(): points_of = {half: lax.ppermute(points, AXES, along_line(half))}  4.04 us
    ppermute x3, starting transfers between devices, per_device(): lax.ppermute(total[k], AXES, [(b, a) for a, b in along_line(k)])  4 us
    ppermute x3, waiting for transfers between devices, per_device(): lax.ppermute(total[k], AXES, [(b, a) for a, b in along_line(k)])  3.94 us
    ppermute x3, starting transfers between devices, per_device(): lax.ppermute(both, AXES, along_outer(k))  3.55 us
    pallas_call x2, Pallas kernels, times_columns(): pl.pallas_call(functools.partial(tile_kernel, len(cols), len(rows)), out_...  2.13 us
    ppermute x1, waiting for transfers between devices, per_device(): points_of[k] = lax.ppermute(points, AXES, along_line(k))  1.77 us
    ppermute x1, starting transfers between devices, per_device(): points_of[k] = lax.ppermute(points, AXES, along_line(k))  1.58 us
    ppermute x3, waiting for transfers between devices, per_device(): lax.ppermute(both, AXES, along_outer(k))  1.37 us
  transfers between devices with their start and end apart: 10, of which 5 were waited for; matrix products, arithmetic and copies ran while one was open for 0% of the time, Pallas kernels for 10%

profile of v9, /device:TPU:0, one launch (start us, length us, event | category | flops | bytes accessed | tf_op | source)
XLA Modules:
  0.0 27.3 jit_solution(2577030321274796106)
XLA Ops:
  0.0 0.0 copy-start
  0.0 0.0 copy-start.1
  0.0 4.0 %collective-permute-start.4 = (f32[112,256]{1,0:T(8,128)}, f32[112,256]{1,0:T(8,128)S(1)}, u32[]{:S(2)}, u32[]{:S(2)}) collective-permute-start(f32[112,256]{1,0:T(8,128)} %refs_1_.1), channel_id=1, source_target_pairs={{0,4},{1,5},{2,6},{3,7},{4,0},{5,1},{6,2},{7,3},{8,12},{9,13},{10,... | collective-permute-start | bytes 344072 | tf_op jit(solution)/shard_map/ppermute | solution.py:265
  4.1 0.0 copy-done
  4.1 0.0 copy-done.1
  4.1 2.5 %collective-permute-start = (f32[112,384]{1,0:T(8,128)S(1)}, f32[112,384]{1,0:T(8,128)S(1)}, u32[]{:S(2)}, u32[]{:S(2)}) collective-permute-start(f32[112,384]{1,0:T(8,128)S(1)} %join.1), channel_id=1, source_target_pairs={{0,24},{1,25},{2,26},{3,27},{4,28},{5,29},{6,30},{7,31},{8,16},{9,... | collective-permute-start | bytes 516104 | tf_op jit(solution)/shard_map/ppermute | solution.py:269
  6.6 0.5 %collective-permute-start.1 = (f32[112,384]{1,0:T(8,128)S(1)}, f32[112,384]{1,0:T(8,128)S(1)}, u32[]{:S(2)}, u32[]{:S(2)}) collective-permute-start(f32[112,384]{1,0:T(8,128)S(1)} %join.1), channel_id=1, source_target_pairs={{0,8},{1,9},{2,10},{3,11},{4,12},{5,13},{6,14},{7,15},{8,0},{9,1},... | collective-permute-start | bytes 516104 | tf_op jit(solution)/shard_map/ppermute | solution.py:269
  7.1 0.5 %collective-permute-start.2 = (f32[112,384]{1,0:T(8,128)S(1)}, f32[112,384]{1,0:T(8,128)S(1)}, u32[]{:S(2)}, u32[]{:S(2)}) collective-permute-start(f32[112,384]{1,0:T(8,128)S(1)} %join.1), channel_id=1, source_target_pairs={{0,16},{1,17},{2,18},{3,19},{4,20},{5,21},{6,22},{7,23},{8,24},{9,... | collective-permute-start | bytes 516104 | tf_op jit(solution)/shard_map/ppermute | solution.py:269
  7.7 1.6 %collective-permute-start.6 = (f32[112,256]{1,0:T(8,128)S(1)}, f32[112,256]{1,0:T(8,128)S(1)}, u32[]{:S(2)}, u32[]{:S(2)}) collective-permute-start(f32[112,256]{1,0:T(8,128)S(1)} %copy-done), channel_id=1, source_target_pairs={{0,2},{1,3},{2,0},{3,1},{4,6},{5,7},{6,4},{7,5},{8,10},{9,11},{10,... | collective-permute-start | bytes 344072 | tf_op jit(solution)/shard_map/ppermute | solution.py:271
  10.5 0.0 copy-start.2
  10.5 0.0 collective-permute-done.4.refs_0_
  10.6 0.5 %collective-permute-start.5 = (f32[112,256]{1,0:T(8,128)S(1)}, f32[112,256]{1,0:T(8,128)S(1)}, u32[]{:S(2)}, u32[]{:S(2)}) collective-permute-start(f32[112,256]{1,0:T(8,128)S(1)} %collective-permute-done.4.refs_0_), channel_id=1, source_target_pairs={{0,2},{1,3},{2,0},{3,1},{4,6},{5,7},{6,4},{7,5},{8,10},{9,11},{10,... | collective-permute-start | bytes 344072 | tf_op jit(solution)/shard_map/ppermute | solution.py:273
  11.1 0.1 copy-done.2
  11.2 0.2 rows.2
  11.4 1.8 %collective-permute-done.6.refs_0_ = f32[112,256]{1,0:T(8,128)S(1)} collective-permute-done((f32[112,256]{1,0:T(8,128)S(1)}, f32[112,256]{1,0:T(8,128)S(1)}, u32[]{:S(2)}, u32[]{:S(2)}) %collective-permute-start.6) | collective-permute-done | bytes 114720 | tf_op jit(solution)/shard_map/ppermute | solution.py:271
  13.2 0.1 rows.3.refs_2_.refs_3_
  13.3 0.0 collective-permute-done
  13.3 1.4 %collective-permute-done.1 = f32[112,384]{1,0:T(8,128)S(1)} collective-permute-done((f32[112,384]{1,0:T(8,128)S(1)}, f32[112,384]{1,0:T(8,128)S(1)}, u32[]{:S(2)}, u32[]{:S(2)}) %collective-permute-start.1) | collective-permute-done | bytes 172064 | tf_op jit(solution)/shard_map/ppermute | solution.py:269
  14.7 0.0 collective-permute-done.2
  14.7 0.1 collective-permute-start.3
  14.8 1.1 %tile.2 = (f32[112,128]{1,0:T(8,128)S(1)}, f32[112,128]{1,0:T(8,128)S(1)}, f32[112,128]{1,0:T(8,128)S(1)}, bf16[448,1152]{1,0:T(8,128)(2,1)S(1)}, bf16[448,256]{1,0:T(8,128)(2,1)S(1)}) custom-call(f32[1,256]{1,0:T(1,128)S(1)} %bitcast.9, f32[1,1]{1,0:T(1,128)} %bitcast.3.amp_ref, f32[1,1]{1,0:T(1,128)} %bitcast.5.noise_ref, ...), custom_call_target="tpu_custom_call" | custom-call | flops 20000000000 | bytes 1024 | tf_op jit(solution)/shard_map/tile/pallas_call | solution.py:178
  15.9 0.0 collective-permute-done.5.refs_0_
  15.9 0.7 %last.1 = (f32[112,128]{1,0:T(8,128)S(1)}, bf16[112,1152]{1,0:T(8,128)(2,1)S(1)}) custom-call(f32[1,256]{1,0:T(1,128)S(1)} %bitcast.10, f32[112,256]{1,0:T(8,128)S(1)} %collective-permute-done.5.refs_0_, bf16[448,1152]{1,0:T(8,128)(2,1)S(1)} %get-tuple-element.26.refs_1_, bf16[448,256]{1,0:T(8,128)(2,1)S(1)} %get-tuple-element.27.refs_2_), custom_call_target="tpu_custom_call" | custom-call | flops 10000000000 | bytes 1024 | tf_op jit(solution)/shard_map/last/pallas_call | solution.py:209
  16.6 0.4 %collective-permute-done.3.refs_0_ = f32[448,384]{1,0:T(8,128)S(1)} collective-permute-done((f32[448,384]{1,0:T(8,128)S(1)}, f32[448,384]{1,0:T(8,128)S(1)}, u32[]{:S(2)}, u32[]{:S(2)}) %collective-permute-start.3) | collective-permute-done | bytes 688160 | tf_op jit(solution)/shard_map/ppermute | solution.py:275
  16.9 1.1 %tile.3 = (f32[112,128]{1,0:T(8,128)S(1)}, f32[112,128]{1,0:T(8,128)S(1)}, f32[112,128]{1,0:T(8,128)S(1)}, bf16[448,1152]{1,0:T(8,128)(2,1)S(1)}, bf16[448,256]{1,0:T(8,128)(2,1)S(1)}) custom-call(f32[1,256]{1,0:T(1,128)S(1)} %bitcast.11, f32[1,1]{1,0:T(1,128)} %bitcast.4.amp_ref, f32[1,1]{1,0:T(1,128)} %bitcast.6.noise_ref, ...), custom_call_target="tpu_custom_call" | custom-call | flops 10000000000 | bytes 1024 | tf_op jit(solution)/shard_map/tile/pallas_call | solution.py:178
  18.0 1.2 %collective-permute-start.7 = (f32[112,128]{1,0:T(8,128)S(1)}, f32[112,128]{1,0:T(8,128)S(1)}, u32[]{:S(2)}, u32[]{:S(2)}) collective-permute-start(f32[112,128]{1,0:T(8,128)S(1)} %get-tuple-element.32), channel_id=1, source_target_pairs={{4,0},{5,1},{6,2},{7,3},{0,4},{1,5},{2,6},{3,7},{12,8},{13,9},{14,... | collective-permute-start | bytes 172040 | tf_op jit(solution)/shard_map/ppermute | solution.py:291
  19.2 2.8 %collective-permute-start.8 = (f32[112,128]{1,0:T(8,128)S(1)}, f32[112,128]{1,0:T(8,128)S(1)}, u32[]{:S(2)}, u32[]{:S(2)}) collective-permute-start(f32[112,128]{1,0:T(8,128)S(1)} %get-tuple-element.33), channel_id=1, source_target_pairs={{6,0},{7,1},{4,2},{5,3},{2,4},{3,5},{0,6},{1,7},{14,8},{15,9},{12,... | collective-permute-start | bytes 172040 | tf_op jit(solution)/shard_map/ppermute | solution.py:291
  22.0 0.0 collective-permute-start.9
  22.0 0.7 %near.1 = f32[112,128]{1,0:T(8,128)S(1)} custom-call(bf16[448,1152]{1,0:T(8,128)(2,1)S(1)} %get-tuple-element.30.y_ref, bf16[448,256]{1,0:T(8,128)(2,1)S(1)} %get-tuple-element.31.v_ref, bf16[112,1152]{1,0:T(8,128)(2,1)S(1)} %get-tuple-element.20.refs_1_.refs_0_, f32[112,128]{1,0:T(8,128)S(1)} %get-tuple-element.22.refs_1_), custom_call_target="tpu_custom_call" | custom-call | flops 10000000000 | bytes 1024 | tf_op jit(solution)/shard_map/near/pallas_call | solution.py:232
  22.7 3.4 %collective-permute-done.7 = f32[112,128]{1,0:T(8,128)S(1)} collective-permute-done((f32[112,128]{1,0:T(8,128)S(1)}, f32[112,128]{1,0:T(8,128)S(1)}, u32[]{:S(2)}, u32[]{:S(2)}) %collective-permute-start.7) | collective-permute-done | bytes 57376 | tf_op jit(solution)/shard_map/ppermute | solution.py:291
  26.1 0.0 collective-permute-done.8
  26.1 0.6 %collective-permute-done.9 = f32[112,128]{1,0:T(8,128)S(1)} collective-permute-done((f32[112,128]{1,0:T(8,128)S(1)}, f32[112,128]{1,0:T(8,128)S(1)}, u32[]{:S(2)}, u32[]{:S(2)}) %collective-permute-start.9) | collective-permute-done | bytes 57376 | tf_op jit(solution)/shard_map/ppermute | solution.py:291
  26.6 0.6 %add_add_fusion = f32[112,128]{1,0:T(8,128)} fusion(f32[112,128]{1,0:T(8,128)S(1)} %collective-permute-done.9, f32[112,128]{1,0:T(8,128)S(1)} %collective-permute-done.8, f32[112,128]{1,0:T(8,128)S(1)} %near.1, f32[112,128]{1,0:T(8,128)S(1)} %collective-permute-done.7), kind=kLoop, calls=%fused_computation.1 | loop fusion | flops 43008 | bytes 286720 | tf_op jit(solution)/shard_map/add | solution.py:293
  (3 shorter events, 0.1 us)
Async XLA Ops:
  0.0 4.1 %copy-start = (f32[112,256]{1,0:T(8,128)S(1)}, f32[112,256]{1,0:T(8,128)}, u32[]{:S(2)}) copy-start(f32[112,256]{1,0:T(8,128)} %refs_1_.1) | copy-start | bytes 344068
  0.0 4.1 %copy-start.1 = (f32[112,128]{1,0:T(8,128)S(1)}, f32[112,128]{1,0:T(8,128)}, u32[]{:S(2)}) copy-start(f32[112,128]{1,0:T(8,128)} %b_ref.1) | copy-start | bytes 172036
  0.0 10.5 %collective-permute-start.4 = (f32[112,256]{1,0:T(8,128)}, f32[112,256]{1,0:T(8,128)S(1)}, u32[]{:S(2)}, u32[]{:S(2)}) collective-permute-start(f32[112,256]{1,0:T(8,128)} %refs_1_.1), channel_id=1, source_target_pairs={{0,4},{1,5},{2,6},{3,7},{4,0},{5,1},{6,2},{7,3},{8,12},{9,13},{10,... | collective-permute-start | bytes 344072 | tf_op jit(solution)/shard_map/ppermute | solution.py:265
  4.1 9.2 %collective-permute-start = (f32[112,384]{1,0:T(8,128)S(1)}, f32[112,384]{1,0:T(8,128)S(1)}, u32[]{:S(2)}, u32[]{:S(2)}) collective-permute-start(f32[112,384]{1,0:T(8,128)S(1)} %join.1), channel_id=1, source_target_pairs={{0,24},{1,25},{2,26},{3,27},{4,28},{5,29},{6,30},{7,31},{8,16},{9,... | collective-permute-start | bytes 516104 | tf_op jit(solution)/shard_map/ppermute | solution.py:269
  6.6 8.1 %collective-permute-start.1 = (f32[112,384]{1,0:T(8,128)S(1)}, f32[112,384]{1,0:T(8,128)S(1)}, u32[]{:S(2)}, u32[]{:S(2)}) collective-permute-start(f32[112,384]{1,0:T(8,128)S(1)} %join.1), channel_id=1, source_target_pairs={{0,8},{1,9},{2,10},{3,11},{4,12},{5,13},{6,14},{7,15},{8,0},{9,1},... | collective-permute-start | bytes 516104 | tf_op jit(solution)/shard_map/ppermute | solution.py:269
  7.1 7.5 %collective-permute-start.2 = (f32[112,384]{1,0:T(8,128)S(1)}, f32[112,384]{1,0:T(8,128)S(1)}, u32[]{:S(2)}, u32[]{:S(2)}) collective-permute-start(f32[112,384]{1,0:T(8,128)S(1)} %join.1), channel_id=1, source_target_pairs={{0,16},{1,17},{2,18},{3,19},{4,20},{5,21},{6,22},{7,23},{8,24},{9,... | collective-permute-start | bytes 516104 | tf_op jit(solution)/shard_map/ppermute | solution.py:269
  7.7 5.5 %collective-permute-start.6 = (f32[112,256]{1,0:T(8,128)S(1)}, f32[112,256]{1,0:T(8,128)S(1)}, u32[]{:S(2)}, u32[]{:S(2)}) collective-permute-start(f32[112,256]{1,0:T(8,128)S(1)} %copy-done), channel_id=1, source_target_pairs={{0,2},{1,3},{2,0},{3,1},{4,6},{5,7},{6,4},{7,5},{8,10},{9,11},{10,... | collective-permute-start | bytes 344072 | tf_op jit(solution)/shard_map/ppermute | solution.py:271
  10.5 0.7 %copy-start.2 = (f32[256]{0:T(256)S(1)}, f32[256]{0:T(256)}, u32[]{:S(2)}) copy-start(f32[256]{0:T(256)} %param.7) | copy-start | bytes 3076
  10.6 5.3 %collective-permute-start.5 = (f32[112,256]{1,0:T(8,128)S(1)}, f32[112,256]{1,0:T(8,128)S(1)}, u32[]{:S(2)}, u32[]{:S(2)}) collective-permute-start(f32[112,256]{1,0:T(8,128)S(1)} %collective-permute-done.4.refs_0_), channel_id=1, source_target_pairs={{0,2},{1,3},{2,0},{3,1},{4,6},{5,7},{6,4},{7,5},{8,10},{9,11},{10,... | collective-permute-start | bytes 344072 | tf_op jit(solution)/shard_map/ppermute | solution.py:273
  14.7 2.2 %collective-permute-start.3 = (f32[448,384]{1,0:T(8,128)S(1)}, f32[448,384]{1,0:T(8,128)S(1)}, u32[]{:S(2)}, u32[]{:S(2)}) collective-permute-start(f32[448,384]{1,0:T(8,128)S(1)} %pad_maximum_fusion.refs_0_), channel_id=1, source_target_pairs={{0,1},{1,0},{2,3},{3,2},{4,5},{5,4},{6,7},{7,6},{8,9},{9,8},{10,11... | collective-permute-start | bytes 2064392 | tf_op jit(solution)/shard_map/ppermute | solution.py:275
  18.0 8.1 %collective-permute-start.7 = (f32[112,128]{1,0:T(8,128)S(1)}, f32[112,128]{1,0:T(8,128)S(1)}, u32[]{:S(2)}, u32[]{:S(2)}) collective-permute-start(f32[112,128]{1,0:T(8,128)S(1)} %get-tuple-element.32), channel_id=1, source_target_pairs={{4,0},{5,1},{6,2},{7,3},{0,4},{1,5},{2,6},{3,7},{12,8},{13,9},{14,... | collective-permute-start | bytes 172040 | tf_op jit(solution)/shard_map/ppermute | solution.py:291
  19.2 6.8 %collective-permute-start.8 = (f32[112,128]{1,0:T(8,128)S(1)}, f32[112,128]{1,0:T(8,128)S(1)}, u32[]{:S(2)}, u32[]{:S(2)}) collective-permute-start(f32[112,128]{1,0:T(8,128)S(1)} %get-tuple-element.33), channel_id=1, source_target_pairs={{6,0},{7,1},{4,2},{5,3},{2,4},{3,5},{0,6},{1,7},{14,8},{15,9},{12,... | collective-permute-start | bytes 172040 | tf_op jit(solution)/shard_map/ppermute | solution.py:291
  22.0 4.6 %collective-permute-start.9 = (f32[112,128]{1,0:T(8,128)S(1)}, f32[112,128]{1,0:T(8,128)S(1)}, u32[]{:S(2)}, u32[]{:S(2)}) collective-permute-start(f32[112,128]{1,0:T(8,128)S(1)} %get-tuple-element.34), channel_id=1, source_target_pairs={{2,0},{3,1},{0,2},{1,3},{6,4},{7,5},{4,6},{5,7},{10,8},{11,9},{8,1... | collective-permute-start | bytes 172040 | tf_op jit(solution)/shard_map/ppermute | solution.py:291
